TPU v7x, 32 devices: a whole 2x2x4 slice. The times are simulated.
32 devices in a mesh: rows: 8 (over z, y), img: 4 (over x, core).
Axes of the slice: x: 2, y: 2, z: 4, core: 2. Of those that a mesh axis runs over, the one named last changes fastest.
Arguments:
- images_in: bfloat16 [16, 32, 44, 2048], P('img', 'rows'), may hold values from -6 to 6
- out_grad: bfloat16 [16, 32, 44, 2048], P('img', 'rows'), may hold values from -6 to 6
- box_rows: int32 [16, 100, 2], P('img'), may hold values from 0 to 31
- box_cols: int32 [16, 100, 2], P('img'), may hold values from 0 to 43
- box_count: int32 [16], P('img'), may hold values from 1 to 100, as said below
- valid_mask: int32 [16, 32, 44], P('img', 'rows'), may hold values 0 or 1
- reduce_one: bfloat16 [2048, 512], P(('rows', 'img')), may hold values from -0.125 to 0.125
- offset_one: bfloat16 [18432, 18], P(('rows', 'img')), may hold values from -0.107910156 to 0.107910156
- deform_one: bfloat16 [4608, 512], P(('rows', 'img')), may hold values from -0.09375 to 0.09375
- expand_one: bfloat16 [512, 2048], P(('rows', 'img')), may hold values from -0.25 to 0.25
- mid_gain_one: bfloat16 [2, 512], P(None, ('rows', 'img')), may hold values from 0.5 to 1.5
- mid_bias_one: bfloat16 [2, 512], P(None, ('rows', 'img')), may hold values from -3 to 3
- wide_gain_one: bfloat16 [2048], P(('rows', 'img')), may hold values from 0.5 to 1.5
- wide_bias_one: bfloat16 [2048], P(('rows', 'img')), may hold values from -3 to 3
- reduce_two: bfloat16 [2048, 512], P(('rows', 'img')), may hold values from -0.125 to 0.125
- spatial_two: bfloat16 [4608, 512], P(('rows', 'img')), may hold values from -0.09375 to 0.09375
- expand_two: bfloat16 [512, 2048], P(('rows', 'img')), may hold values from -0.25 to 0.25
- mid_gain_two: bfloat16 [2, 512], P(None, ('rows', 'img')), may hold values from 0.5 to 1.5
- mid_bias_two: bfloat16 [2, 512], P(None, ('rows', 'img')), may hold values from -3 to 3
- wide_gain_two: bfloat16 [2048], P(('rows', 'img')), may hold values from 0.5 to 1.5
- wide_bias_two: bfloat16 [2048], P(('rows', 'img')), may hold values from -3 to 3
Outputs:
- block_out: bfloat16 [16, 32, 44, 2048], P('img', 'rows')
- grad_images: float32 [16, 32, 44, 2048], P('img', 'rows')
- grad_reduce_one: float32 [2048, 512], P(('rows', 'img'))
- grad_offset_one: float32 [18432, 18], P(('rows', 'img'))
- grad_deform_one: float32 [4608, 512], P(('rows', 'img'))
- grad_expand_one: float32 [512, 2048], P(('rows', 'img'))
- grad_mid_gain_one: float32 [2, 512], P(None, ('rows', 'img'))
- grad_mid_bias_one: float32 [2, 512], P(None, ('rows', 'img'))
- grad_wide_gain_one: float32 [2048], P(('rows', 'img'))
- grad_wide_bias_one: float32 [2048], P(('rows', 'img'))
- grad_reduce_two: float32 [2048, 512], P(('rows', 'img'))
- grad_spatial_two: float32 [4608, 512], P(('rows', 'img'))
- grad_expand_two: float32 [512, 2048], P(('rows', 'img'))
- grad_mid_gain_two: float32 [2, 512], P(None, ('rows', 'img'))
- grad_mid_bias_two: float32 [2, 512], P(None, ('rows', 'img'))
- grad_wide_gain_two: float32 [2048], P(('rows', 'img'))
- grad_wide_bias_two: float32 [2048], P(('rows', 'img'))
Inputs may be any that keep to these rules, and one draw needn't show every extreme that they name: Image i uses its first box_count[i] box slots, and some image uses all 100.
All inputs are finite; a program needn't handle non-finite values. No bound on the sum of `valid_mask` on one device may be relied on, other than what follows from the above.
Results may differ from a plain program's by a relative error of at most 0.025.
Values may be sent and summed in bfloat16 or wider, within the bound.
No kernel may reach another device: no remote copies, remote signals or barrier semaphores. Data moves between devices by JAX's collectives and lax.ppermute only.
A program may use at most 320 MiB of HBM per device.

v0:
```python
from functools import partial

import jax
import jax.numpy as jnp
from jax import lax
from jax.sharding import PartitionSpec as P

CLIP = 8
HALO = 10
MB = 2


epsilon = 1e-05
exact = lax.Precision.HIGHEST


def from_behind(value, axis, steps):
    count = lax.axis_size(axis)
    first, last = (max(0, -steps), min(count, count - steps))
    return lax.ppermute(value, axis, [(source, source + steps) for source in range(first, last)])


def padded_2(cells, sides, width):
    for axis, dim in sides:
        count = lax.axis_size(axis)
        ends = count - 1
        head = lax.slice_in_dim(cells, 0, width, axis=dim)
        tail = lax.slice_in_dim(cells, cells.shape[dim] - width, cells.shape[dim], axis=dim)
        cells = jnp.concatenate(
            [
                lax.ppermute(tail, axis, [(i, (i + 1) % count) for i in range(ends)]),
                cells,
                lax.ppermute(head, axis, [((i + 1) % count, i) for i in range(ends)]),
            ],
            axis=dim,
        )
    return cells


def spline(values):
    magnitude = jnp.abs(values)
    outer = 1.5 - magnitude
    return jnp.where(
        magnitude < 0.5,
        0.75 - values * values,
        jnp.where(magnitude < 1.5, 0.5 * outer * outer, 0.0),
    )


def silu_slope(values):
    logistic = jax.nn.sigmoid(values)
    return logistic * (1.0 + values * (1.0 - logistic))


def tent_weights(clipped, rel_rows):
    tap_ids = jnp.arange(9)
    base_rows = (tap_ids // 3 - 1).astype(jnp.float32)
    base_cols = (tap_ids % 3 - 1).astype(jnp.float32)
    shift_rows = clipped[..., :9] + base_rows
    shift_cols = clipped[..., 9:] + base_cols
    span_cols = clipped.shape[-2]
    rel_cols = (jnp.arange(span_cols)[None, :] - jnp.arange(span_cols)[:, None]).astype(jnp.float32)
    weight_rows = spline(shift_rows[..., None] - rel_rows[:, None, None, :])
    weight_cols = spline(shift_cols[..., None] - rel_cols[:, None, :])
    return weight_rows[..., :, None] * weight_cols[..., None, :]


def box_weights(box_rows, box_cols, box_count, valid_mask, strip_rows, span_cols):
    row_ids = lax.axis_index("rows") * strip_rows + jnp.arange(strip_rows)
    col_ids = jnp.arange(span_cols)
    row_low = jnp.minimum(box_rows[..., 0], box_rows[..., 1])
    row_high = jnp.maximum(box_rows[..., 0], box_rows[..., 1])
    col_low = jnp.minimum(box_cols[..., 0], box_cols[..., 1])
    col_high = jnp.maximum(box_cols[..., 0], box_cols[..., 1])
    inside_rows = ((row_ids >= row_low[..., None]) & (row_ids <= row_high[..., None])).astype(
        jnp.float32
    )
    inside_cols = ((col_ids >= col_low[..., None]) & (col_ids <= col_high[..., None])).astype(
        jnp.float32
    )
    live_boxes = (jnp.arange(box_rows.shape[1])[None, :] < box_count[:, None]).astype(jnp.float32)
    covered = jnp.einsum("ib,ibh,ibw->ihw", live_boxes, inside_rows, inside_cols, precision=exact)
    return valid_mask.astype(jnp.float32) * (
        0.5 + covered / box_count.astype(jnp.float32)[:, None, None]
    )


def norm_forward(values, gain_term, bias_term):
    totals = lax.psum((jnp.sum(values, axis=0), jnp.sum(values * values, axis=0)), ("rows", "img"))
    total_count = values.shape[0] * lax.axis_size(("rows", "img"))
    center = totals[0] / total_count
    spread = lax.rsqrt(totals[1] / total_count - center * center + epsilon)
    normed = (values - center) * spread
    return (normed, spread, normed * gain_term.astype(jnp.float32) + bias_term.astype(jnp.float32))


def norm_backward(upstream, normed, spread, gain_term):
    totals = lax.psum(
        (jnp.sum(upstream, axis=0), jnp.sum(upstream * normed, axis=0)), ("rows", "img")
    )
    total_count = upstream.shape[0] * lax.axis_size(("rows", "img"))
    gain_float = gain_term.astype(jnp.float32)
    result = spread * (
        upstream * gain_float
        - gain_float * totals[0] / total_count
        - normed * (gain_float * totals[1] / total_count)
    )
    return (result, totals[1], totals[0])


def tap_slices(source, spacing, row_begin, strip_rows, span_cols, mirror):
    padded = jnp.pad(source, ((0, 0), (0, 0), (spacing, spacing), (0, 0)))
    portions = []
    for tap_index in range(9):
        row_tap = tap_index // 3
        col_tap = tap_index % 3
        if mirror:
            row_tap = 2 - row_tap
            col_tap = 2 - col_tap
        row_start = row_begin + row_tap * spacing
        col_start = col_tap * spacing
        portions.append(
            padded[
                :, row_start : row_start + strip_rows, col_start : col_start + span_cols, :
            ].reshape(-1, source.shape[-1])
        )
    return portions


def tap_product(portions, weight, channels):
    running = jnp.dot(portions[0], weight[:channels], preferred_element_type=jnp.float32)
    for tap_index in range(1, 9):
        running = running + jnp.dot(
            portions[tap_index],
            weight[tap_index * channels : (tap_index + 1) * channels],
            preferred_element_type=jnp.float32,
        )
    return running


def tap_transposed(portions, weight, channels):
    running = jnp.einsum(
        "pn,kn->pk", portions[0], weight[:channels], preferred_element_type=jnp.float32
    )
    for tap_index in range(1, 9):
        running = running + jnp.einsum(
            "pn,kn->pk",
            portions[tap_index],
            weight[tap_index * channels : (tap_index + 1) * channels],
            preferred_element_type=jnp.float32,
        )
    return running


def tap_weight_grads(portions, upstream):
    return jnp.concatenate(
        [
            jnp.einsum("pk,pn->kn", portion, upstream, preferred_element_type=jnp.float32)
            for portion in portions
        ],
        axis=0,
    )


def gather_rows(hidden, strip_rows):
    hop_total = -(-HALO // strip_rows)
    above_list = []
    below_list = []
    for hop_index in range(1, hop_total + 1):
        row_count = min(strip_rows, HALO - (hop_index - 1) * strip_rows)
        above_list.insert(0, from_behind(hidden[:, strip_rows - row_count :], "rows", hop_index))
        below_list.append(from_behind(hidden[:, :row_count], "rows", -hop_index))
    return jnp.concatenate(above_list + [hidden] + below_list, axis=1)


def return_rows(window_grad, strip_rows):
    hop_total = -(-HALO // strip_rows)
    own_rows = window_grad[:, HALO : HALO + strip_rows]
    top_end = HALO
    bottom_start = HALO + strip_rows
    for hop_index in range(1, hop_total + 1):
        row_count = min(strip_rows, HALO - (hop_index - 1) * strip_rows)
        upper_part = window_grad[:, top_end - row_count : top_end]
        lower_part = window_grad[:, bottom_start : bottom_start + row_count]
        top_end = top_end - row_count
        bottom_start = bottom_start + row_count
        from_below = from_behind(upper_part, "rows", -hop_index)
        from_above = from_behind(lower_part, "rows", hop_index)
        own_rows = own_rows.at[:, strip_rows - row_count :].add(from_below)
        own_rows = own_rows.at[:, :row_count].add(from_above)
    return own_rows


def local_slice(full_grad, axis_dim):
    piece_size = full_grad.shape[axis_dim] // lax.axis_size(("rows", "img"))
    return lax.dynamic_slice_in_dim(
        full_grad, lax.axis_index(("rows", "img")) * piece_size, piece_size, axis_dim
    )


def on_device(
    images_in,
    out_grad,
    box_rows,
    box_cols,
    box_count,
    valid_mask,
    reduce_one,
    offset_one,
    deform_one,
    expand_one,
    mid_gain_one,
    mid_bias_one,
    wide_gain_one,
    wide_bias_one,
    reduce_two,
    spatial_two,
    expand_two,
    mid_gain_two,
    mid_bias_two,
    wide_gain_two,
    wide_bias_two,
):
    local_images, strip_rows, span_cols, channels_wide = images_in.shape
    per_section = local_images // MB
    pixels = per_section * strip_rows * span_cols
    window_rows = strip_rows + 2 * HALO
    grad_weight = box_weights(box_rows, box_cols, box_count, valid_mask, strip_rows, span_cols)
    rel_rows = (jnp.arange(window_rows)[None, :] - (HALO + jnp.arange(strip_rows))[:, None]).astype(
        jnp.float32
    )
    norm_grads = {
        "wide_two": [],
        "mid_two_second": [],
        "mid_two_first": [],
        "wide_one": [],
        "mid_one_second": [],
        "mid_one_first": [],
    }
    outputs = []
    images_grads = []
    weight_totals = None

    def record(label, gain_grad, bias_grad):
        norm_grads[label].append((gain_grad, bias_grad))

    for section_index in range(MB):
        gathered = (
            lax.all_gather(reduce_one, ("rows", "img"), axis=0, tiled=True),
            lax.all_gather(offset_one, ("rows", "img"), axis=0, tiled=True),
            lax.all_gather(deform_one, ("rows", "img"), axis=0, tiled=True),
            lax.all_gather(expand_one, ("rows", "img"), axis=0, tiled=True),
            lax.all_gather(mid_gain_one, ("rows", "img"), axis=1, tiled=True),
            lax.all_gather(mid_bias_one, ("rows", "img"), axis=1, tiled=True),
            lax.all_gather(wide_gain_one, ("rows", "img"), axis=0, tiled=True),
            lax.all_gather(wide_bias_one, ("rows", "img"), axis=0, tiled=True),
            lax.all_gather(reduce_two, ("rows", "img"), axis=0, tiled=True),
            lax.all_gather(spatial_two, ("rows", "img"), axis=0, tiled=True),
            lax.all_gather(expand_two, ("rows", "img"), axis=0, tiled=True),
            lax.all_gather(mid_gain_two, ("rows", "img"), axis=1, tiled=True),
            lax.all_gather(mid_bias_two, ("rows", "img"), axis=1, tiled=True),
            lax.all_gather(wide_gain_two, ("rows", "img"), axis=0, tiled=True),
            lax.all_gather(wide_bias_two, ("rows", "img"), axis=0, tiled=True),
        )
        (
            weight_reduce_one,
            weight_offset_one,
            weight_deform_one,
            weight_expand_one,
            gain_mid_one,
            bias_mid_one,
            gain_wide_one,
            bias_wide_one,
            weight_reduce_two,
            weight_spatial_two,
            weight_expand_two,
            gain_mid_two,
            bias_mid_two,
            gain_wide_two,
            bias_wide_two,
        ) = gathered
        channels_mid = weight_reduce_one.shape[1]
        inputs = images_in[section_index * per_section : (section_index + 1) * per_section]
        flat_inputs = inputs.reshape(pixels, channels_wide)
        first_conv = jnp.dot(flat_inputs, weight_reduce_one, preferred_element_type=jnp.float32)
        normed_a1, spread_a1, pre_a1 = norm_forward(first_conv, gain_mid_one[0], bias_mid_one[0])
        hidden = (
            jax.nn.silu(pre_a1)
            .astype(jnp.bfloat16)
            .reshape(per_section, strip_rows, span_cols, channels_mid)
        )
        window = gather_rows(hidden, strip_rows)
        tap_weights = (
            weight_offset_one.reshape(9, channels_wide, 18)
            .transpose(1, 0, 2)
            .reshape(channels_wide, 162)
        )
        partial_offsets = jnp.dot(
            flat_inputs, tap_weights, preferred_element_type=jnp.float32
        ).reshape(per_section, strip_rows, span_cols, 162)
        offset_edges = padded_2(partial_offsets, (("rows", 1),), 2)
        offset_edges = jnp.pad(offset_edges, ((0, 0), (0, 0), (2, 2), (0, 0)))
        offsets = offset_edges[:, 0:strip_rows, 0:span_cols, 0:18]
        for tap_index in range(1, 9):
            row_start = 2 * (tap_index // 3)
            col_start = 2 * (tap_index % 3)
            offsets = (
                offsets
                + offset_edges[
                    :,
                    row_start : row_start + strip_rows,
                    col_start : col_start + span_cols,
                    tap_index * 18 : (tap_index + 1) * 18,
                ]
            )
        squashed = jnp.tanh(offsets / CLIP)
        clipped = CLIP * squashed
        sampler_float, tent_back = jax.vjp(partial(tent_weights, rel_rows=rel_rows), clipped)
        sampler = sampler_float.reshape(
            per_section, strip_rows * span_cols, 9, window_rows * span_cols
        ).astype(jnp.bfloat16)
        flat_window = window.reshape(per_section, window_rows * span_cols, channels_mid)
        sampled = jnp.einsum(
            "npkq,nqm->npkm", sampler, flat_window, preferred_element_type=jnp.float32
        ).astype(jnp.bfloat16)
        flat_sampled = sampled.reshape(pixels, 9 * channels_mid)
        second = jnp.dot(flat_sampled, weight_deform_one, preferred_element_type=jnp.float32)
        normed_a2, spread_a2, pre_a2 = norm_forward(second, gain_mid_one[1], bias_mid_one[1])
        hidden_two = jax.nn.silu(pre_a2).astype(jnp.bfloat16)
        third_conv = jnp.dot(hidden_two, weight_expand_one, preferred_element_type=jnp.float32)
        normed_a3, spread_a3, pre_a3 = norm_forward(third_conv, gain_wide_one, bias_wide_one)
        joined_one = pre_a3 + flat_inputs.astype(jnp.float32)
        middle = jax.nn.silu(joined_one).astype(jnp.bfloat16)
        fourth = jnp.dot(middle, weight_reduce_two, preferred_element_type=jnp.float32)
        normed_b1, spread_b1, pre_b1 = norm_forward(fourth, gain_mid_two[0], bias_mid_two[0])
        inner_one = (
            jax.nn.silu(pre_b1)
            .astype(jnp.bfloat16)
            .reshape(per_section, strip_rows, span_cols, channels_mid)
        )
        inner_rim = padded_2(inner_one, (("rows", 1),), 1)
        inner_pieces = tap_slices(inner_rim, 1, 0, strip_rows, span_cols, False)
        fifth_conv = tap_product(inner_pieces, weight_spatial_two, channels_mid)
        normed_b2, spread_b2, pre_b2 = norm_forward(fifth_conv, gain_mid_two[1], bias_mid_two[1])
        inner_two = jax.nn.silu(pre_b2).astype(jnp.bfloat16)
        sixth_conv = jnp.dot(inner_two, weight_expand_two, preferred_element_type=jnp.float32)
        normed_b3, spread_b3, pre_b3 = norm_forward(sixth_conv, gain_wide_two, bias_wide_two)
        joined_two = pre_b3 + middle.astype(jnp.float32)
        final_sum = jax.nn.silu(joined_two)
        outputs.append(
            final_sum.astype(jnp.bfloat16).reshape(
                per_section, strip_rows, span_cols, channels_wide
            )
        )
        section_weight = grad_weight[
            section_index * per_section : (section_index + 1) * per_section
        ].reshape(pixels, 1)
        upstream = (
            out_grad[section_index * per_section : (section_index + 1) * per_section]
            .reshape(pixels, channels_wide)
            .astype(jnp.float32)
            * section_weight
        )
        masked_six = upstream * silu_slope(joined_two)
        back_sixth, gain_grad, bias_grad = norm_backward(
            masked_six, normed_b3, spread_b3, gain_wide_two
        )
        record("wide_two", gain_grad, bias_grad)
        back_sixth = back_sixth.astype(jnp.bfloat16)
        grad_expand_two = jnp.einsum(
            "pk,pn->kn", inner_two, back_sixth, preferred_element_type=jnp.float32
        )
        masked_five = jnp.einsum(
            "pn,kn->pk", back_sixth, weight_expand_two, preferred_element_type=jnp.float32
        ) * silu_slope(pre_b2)
        back_fifth, gain_grad, bias_grad = norm_backward(
            masked_five, normed_b2, spread_b2, gain_mid_two[1]
        )
        record("mid_two_second", gain_grad, bias_grad)
        back_fifth = back_fifth.astype(jnp.bfloat16)
        grad_spatial_two = tap_weight_grads(inner_pieces, back_fifth)
        back_rim = padded_2(
            back_fifth.reshape(per_section, strip_rows, span_cols, channels_mid), (("rows", 1),), 1
        )
        back_pieces = tap_slices(back_rim, 1, 0, strip_rows, span_cols, True)
        masked_four = tap_transposed(back_pieces, weight_spatial_two, channels_mid) * silu_slope(
            pre_b1
        )
        back_fourth, gain_grad, bias_grad = norm_backward(
            masked_four, normed_b1, spread_b1, gain_mid_two[0]
        )
        record("mid_two_first", gain_grad, bias_grad)
        back_fourth = back_fourth.astype(jnp.bfloat16)
        grad_reduce_two = jnp.einsum(
            "pk,pn->kn", middle, back_fourth, preferred_element_type=jnp.float32
        )
        back_middle = masked_six + jnp.einsum(
            "pn,kn->pk", back_fourth, weight_reduce_two, preferred_element_type=jnp.float32
        )
        masked_three = back_middle * silu_slope(joined_one)
        back_third, gain_grad, bias_grad = norm_backward(
            masked_three, normed_a3, spread_a3, gain_wide_one
        )
        record("wide_one", gain_grad, bias_grad)
        back_third = back_third.astype(jnp.bfloat16)
        grad_expand_one = jnp.einsum(
            "pk,pn->kn", hidden_two, back_third, preferred_element_type=jnp.float32
        )
        masked_two = jnp.einsum(
            "pn,kn->pk", back_third, weight_expand_one, preferred_element_type=jnp.float32
        ) * silu_slope(pre_a2)
        back_second, gain_grad, bias_grad = norm_backward(
            masked_two, normed_a2, spread_a2, gain_mid_one[1]
        )
        record("mid_one_second", gain_grad, bias_grad)
        back_second = back_second.astype(jnp.bfloat16)
        grad_deform_one = jnp.einsum(
            "pk,pn->kn", flat_sampled, back_second, preferred_element_type=jnp.float32
        )
        back_sampled = (
            jnp.einsum(
                "pn,kn->pk", back_second, weight_deform_one, preferred_element_type=jnp.float32
            )
            .astype(jnp.bfloat16)
            .reshape(per_section, strip_rows * span_cols, 9, channels_mid)
        )
        back_window = jnp.einsum(
            "npkq,npkm->nqm", sampler, back_sampled, preferred_element_type=jnp.float32
        )
        back_sampler = jnp.einsum(
            "npkm,nqm->npkq", back_sampled, flat_window, preferred_element_type=jnp.float32
        )
        (back_clipped,) = tent_back(back_sampler.reshape(sampler_float.shape))
        back_offsets = (back_clipped * (1.0 - squashed * squashed)).astype(jnp.bfloat16)
        back_offset_rim = padded_2(back_offsets, (("rows", 1),), 2)
        back_offset_rim = jnp.pad(back_offset_rim, ((0, 0), (0, 0), (2, 2), (0, 0)))
        offset_portions = []
        for tap_index in range(9):
            row_start = 4 - 2 * (tap_index // 3)
            col_start = 4 - 2 * (tap_index % 3)
            offset_portions.append(
                back_offset_rim[
                    :, row_start : row_start + strip_rows, col_start : col_start + span_cols, :
                ]
            )
        stacked_offsets = jnp.concatenate(offset_portions, axis=-1).reshape(pixels, 162)
        grad_offset_one = (
            jnp.einsum(
                "pc,pk->ck", flat_inputs, stacked_offsets, preferred_element_type=jnp.float32
            )
            .reshape(channels_wide, 9, 18)
            .transpose(1, 0, 2)
            .reshape(9 * channels_wide, 18)
        )
        offset_to_images = jnp.einsum(
            "pk,ck->pc", stacked_offsets, tap_weights, preferred_element_type=jnp.float32
        )
        window_grad = back_window.reshape(per_section, window_rows, span_cols, channels_mid)
        own_grad = return_rows(window_grad, strip_rows)
        masked_one = own_grad.reshape(pixels, channels_mid) * silu_slope(pre_a1)
        back_first, gain_grad, bias_grad = norm_backward(
            masked_one, normed_a1, spread_a1, gain_mid_one[0]
        )
        record("mid_one_first", gain_grad, bias_grad)
        back_first = back_first.astype(jnp.bfloat16)
        grad_reduce_one = jnp.einsum(
            "pk,pn->kn", flat_inputs, back_first, preferred_element_type=jnp.float32
        )
        images_grads.append(
            (
                masked_three
                + jnp.einsum(
                    "pn,kn->pk", back_first, weight_reduce_one, preferred_element_type=jnp.float32
                )
                + offset_to_images
            ).reshape(per_section, strip_rows, span_cols, channels_wide)
        )
        section_shards = (
            lax.psum_scatter(grad_reduce_one, ("rows", "img"), scatter_dimension=0, tiled=True),
            lax.psum_scatter(grad_offset_one, ("rows", "img"), scatter_dimension=0, tiled=True),
            lax.psum_scatter(grad_deform_one, ("rows", "img"), scatter_dimension=0, tiled=True),
            lax.psum_scatter(grad_expand_one, ("rows", "img"), scatter_dimension=0, tiled=True),
            lax.psum_scatter(grad_reduce_two, ("rows", "img"), scatter_dimension=0, tiled=True),
            lax.psum_scatter(grad_spatial_two, ("rows", "img"), scatter_dimension=0, tiled=True),
            lax.psum_scatter(grad_expand_two, ("rows", "img"), scatter_dimension=0, tiled=True),
        )
        if weight_totals is None:
            weight_totals = tuple(section_shards)
        else:
            weight_totals = tuple(
                (earlier + later for earlier, later in zip(weight_totals, section_shards))
            )

    def summed(label, member):
        entries = norm_grads[label]
        running = entries[0][member]
        for entry in entries[1:]:
            running = running + entry[member]
        return running

    grad_mid_gain_one = local_slice(
        jnp.stack([summed("mid_one_first", 0), summed("mid_one_second", 0)]), 1
    )
    grad_mid_bias_one = local_slice(
        jnp.stack([summed("mid_one_first", 1), summed("mid_one_second", 1)]), 1
    )
    grad_wide_gain_one = local_slice(summed("wide_one", 0), 0)
    grad_wide_bias_one = local_slice(summed("wide_one", 1), 0)
    grad_mid_gain_two = local_slice(
        jnp.stack([summed("mid_two_first", 0), summed("mid_two_second", 0)]), 1
    )
    grad_mid_bias_two = local_slice(
        jnp.stack([summed("mid_two_first", 1), summed("mid_two_second", 1)]), 1
    )
    grad_wide_gain_two = local_slice(summed("wide_two", 0), 0)
    grad_wide_bias_two = local_slice(summed("wide_two", 1), 0)
    block_out = jnp.concatenate(outputs, axis=0)
    grad_images = jnp.concatenate(images_grads, axis=0)
    return (
        block_out,
        grad_images,
        weight_totals[0],
        weight_totals[1],
        weight_totals[2],
        weight_totals[3],
        grad_mid_gain_one,
        grad_mid_bias_one,
        grad_wide_gain_one,
        grad_wide_bias_one,
        weight_totals[4],
        weight_totals[5],
        weight_totals[6],
        grad_mid_gain_two,
        grad_mid_bias_two,
        grad_wide_gain_two,
        grad_wide_bias_two,
    )


def solution(mesh):
    return jax.shard_map(
        on_device,
        mesh=mesh,
        in_specs=(
            P("img", "rows", None, None),
            P("img", "rows", None, None),
            P("img", None, None),
            P("img", None, None),
            P("img"),
            P("img", "rows", None),
            P(("rows", "img"), None),
            P(("rows", "img"), None),
            P(("rows", "img"), None),
            P(("rows", "img"), None),
            P(None, ("rows", "img")),
            P(None, ("rows", "img")),
            P(("rows", "img")),
            P(("rows", "img")),
            P(("rows", "img"), None),
            P(("rows", "img"), None),
            P(("rows", "img"), None),
            P(None, ("rows", "img")),
            P(None, ("rows", "img")),
            P(("rows", "img")),
            P(("rows", "img")),
        ),
        out_specs=(
            P("img", "rows", None, None),
            P("img", "rows", None, None),
            P(("rows", "img"), None),
            P(("rows", "img"), None),
            P(("rows", "img"), None),
            P(("rows", "img"), None),
            P(None, ("rows", "img")),
            P(None, ("rows", "img")),
            P(("rows", "img")),
            P(("rows", "img")),
            P(("rows", "img"), None),
            P(("rows", "img"), None),
            P(("rows", "img"), None),
            P(None, ("rows", "img")),
            P(None, ("rows", "img")),
            P(("rows", "img")),
            P(("rows", "img")),
        ),
        check_vma=False,
    )
```

profile of v0, /device:TPU:0, one launch (start us, length us, event | category | flops | bytes accessed | tf_op | source)
XLA Modules:
  0.0 2453.6 jit_solution(12911421022610800584)
XLA Ops:
  10.6 46.7 %all-gather = bf16[32,576,18]{1,2,0:T(8,128)(2,1)S(1)} all-gather(bf16[1,576,18]{1,2,0:T(8,128)(2,1)} %bitcast.294), channel_id=1, replica_groups=mesh['rows'=8,'img'=4] {'rows','img'}, dimensions={0}, use_global_device_ids=true | all-gather | bytes 684288 | tf_op jit(solution)/shard_map/all_gather | solution.py:250
  73.4 5.3 collective-permute-start.10
  80.5 39.4 %all-gather.1 = bf16[32,16,2]{1,2,0:T(2,128)(2,1)S(1)} all-gather(bf16[1,16,2]{1,2,0:T(2,128)(2,1)S(1)} %bitcast.328), channel_id=1, replica_groups=mesh['rows'=8,'img'=4] {'rows','img'}, dimensions={0}, use_global_device_ids=true | all-gather | bytes 2112 | tf_op jit(solution)/shard_map/all_gather | solution.py:253
  120.6 36.4 %all-gather.2 = bf16[32,16,2]{1,2,0:T(2,128)(2,1)S(1)} all-gather(bf16[1,16,2]{1,2,0:T(2,128)(2,1)S(1)} %bitcast.329), channel_id=1, replica_groups=mesh['rows'=8,'img'=4] {'rows','img'}, dimensions={0}, use_global_device_ids=true | all-gather | bytes 2112 | tf_op jit(solution)/shard_map/all_gather | solution.py:254
  157.8 37.9 %all-gather.3 = bf16[32,16,2]{1,2,0:T(2,128)(2,1)S(1)} all-gather(bf16[1,16,2]{1,2,0:T(2,128)(2,1)S(1)} %bitcast.330), channel_id=1, replica_groups=mesh['rows'=8,'img'=4] {'rows','img'}, dimensions={0}, use_global_device_ids=true | all-gather | bytes 2112 | tf_op jit(solution)/shard_map/all_gather | solution.py:260
  196.4 36.4 %all-gather.4 = bf16[32,16,2]{1,2,0:T(2,128)(2,1)S(1)} all-gather(bf16[1,16,2]{1,2,0:T(2,128)(2,1)S(1)} %bitcast.331), channel_id=1, replica_groups=mesh['rows'=8,'img'=4] {'rows','img'}, dimensions={0}, use_global_device_ids=true | all-gather | bytes 2112 | tf_op jit(solution)/shard_map/all_gather | solution.py:261
  233.5 5.3 slice_convert_fusion
  239.8 37.4 %all-reduce.28 = (bf16[2048]{0:T(1024)(128)(2,1)S(1)}, bf16[2048]{0:T(1024)(128)(2,1)S(1)}, bf16[2048]{0:T(1024)(128)(2,1)S(1)}, bf16[2048]{0:T(1024)(128)(2,1)S(1)}) all-reduce(bf16[2048]{0:T(1024)(128)(2,1)S(1)} %dynamic-update-slice.29, bf16[2048]{0:T(1024)(128)(2,1)S(1)} %dynamic-update-slice.28, ...), channel_id=1, replica_groups=mesh['rows'=8,'img'=4] {'rows','img'}, use_global_device_ids=true, to_apply=%add.13 | all-reduce | flops 8192 | bytes 32768
  309.5 13.2 multiply_convert_fusion.1
  329.6 43.4 %all-reduce.27 = (f32[512]{0:T(512)}, f32[512]{0:T(512)}, f32[512]{0:T(512)}, f32[512]{0:T(512)}) all-reduce(f32[512]{0:T(512)} %get-tuple-element.395, f32[512]{0:T(512)} %get-tuple-element.394, f32[512]{0:T(512)} %get-tuple-element.387, f32[512]{0:T(512)} %get-tuple-element.386), channel_id=1, replica_groups=mesh['rows'=8,'img'=4] {'rows','img'}, use_global_device_ids=true, to_apply=%region_27.28 | all-reduce | flops 2048 | bytes 16384 | tf_op jit(solution)/shard_map/psum | solution.py:89
  397.3 13.5 multiply_convert_fusion
  410.8 25.1 %convert_element_type.246 = bf16[2,176,9,1056]{3,1,2,0:T(8,128)(2,1)} reshape(bf16[2,4,44,9,24,44]{5,4,2,1,3,0:T(8,128)(2,1)} %multiply_convert_fusion.1) | data formatting | bytes 13381632 | tf_op jit(solution)/shard_map/convert_element_type | solution.py:321
  435.9 25.2 %convert_element_type.261 = bf16[2,176,9,1056]{3,1,2,0:T(8,128)(2,1)} reshape(bf16[2,4,44,9,24,44]{5,4,2,1,3,0:T(8,128)(2,1)} %multiply_convert_fusion) | data formatting | bytes 13381632 | tf_op jit(solution)/shard_map/convert_element_type | solution.py:321
  485.4 15.1 collective-permute-done.5
  501.9 12.7 collective-permute-done.7
  525.5 8.1 copy.309
  533.6 10.8 reshape.896
  544.4 8.1 convolution_convert_fusion.2
  552.5 8.1 copy.321
  560.6 10.0 reshape.910
  570.7 8.0 fusion.225
  582.0 40.5 %all-reduce.26 = (f32[512]{0:T(512)S(1)}, f32[512]{0:T(512)S(1)}, f32[512]{0:T(512)S(1)}, f32[512]{0:T(512)S(1)}) all-reduce(f32[512]{0:T(512)} %get-tuple-element.393, f32[512]{0:T(512)} %get-tuple-element.392, f32[512]{0:T(512)} %get-tuple-element.385, f32[512]{0:T(512)} %get-tuple-element.384), channel_id=1, replica_groups=mesh['rows'=8,'img'=4] {'rows','img'}, use_global_device_ids=true, to_apply=%region_31.32 | all-reduce | flops 2048 | bytes 16384 | tf_op jit(solution)/shard_map/psum | solution.py:89
  629.9 40.2 %all-reduce.25 = (f32[2048]{0:T(1024)S(1)}, f32[2048]{0:T(1024)S(1)}, f32[2048]{0:T(1024)S(1)}, f32[2048]{0:T(1024)S(1)}) all-reduce(f32[2048]{0:T(1024)S(1)} %get-tuple-element.363, f32[2048]{0:T(1024)S(1)} %get-tuple-element.362, f32[2048]{0:T(1024)S(1)} %get-tuple-element.359, ...), channel_id=1, replica_groups=mesh['rows'=8,'img'=4] {'rows','img'}, use_global_device_ids=true, to_apply=%region_35.36 | all-reduce | flops 8192 | bytes 65536 | tf_op jit(solution)/shard_map/psum | solution.py:89
  681.2 40.3 %all-reduce.24 = (f32[512]{0:T(512)S(1)}, f32[512]{0:T(512)S(1)}, f32[512]{0:T(512)S(1)}, f32[512]{0:T(512)S(1)}) all-reduce(f32[512]{0:T(512)S(1)} %get-tuple-element.391, f32[512]{0:T(512)S(1)} %get-tuple-element.390, f32[512]{0:T(512)S(1)} %get-tuple-element.383, ...), channel_id=1, replica_groups=mesh['rows'=8,'img'=4] {'rows','img'}, use_global_device_ids=true, to_apply=%region_39.40 | all-reduce | flops 2048 | bytes 16384 | tf_op jit(solution)/shard_map/psum | solution.py:89
  793.8 40.8 %all-reduce.23 = (f32[512]{0:T(512)S(1)}, f32[512]{0:T(512)S(1)}, f32[512]{0:T(512)S(1)}, f32[512]{0:T(512)S(1)}) all-reduce(f32[512]{0:T(512)S(1)} %get-tuple-element.389, f32[512]{0:T(512)S(1)} %get-tuple-element.388, f32[512]{0:T(512)S(1)} %get-tuple-element.381, ...), channel_id=1, replica_groups=mesh['rows'=8,'img'=4] {'rows','img'}, use_global_device_ids=true, to_apply=%region_43.44 | all-reduce | flops 2048 | bytes 16384 | tf_op jit(solution)/shard_map/psum | solution.py:89
  841.9 41.3 %all-reduce.22 = (f32[2048]{0:T(1024)S(1)}, f32[2048]{0:T(1024)S(1)}, f32[2048]{0:T(1024)S(1)}, f32[2048]{0:T(1024)S(1)}) all-reduce(f32[2048]{0:T(1024)S(1)} %get-tuple-element.361, f32[2048]{0:T(1024)S(1)} %get-tuple-element.360, f32[2048]{0:T(1024)S(1)} %get-tuple-element.357, ...), channel_id=1, replica_groups=mesh['rows'=8,'img'=4] {'rows','img'}, use_global_device_ids=true, to_apply=%region_47.48 | all-reduce | flops 8192 | bytes 65536 | tf_op jit(solution)/shard_map/psum | solution.py:89
  883.3 9.0 fusion.210
  892.3 39.6 %all-reduce.21 = (f32[2048]{0:T(1024)S(1)}, f32[2048]{0:T(1024)S(1)}, f32[2048]{0:T(1024)S(1)}, f32[2048]{0:T(1024)S(1)}) all-reduce(f32[2048]{0:T(1024)S(1)} %get-tuple-element.537, f32[2048]{0:T(1024)S(1)} %get-tuple-element.538, f32[2048]{0:T(1024)S(1)} %get-tuple-element.355, ...), channel_id=1, replica_groups=mesh['rows'=8,'img'=4] {'rows','img'}, use_global_device_ids=true, to_apply=%region_51.52 | all-reduce | flops 8192 | bytes 65536 | tf_op jit(solution)/shard_map/psum | solution.py:98
  932.0 6.1 multiply_convert_fusion.3
  942.3 40.7 %all-reduce.20 = (f32[512]{0:T(512)S(1)}, f32[512]{0:T(512)S(1)}, f32[512]{0:T(512)S(1)}, f32[512]{0:T(512)S(1)}) all-reduce(f32[512]{0:T(512)S(1)} %get-tuple-element.371, f32[512]{0:T(512)S(1)} %get-tuple-element.370, f32[512]{0:T(512)S(1)} %get-tuple-element.379, ...), channel_id=1, replica_groups=mesh['rows'=8,'img'=4] {'rows','img'}, use_global_device_ids=true, to_apply=%region_55.56 | all-reduce | flops 2048 | bytes 16384 | tf_op jit(solution)/shard_map/psum | solution.py:98
  1046.5 41.3 %all-reduce.19 = (f32[512]{0:T(512)S(1)}, f32[512]{0:T(512)S(1)}, f32[512]{0:T(512)S(1)}, f32[512]{0:T(512)S(1)}) all-reduce(f32[512]{0:T(512)S(1)} %get-tuple-element.369, f32[512]{0:T(512)S(1)} %get-tuple-element.368, f32[512]{0:T(512)S(1)} %get-tuple-element.377, ...), channel_id=1, replica_groups=mesh['rows'=8,'img'=4] {'rows','img'}, use_global_device_ids=true, to_apply=%region_59.60 | all-reduce | flops 2048 | bytes 16384 | tf_op jit(solution)/shard_map/psum | solution.py:98
  1090.7 5.9 fusion.209
  1099.1 41.3 %all-reduce.18 = (f32[2048]{0:T(1024)S(1)}, f32[2048]{0:T(1024)S(1)}, f32[2048]{0:T(1024)S(1)}, f32[2048]{0:T(1024)S(1)}) all-reduce(f32[2048]{0:T(1024)S(1)} %get-tuple-element.349, f32[2048]{0:T(1024)S(1)} %get-tuple-element.348, f32[2048]{0:T(1024)S(1)} %get-tuple-element.353, ...), channel_id=1, replica_groups=mesh['rows'=8,'img'=4] {'rows','img'}, use_global_device_ids=true, to_apply=%region_63.64 | all-reduce | flops 8192 | bytes 65536 | tf_op jit(solution)/shard_map/psum | solution.py:98
  1148.8 39.6 %all-reduce.17 = (f32[512]{0:T(512)S(1)}, f32[512]{0:T(512)S(1)}, f32[512]{0:T(512)S(1)}, f32[512]{0:T(512)S(1)}) all-reduce(f32[512]{0:T(512)S(1)} %get-tuple-element.367, f32[512]{0:T(512)S(1)} %get-tuple-element.366, f32[512]{0:T(512)S(1)} %get-tuple-element.375, ...), channel_id=1, replica_groups=mesh['rows'=8,'img'=4] {'rows','img'}, use_global_device_ids=true, to_apply=%region_67.68 | all-reduce | flops 2048 | bytes 16384 | tf_op jit(solution)/shard_map/psum | solution.py:98
  1198.7 6.0 convolution_convert_fusion
  1204.6 7.3 reshape.1001
  1211.9 15.3 fusion.34
  1227.2 10.5 fusion.37
  1237.8 30.0 %reshape.933 = f32[2,4,44,9,24,44]{5,4,2,1,3,0:T(8,128)} reshape(f32[2,176,9,1056]{3,1,2,0:T(8,128)} %fusion.37) | data formatting | bytes 26763264 | tf_op jit(solution)/shard_map/reshape | solution.py:433
  1267.7 28.1 %multiply_reduce_fusion.3 = (f32[2,4,44,9,44]{4,2,1,3,0:T(8,128)}, f32[2,4,44,9,24]{4,2,1,3,0:T(8,128)}) fusion(f32[2,4,44,9,24,44]{5,4,2,1,3,0:T(8,128)} %reshape.933, f32[2,4,44,9,24]{4,2,1,3,0:T(8,128)S(1)} %copy-done.16, f32[2,4,44,9,44]{4,2,1,3,0:T(8,128)S(1)} %copy-done.18), kind=kLoop, calls=%fused_computation.3 | loop fusion | flops 13166208 | bytes 15105024 | tf_op jit(solution)/shard_map/transpose(jvp())/reduce_sum | solution.py:65
  1295.9 30.0 %reshape.948 = f32[2,4,44,9,24,44]{5,4,2,1,3,0:T(8,128)} reshape(f32[2,176,9,1056]{3,1,2,0:T(8,128)} %fusion.34) | data formatting | bytes 26763264 | tf_op jit(solution)/shard_map/reshape | solution.py:433
  1325.8 28.1 %multiply_reduce_fusion.1 = (f32[2,4,44,9,44]{4,2,1,3,0:T(8,128)}, f32[2,4,44,9,24]{4,2,1,3,0:T(8,128)}) fusion(f32[2,4,44,9,24,44]{5,4,2,1,3,0:T(8,128)} %reshape.948, f32[2,4,44,9,24]{4,2,1,3,0:T(8,128)S(1)} %copy-done.12, f32[2,4,44,9,44]{4,2,1,3,0:T(8,128)S(1)} %copy-done.14), kind=kLoop, calls=%fused_computation.1 | loop fusion | flops 13166208 | bytes 15105024 | tf_op jit(solution)/shard_map/transpose(jvp())/reduce_sum | solution.py:65
  1354.0 5.6 fusion.62
  1417.6 11.2 convolution_bitcast_fusion
  1428.8 6.2 copy.333
  1437.3 5.8 collective-permute-start.35
  1444.5 11.1 convolution_bitcast_fusion.1
  1455.5 6.2 copy.325
  1465.6 10.0 collective-permute-start.25
  1477.0 22.0 collective-permute-done.34
  1507.1 19.2 collective-permute-start.37
  1528.8 9.3 collective-permute-done.36
  1545.5 82.6 %all-reduce.16 = (f32[512]{0:T(512)S(1)}, f32[512]{0:T(512)S(1)}, f32[512]{0:T(512)S(1)}, f32[512]{0:T(512)S(1)}) all-reduce(f32[512]{0:T(512)S(1)} %get-tuple-element.556, f32[512]{0:T(512)S(1)} %get-tuple-element.557, f32[512]{0:T(512)S(1)} %get-tuple-element.365, ...), channel_id=1, replica_groups=mesh['rows'=8,'img'=4] {'rows','img'}, use_global_device_ids=true, to_apply=%region_99.100 | all-reduce | flops 2048 | bytes 16384 | tf_op jit(solution)/shard_map/psum | solution.py:98
  1634.9 5.4 copy.361
  1662.6 12.4 add.992
  1680.7 5.3 convolution_add_fusion
  1708.8 5.8 fusion.13
  1720.1 6.2 copy.342
  1729.4 18.3 reduce-scatter.20.cloned.1.call-done
  1747.7 139.9 %reduce-scatter.14.cloned.1.call-done = f32[16,2048]{1,0:T(8,128)} async-done(((f32[512,2048]{1,0:T(8,128)}), f32[16,2048]{1,0:T(8,128)}) %reduce-scatter.14.cloned.1.call-update) | async-done | bytes 131088 | tf_op jit(solution)/shard_map/reduce_scatter | solution.py:482
  1887.7 139.6 %reduce-scatter.16.cloned.1.call-done = f32[64,512]{1,0:T(8,128)} async-done(((f32[2048,512]{1,0:T(8,128)}), f32[64,512]{1,0:T(8,128)}) %reduce-scatter.16.cloned.1.call-update) | async-done | bytes 131088 | tf_op jit(solution)/shard_map/reduce_scatter | solution.py:483
  2027.3 139.8 %reduce-scatter.22.cloned.1.call-done = f32[64,512]{1,0:T(8,128)} async-done(((f32[2048,512]{1,0:T(8,128)}), f32[64,512]{1,0:T(8,128)}) %reduce-scatter.22.cloned.1.call-update) | async-done | bytes 131088
  2167.0 138.7 %reduce-scatter.18.cloned.1.call-done = f32[144,512]{1,0:T(8,128)} async-done(((f32[4608,512]{1,0:T(8,128)}), f32[144,512]{1,0:T(8,128)}) %reduce-scatter.18.cloned.1.call-update) | async-done | bytes 294928 | tf_op jit(solution)/shard_map/reduce_scatter | solution.py:484
  2305.8 141.1 %reduce-scatter.12.cloned.1.call-done = f32[144,512]{1,0:T(8,128)} async-done(((f32[4608,512]{1,0:T(8,128)}), f32[144,512]{1,0:T(8,128)}) %reduce-scatter.12.cloned.1.call-update) | async-done | bytes 294928 | tf_op jit(solution)/shard_map/reduce_scatter | solution.py:481
  (916 shorter events, 465.7 us)
Async XLA Ops:
  7.2 315.5 %all-gather.12.cloned.1.call-start = ((), (), s32[]{:S(2)}) async-start(), calls=%async_computation.7 | async-start | bytes 2162688 | tf_op jit(solution)/shard_map/all_gather | solution.py:249
  7.9 562.8 %all-gather.14.cloned.1.call-start = ((), (), s32[]{:S(2)}) async-start(), calls=%async_computation.8 | async-start | bytes 4866048 | tf_op jit(solution)/shard_map/all_gather | solution.py:251
  8.7 613.9 %all-gather.16.cloned.1.call-start = ((), (), s32[]{:S(2)}) async-start(), calls=%async_computation.9 | async-start | bytes 2162688 | tf_op jit(solution)/shard_map/all_gather | solution.py:252
  9.4 666.1 %all-gather.18.cloned.1.call-start = ((), (), s32[]{:S(2)}) async-start(), calls=%async_computation.10 | async-start | bytes 2162688 | tf_op jit(solution)/shard_map/all_gather | solution.py:257
  10.0 769.5 %all-gather.20.cloned.1.call-start = ((), (), s32[]{:S(2)}) async-start(), calls=%async_computation.11 | async-start | bytes 4866048 | tf_op jit(solution)/shard_map/all_gather | solution.py:258
  10.6 824.1 %all-gather.22.cloned.1.call-start = ((), (), s32[]{:S(2)}) async-start(), calls=%async_computation.12 | async-start | bytes 2162688 | tf_op jit(solution)/shard_map/all_gather | solution.py:259
  66.3 235.4 %collective-permute-start = (f32[2,2,44,162]{2,1,3,0:T(2,128)}, f32[2,2,44,162]{2,1,3,0:T(2,128)S(1)}, u32[]{:S(2)}, u32[]{:S(2)}) collective-permute-start(f32[2,2,44,162]{2,1,3,0:T(2,128)} %get-tuple-element.478), channel_id=1, source_target_pairs={{0,4},{4,8},{8,12},{12,16},{16,20},{20,24},{24,28},{1,5},{5,9},{9,... | collective-permute-start | bytes 342152 | tf_op jit(solution)/shard_map/ppermute | solution.py:31
  67.6 234.1 %collective-permute-start.1 = (f32[2,2,44,162]{2,1,3,0:T(2,128)}, f32[2,2,44,162]{2,1,3,0:T(2,128)}, u32[]{:S(2)}, u32[]{:S(2)}) collective-permute-start(f32[2,2,44,162]{2,1,3,0:T(2,128)} %get-tuple-element.479), channel_id=1, source_target_pairs={{4,0},{8,4},{12,8},{16,12},{20,16},{24,20},{28,24},{5,1},{9,5},{13... | collective-permute-start | bytes 342152 | tf_op jit(solution)/shard_map/ppermute | solution.py:33
  69.0 88.8 %copy-start.231 = (bf16[2,16]{1,0:T(2,128)(2,1)S(1)}, bf16[2,16]{1,0:T(2,128)(2,1)}, u32[]{:S(2)}) copy-start(bf16[2,16]{1,0:T(2,128)(2,1)} %param.78) | copy-start | bytes 196
  69.0 127.4 %copy-start.232 = (bf16[2,16]{1,0:T(2,128)(2,1)S(1)}, bf16[2,16]{1,0:T(2,128)(2,1)}, u32[]{:S(2)}) copy-start(bf16[2,16]{1,0:T(2,128)(2,1)} %param.79) | copy-start | bytes 196
  72.2 166.6 %copy-start.34 = (f32[2,4,44,162]{2,1,3,0:T(4,128)}, f32[2,4,44,162]{2,1,3,0:T(4,128)S(1)}, u32[]{:S(2)}) copy-start(f32[2,4,44,162]{2,1,3,0:T(4,128)S(1)} %copy.313) | copy-start | bytes 684292
  73.4 224.2 %collective-permute-start.10 = (f32[2,2,44,162]{2,1,3,0:T(2,128)}, f32[2,2,44,162]{2,1,3,0:T(2,128)}, u32[]{:S(2)}, u32[]{:S(2)}) collective-permute-start(f32[2,2,44,162]{2,1,3,0:T(2,128)} %get-tuple-element.480), channel_id=1, source_target_pairs={{0,4},{4,8},{8,12},{12,16},{16,20},{20,24},{24,28},{1,5},{5,9},{9,... | collective-permute-start | bytes 342152 | tf_op jit(solution)/shard_map/ppermute | solution.py:31
  78.6 219.0 %collective-permute-start.11 = (f32[2,2,44,162]{2,1,3,0:T(2,128)}, f32[2,2,44,162]{2,1,3,0:T(2,128)}, u32[]{:S(2)}, u32[]{:S(2)}) collective-permute-start(f32[2,2,44,162]{2,1,3,0:T(2,128)} %get-tuple-element.481), channel_id=1, source_target_pairs={{4,0},{8,4},{12,8},{16,12},{20,16},{24,20},{28,24},{5,1},{9,5},{13... | collective-permute-start | bytes 342152 | tf_op jit(solution)/shard_map/ppermute | solution.py:33
  80.0 1647.7 %reduce-scatter.24.cloned.1.call-start = ((), (), s32[]{:S(2)}) async-start(), calls=%async_computation.19 | async-start | bytes 9732096
  80.2 225.3 %copy-start.171 = (f32[4,24]{1,0:T(4,128)}, f32[4,24]{1,0:T(4,128)S(1)}, u32[]{:S(2)}) copy-start(f32[4,24]{1,0:T(4,128)S(1)} %subtract_convert_fusion.1) | copy-start | bytes 1156
  306.9 90.4 %copy-start.11 = (f32[2,4,44,9,24]{4,2,1,3,0:T(8,128)}, f32[2,4,44,9,24]{4,2,1,3,0:T(8,128)S(1)}, u32[]{:S(2)}) copy-start(f32[2,4,44,9,24]{4,2,1,3,0:T(8,128)S(1)} %get-tuple-element.630) | copy-start | bytes 912388
  308.3 89.0 %copy-start.13 = (f32[2,4,44,9,44]{4,2,1,3,0:T(8,128)}, f32[2,4,44,9,44]{4,2,1,3,0:T(8,128)S(1)}, u32[]{:S(2)}) copy-start(f32[2,4,44,9,44]{4,2,1,3,0:T(8,128)S(1)} %get-tuple-element.535) | copy-start | bytes 1672708
  380.5 95.4 %collective-permute-start.4 = (bf16[2,4,44,512]{3,2,1,0:T(8,128)(2,1)}, bf16[2,4,44,512]{3,2,1,0:T(8,128)(2,1)}, u32[]{:S(2)}, u32[]{:S(2)}) collective-permute-start(bf16[2,4,44,512]{3,2,1,0:T(8,128)(2,1)} %reshape.894), channel_id=1, source_target_pairs={{0,4},{4,8},{8,12},{12,16},{16,20},{20,24},{24,28},{1,5},{5,9},{9,... | collective-permute-start | bytes 1081352 | tf_op jit(solution)/shard_map/ppermute | solution.py:20
  385.7 84.5 %collective-permute-start.3 = (bf16[2,4,44,512]{3,2,1,0:T(8,128)(2,1)}, bf16[2,4,44,512]{3,2,1,0:T(8,128)(2,1)}, u32[]{:S(2)}, u32[]{:S(2)}) collective-permute-start(bf16[2,4,44,512]{3,2,1,0:T(8,128)(2,1)} %reshape.894), channel_id=1, source_target_pairs={{0,8},{4,12},{8,16},{12,20},{16,24},{20,28},{1,9},{5,13},{9,17},{1... | collective-permute-start | bytes 1081352 | tf_op jit(solution)/shard_map/ppermute | solution.py:20
  391.4 73.3 %collective-permute-start.12 = (bf16[2,2,44,512]{3,2,1,0:T(8,128)(2,1)}, bf16[2,2,44,512]{3,2,1,0:T(8,128)(2,1)}, u32[]{:S(2)}, u32[]{:S(2)}) collective-permute-start(bf16[2,2,44,512]{3,2,1,0:T(8,128)(2,1)} %get-tuple-element.525), channel_id=1, source_target_pairs={{0,12},{4,16},{8,20},{12,24},{16,28},{1,13},{5,17},{9,21},{13,25},... | collective-permute-start | bytes 540680 | tf_op jit(solution)/shard_map/ppermute | solution.py:20
  394.0 68.5 %collective-permute-start.2 = (bf16[2,2,44,512]{3,2,1,0:T(8,128)(2,1)}, bf16[2,2,44,512]{3,2,1,0:T(8,128)(2,1)}, u32[]{:S(2)}, u32[]{:S(2)}) collective-permute-start(bf16[2,2,44,512]{3,2,1,0:T(8,128)(2,1)} %get-tuple-element.523), channel_id=1, source_target_pairs={{0,12},{4,16},{8,20},{12,24},{16,28},{1,13},{5,17},{9,21},{13,25},... | collective-permute-start | bytes 540680 | tf_op jit(solution)/shard_map/ppermute | solution.py:20
  461.0 55.8 %collective-permute-start.16 = (bf16[2,4,44,512]{3,2,1,0:T(8,128)(2,1)S(1)}, bf16[2,4,44,512]{3,2,1,0:T(8,128)(2,1)S(1)}, u32[]{:S(2)}, u32[]{:S(2)}) collective-permute-start(bf16[2,4,44,512]{3,2,1,0:T(8,128)(2,1)S(1)} %copy-done.67), channel_id=1, source_target_pairs={{8,0},{12,4},{16,8},{20,12},{24,16},{28,20},{9,1},{13,5},{17,9},{2... | collective-permute-start | bytes 1081352 | tf_op jit(solution)/shard_map/ppermute | solution.py:20
  462.5 39.3 %collective-permute-start.15 = (bf16[2,4,44,512]{3,2,1,0:T(8,128)(2,1)S(1)}, bf16[2,4,44,512]{3,2,1,0:T(8,128)(2,1)S(1)}, u32[]{:S(2)}, u32[]{:S(2)}) collective-permute-start(bf16[2,4,44,512]{3,2,1,0:T(8,128)(2,1)S(1)} %copy-done.67), channel_id=1, source_target_pairs={{4,0},{8,4},{12,8},{16,12},{20,16},{24,20},{28,24},{5,1},{9,5},{13... | collective-permute-start | bytes 1081352 | tf_op jit(solution)/shard_map/ppermute | solution.py:20
  464.7 19.2 collective-permute-start.14
  470.3 10.2 collective-permute-start.13
  475.9 25.9 %collective-permute-start.6 = (bf16[2,4,44,512]{3,2,1,0:T(8,128)(2,1)S(1)}, bf16[2,4,44,512]{3,2,1,0:T(8,128)(2,1)S(1)}, u32[]{:S(2)}, u32[]{:S(2)}) collective-permute-start(bf16[2,4,44,512]{3,2,1,0:T(8,128)(2,1)S(1)} %copy-done.68), channel_id=1, source_target_pairs={{8,0},{12,4},{16,8},{20,12},{24,16},{28,20},{9,1},{13,5},{17,9},{2... | collective-permute-start | bytes 1081352 | tf_op jit(solution)/shard_map/ppermute | solution.py:20
  480.5 19.9 collective-permute-start.5
  484.0 32.9 %collective-permute-start.17 = (bf16[2,2,44,512]{3,2,1,0:T(8,128)(2,1)S(1)}, bf16[2,2,44,512]{3,2,1,0:T(8,128)(2,1)S(1)}, u32[]{:S(2)}, u32[]{:S(2)}) collective-permute-start(bf16[2,2,44,512]{3,2,1,0:T(8,128)(2,1)S(1)} %copy-done.142), channel_id=1, source_target_pairs={{12,0},{16,4},{20,8},{24,12},{28,16},{13,1},{17,5},{21,9},{25,13},... | collective-permute-start | bytes 540680 | tf_op jit(solution)/shard_map/ppermute | solution.py:20
  500.4 14.2 collective-permute-start.7
  675.4 207.8 %copy-start.9 = (bf16[352,2048]{1,0:T(8,128)(2,1)}, bf16[352,2048]{1,0:T(8,128)(2,1)S(1)}, u32[]{:S(2)}) copy-start(bf16[352,2048]{1,0:T(8,128)(2,1)S(1)} %get-tuple-element.540) | copy-start | bytes 4325380
  727.8 13.2 collective-permute-start.18
  732.0 9.0 collective-permute-start.19
  734.9 11.7 collective-permute-start.8
  739.5 7.1 collective-permute-start.9
  834.6 149.0 %copy-start.179 = (f32[512]{0:T(512)}, f32[512]{0:T(512)S(1)}, u32[]{:S(2)}) copy-start(f32[512]{0:T(512)S(1)} %get-tuple-element.613) | copy-start | bytes 6148
  834.6 149.0 %copy-start.181 = (f32[512]{0:T(512)}, f32[512]{0:T(512)S(1)}, u32[]{:S(2)}) copy-start(f32[512]{0:T(512)S(1)} %get-tuple-element.614) | copy-start | bytes 6148
  834.6 149.0 %copy-start.214 = (f32[512]{0:T(512)}, f32[512]{0:T(512)S(1)}, u32[]{:S(2)}) copy-start(f32[512]{0:T(512)S(1)} %get-tuple-element.607) | copy-start | bytes 6148
  834.6 149.0 %copy-start.216 = (f32[512]{0:T(512)}, f32[512]{0:T(512)S(1)}, u32[]{:S(2)}) copy-start(f32[512]{0:T(512)S(1)} %get-tuple-element.608) | copy-start | bytes 6148
  986.0 12.5 collective-permute-start.20
  990.2 8.3 collective-permute-start.21
  992.2 10.9 collective-permute-start.30
  996.7 6.5 collective-permute-start.31
  1363.8 11.9 collective-permute-start.28
  1368.0 7.7 collective-permute-start.29
  1369.4 7.3 collective-permute-start.38
  1374.0 5.7 collective-permute-start.39
  1395.6 352.2 %reduce-scatter.20.cloned.1.call-start = ((), (), s32[]{:S(2)}) async-start(), calls=%async_computation.17 | async-start | bytes 4325376 | tf_op jit(solution)/shard_map/reduce_scatter | solution.py:485
  1402.9 484.8 %reduce-scatter.14.cloned.1.call-start = ((), (), s32[]{:S(2)}) async-start(), calls=%async_computation.14 | async-start | bytes 4325376 | tf_op jit(solution)/shard_map/reduce_scatter | solution.py:482
  1410.3 616.9 %reduce-scatter.16.cloned.1.call-start = ((), (), s32[]{:S(2)}) async-start(), calls=%async_computation.15 | async-start | bytes 4325376 | tf_op jit(solution)/shard_map/reduce_scatter | solution.py:483
  1417.4 749.7 %reduce-scatter.22.cloned.1.call-start = ((), (), s32[]{:S(2)}) async-start(), calls=%async_computation.18 | async-start | bytes 4325376
  1436.0 29.6 %collective-permute-start.32 = (f32[2,4,44,512]{3,0,2,1:T(2,128)S(1)}, f32[2,4,44,512]{3,0,2,1:T(2,128)S(1)}, u32[]{:S(2)}, u32[]{:S(2)}) collective-permute-start(f32[2,4,44,512]{3,0,2,1:T(2,128)S(1)} %get-tuple-element.470), channel_id=1, source_target_pairs={{4,0},{8,4},{12,8},{16,12},{20,16},{24,20},{28,24},{5,1},{9,5},{13... | collective-permute-start | bytes 2162696 | tf_op jit(solution)/shard_map/ppermute | solution.py:20
  1437.3 38.3 %collective-permute-start.35 = (f32[2,4,44,512]{3,0,2,1:T(2,128)S(1)}, f32[2,4,44,512]{3,0,2,1:T(2,128)S(1)}, u32[]{:S(2)}, u32[]{:S(2)}) collective-permute-start(f32[2,4,44,512]{3,0,2,1:T(2,128)S(1)} %get-tuple-element.471), channel_id=1, source_target_pairs={{0,8},{4,12},{8,16},{12,20},{16,24},{20,28},{1,9},{5,13},{9,17},{1... | collective-permute-start | bytes 2162696 | tf_op jit(solution)/shard_map/ppermute | solution.py:20
  1443.2 55.8 %collective-permute-start.34 = (f32[2,4,44,512]{3,0,2,1:T(2,128)S(1)}, f32[2,4,44,512]{3,0,2,1:T(2,128)S(1)}, u32[]{:S(2)}, u32[]{:S(2)}) collective-permute-start(f32[2,4,44,512]{3,0,2,1:T(2,128)S(1)} %get-tuple-element.472), channel_id=1, source_target_pairs={{8,0},{12,4},{16,8},{20,12},{24,16},{28,20},{9,1},{13,5},{17,9},{2... | collective-permute-start | bytes 2162696 | tf_op jit(solution)/shard_map/ppermute | solution.py:20
  1461.8 39.9 %collective-permute-start.33 = (f32[2,4,44,512]{3,0,2,1:T(2,128)S(1)}, f32[2,4,44,512]{3,0,2,1:T(2,128)S(1)}, u32[]{:S(2)}, u32[]{:S(2)}) collective-permute-start(f32[2,4,44,512]{3,0,2,1:T(2,128)S(1)} %get-tuple-element.473), channel_id=1, source_target_pairs={{0,4},{4,8},{8,12},{12,16},{16,20},{20,24},{24,28},{1,5},{5,9},{9,... | collective-permute-start | bytes 2162696 | tf_op jit(solution)/shard_map/ppermute | solution.py:20
  1464.3 41.3 %collective-permute-start.22 = (f32[2,4,44,512]{3,0,2,1:T(2,128)S(1)}, f32[2,4,44,512]{3,0,2,1:T(2,128)S(1)}, u32[]{:S(2)}, u32[]{:S(2)}) collective-permute-start(f32[2,4,44,512]{3,0,2,1:T(2,128)S(1)} %get-tuple-element.464), channel_id=1, source_target_pairs={{4,0},{8,4},{12,8},{16,12},{20,16},{24,20},{28,24},{5,1},{9,5},{13... | collective-permute-start | bytes 2162696 | tf_op jit(solution)/shard_map/ppermute | solution.py:20
  1465.6 41.5 %collective-permute-start.25 = (f32[2,4,44,512]{3,0,2,1:T(2,128)S(1)}, f32[2,4,44,512]{3,0,2,1:T(2,128)S(1)}, u32[]{:S(2)}, u32[]{:S(2)}) collective-permute-start(f32[2,4,44,512]{3,0,2,1:T(2,128)S(1)} %get-tuple-element.465), channel_id=1, source_target_pairs={{0,8},{4,12},{8,16},{12,20},{16,24},{20,28},{1,9},{5,13},{9,17},{1... | collective-permute-start | bytes 2162696 | tf_op jit(solution)/shard_map/ppermute | solution.py:20
  1475.7 50.8 %collective-permute-start.24 = (f32[2,4,44,512]{3,0,2,1:T(2,128)S(1)}, f32[2,4,44,512]{3,0,2,1:T(2,128)S(1)}, u32[]{:S(2)}, u32[]{:S(2)}) collective-permute-start(f32[2,4,44,512]{3,0,2,1:T(2,128)S(1)} %get-tuple-element.466), channel_id=1, source_target_pairs={{8,0},{12,4},{16,8},{20,12},{24,16},{28,20},{9,1},{13,5},{17,9},{2... | collective-permute-start | bytes 2162696 | tf_op jit(solution)/shard_map/ppermute | solution.py:20
  1499.0 28.8 %collective-permute-start.23 = (f32[2,4,44,512]{3,0,2,1:T(2,128)S(1)}, f32[2,4,44,512]{3,0,2,1:T(2,128)S(1)}, u32[]{:S(2)}, u32[]{:S(2)}) collective-permute-start(f32[2,4,44,512]{3,0,2,1:T(2,128)S(1)} %get-tuple-element.467), channel_id=1, source_target_pairs={{0,4},{4,8},{8,12},{12,16},{16,20},{20,24},{24,28},{1,5},{5,9},{9,... | collective-permute-start | bytes 2162696 | tf_op jit(solution)/shard_map/ppermute | solution.py:20
  1501.7 39.4 %collective-permute-start.27 = (f32[2,2,44,512]{3,0,2,1:T(2,128)}, f32[2,2,44,512]{3,0,2,1:T(2,128)S(1)}, u32[]{:S(2)}, u32[]{:S(2)}) collective-permute-start(f32[2,2,44,512]{3,0,2,1:T(2,128)} %get-tuple-element.462), channel_id=1, source_target_pairs={{0,12},{4,16},{8,20},{12,24},{16,28},{1,13},{5,17},{9,21},{13,25},... | collective-permute-start | bytes 1081352 | tf_op jit(solution)/shard_map/ppermute | solution.py:20
  1505.6 34.2 %collective-permute-start.26 = (f32[2,2,44,512]{3,0,2,1:T(2,128)}, f32[2,2,44,512]{3,0,2,1:T(2,128)}, u32[]{:S(2)}, u32[]{:S(2)}) collective-permute-start(f32[2,2,44,512]{3,0,2,1:T(2,128)} %get-tuple-element.463), channel_id=1, source_target_pairs={{12,0},{16,4},{20,8},{24,12},{28,16},{13,1},{17,5},{21,9},{25,13},... | collective-permute-start | bytes 1081352 | tf_op jit(solution)/shard_map/ppermute | solution.py:20
  1507.1 31.2 %collective-permute-start.37 = (f32[2,2,44,512]{3,0,2,1:T(2,128)S(1)}, f32[2,2,44,512]{3,0,2,1:T(2,128)S(1)}, u32[]{:S(2)}, u32[]{:S(2)}) collective-permute-start(f32[2,2,44,512]{3,0,2,1:T(2,128)S(1)} %get-tuple-element.468), channel_id=1, source_target_pairs={{0,12},{4,16},{8,20},{12,24},{16,28},{1,13},{5,17},{9,21},{13,25},... | collective-permute-start | bytes 1081352 | tf_op jit(solution)/shard_map/ppermute | solution.py:20
  1526.5 11.7 collective-permute-start.36
  1640.4 665.4 %reduce-scatter.18.cloned.1.call-start = ((), (), s32[]{:S(2)}) async-start(), calls=%async_computation.16 | async-start | bytes 9732096 | tf_op jit(solution)/shard_map/reduce_scatter | solution.py:484
  1675.0 771.9 %reduce-scatter.12.cloned.1.call-start = ((), (), s32[]{:S(2)}) async-start(), calls=%async_computation.13 | async-start | bytes 9732096 | tf_op jit(solution)/shard_map/reduce_scatter | solution.py:481
  (239 other events, 2255.4 us)
Sparse Core Ops, SparseCore 0:
  10.9 60.3 all-gather.11
  74.2 66.5 all-gather.13
  143.6 55.2 all-gather.15
  201.6 55.3 all-gather.17
  259.8 62.6 all-gather.19
  325.2 55.5 all-gather.21
  1395.7 209.1 reduce-scatter.23
  1607.8 139.8 reduce-scatter.19
  1750.7 136.9 reduce-scatter.13
  1890.5 136.7 reduce-scatter.15
  2030.2 136.7 reduce-scatter.21
  2174.4 131.3 reduce-scatter.17
  2312.2 134.5 reduce-scatter.11
where the time goes:
time: 2470 us; the launch traced here: 2450 us
  waiting for transfers between devices  788 us (32%)
  blocking collectives  766 us (31%)
  local copies, waits for them, and re-layouts  348 us (14%)
  matrix products  217 us (9%)
  other arithmetic  192 us (8%)
  starting transfers between devices  124 us (5%)
    psum x6, blocking collectives, norm_backward(): lax.psum((jnp.sum(upstream, axis=0), jnp.sum(upstream * normed, axis=0)),...  285 us
    psum x6, blocking collectives, norm_forward(): lax.psum((jnp.sum(values, axis=0), jnp.sum(values * values, axis=0)), ('r...  246 us
    unnamed x15, waiting for transfers between devices  143 us
    reduce_scatter x1, waiting for transfers between devices, on_device(): lax.psum_scatter(grad_deform_one, ('rows', 'img'), scatter_dimension=0, t...  141 us
    reduce_scatter x1, waiting for transfers between devices, on_device(): lax.psum_scatter(grad_expand_one, ('rows', 'img'), scatter_dimension=0, t...  140 us
    reduce_scatter x1, waiting for transfers between devices, on_device(): lax.psum_scatter(grad_reduce_two, ('rows', 'img'), scatter_dimension=0, t...  140 us
    reduce_scatter x1, waiting for transfers between devices, on_device(): lax.psum_scatter(grad_spatial_two, ('rows', 'img'), scatter_dimension=0,...  139 us
    ppermute x24, starting transfers between devices, from_behind(): lax.ppermute(value, axis, [(source, source + steps) for source in range(f...  79.1 us
  transfers between devices with their start and end apart: 53, of which 15 were waited for; matrix products, arithmetic and copies ran while one was open for 19% of the time, Pallas kernels for 0%

commit v1 on v0

v1 whole, which is shorter than its diff:
```python
from functools import partial

import jax
import jax.numpy as jnp
from jax import lax
from jax.experimental import pallas as pl
from jax.experimental.pallas import tpu as pltpu
from jax.sharding import PartitionSpec as P

CLIP = 8
HALO = 10
MB = 2
BOTH = ("rows", "img")
MIB = 2**20

epsilon = 1e-05
exact = lax.Precision.HIGHEST
f32 = jnp.float32
bf16 = jnp.bfloat16

STRIP_ROWS = 4
COLS = 44
STRIP = STRIP_ROWS * COLS
QUERIES = 9 * STRIP
LANES = 1664
CELLS = (STRIP_ROWS + 2 * HALO) * COLS
ROW_ORDER = (10, 11, 12, 13, 14, 15, 16, 17, 6, 7, 8, 9, 18, 19, 20, 21, 2, 3, 4, 5, 22, 23, 0, 1)


def dot(left, right):
    return jnp.dot(left, right, preferred_element_type=f32)


def dot_nt(left, right):
    return lax.dot_general(left, right, (((1,), (1,)), ((), ())), preferred_element_type=f32)


def dot_tn(left, right):
    return lax.dot_general(left, right, (((0,), (0,)), ((), ())), preferred_element_type=f32)


def device_count():
    return lax.axis_size(BOTH)


def exchange(value, mask):
    return lax.ppermute(value, BOTH, [(i, i ^ mask) for i in range(device_count())])


def all_sum(value):
    count = device_count()
    bit = 1
    while bit < count:
        masks = [bit, 2 * bit, 3 * bit] if 2 * bit < count else [bit]
        parts = [exchange(value, mask) for mask in masks]
        for part in parts:
            value = value + part
        bit *= 4
    return value


def scatter_sum(chunks, order):
    count = device_count()
    me = lax.axis_index(BOTH)
    bits = [1 << k for k in range(count.bit_length() - 1)][::-1]
    value = chunks.reshape((2,) * len(bits) + chunks.shape[1:])
    order = [b for b in order if b in bits] + [b for b in bits[::-1] if b not in order]
    left = list(bits)
    for position, bit in enumerate(order):
        axis = left.index(bit)
        mine = (me // bit) % 2
        keep = lax.dynamic_index_in_dim(value, mine, axis, keepdims=False)
        send = lax.dynamic_index_in_dim(value, 1 - mine, axis, keepdims=False)
        value = keep.astype(f32) + exchange(send, bit).astype(f32)
        if position < len(order) - 1:
            value = value.astype(bf16)
        left.pop(axis)
    return value


def from_behind(value, steps):
    count = lax.axis_size("rows")
    first, last = (max(0, -steps), min(count, count - steps))
    return lax.ppermute(value, "rows", [(source, source + steps) for source in range(first, last)])


def spline(values):
    magnitude = jnp.abs(values)
    outer = 1.5 - magnitude
    return jnp.where(
        magnitude < 0.5,
        0.75 - values * values,
        jnp.where(magnitude < 1.5, 0.5 * outer * outer, 0.0),
    )


def spline_slope(values):
    magnitude = jnp.abs(values)
    outer = 1.5 - magnitude
    return jnp.where(
        magnitude < 0.5,
        -2.0 * values,
        jnp.where(magnitude < 1.5, jnp.where(values > 0, -outer, outer), 0.0),
    )


def fill_factors(pos_ref, row_ref, col_weight, row_weight, col_slope=None, row_slope=None):
    cell_cols = lax.broadcasted_iota(jnp.int32, (2 * COLS, LANES), 0)
    cell_cols = jnp.where(cell_cols >= COLS, cell_cols - COLS, cell_cols).astype(f32)
    col_gap = pos_ref[0, 1:2, :] - cell_cols
    row_gap = pos_ref[0, 0:1, :] - row_ref[...]
    col_weight[...] = spline(col_gap)
    row_weight[...] = spline(row_gap)
    if col_slope is not None:
        col_slope[...] = spline_slope(col_gap)
        row_slope[...] = spline_slope(row_gap)


def fill_sampler(col_weight, row_weight, sampler):
    low = lax.broadcasted_iota(jnp.int32, (8, 128), 0) < 4

    def body(tile, carry):
        lanes = pl.ds(pl.multiple_of(tile * 128, 128), 128)
        for block in range(6):
            for chunk in range(11):
                halves = []
                for group in (2 * chunk, 2 * chunk + 1):
                    first, last = (8 * group) // COLS, (8 * group + 7) // COLS
                    weight = row_weight[4 * block + first : 4 * block + first + 1, lanes]
                    if first != last:
                        weight = jnp.where(
                            low, weight, row_weight[4 * block + last : 4 * block + last + 1, lanes]
                        )
                    local = group % 11
                    halves.append(col_weight[8 * local : 8 * local + 8, lanes] * weight)
                start = block * STRIP + 16 * chunk
                sampler[start : start + 16, lanes] = jnp.concatenate(halves, axis=0).astype(bf16)
        return carry

    lax.fori_loop(0, LANES // 128, body, 0)


def fill_window(pieces, window):
    for index, piece in enumerate(pieces[:5]):
        window[index * STRIP : (index + 1) * STRIP, :] = piece[0]
    window[5 * STRIP : 6 * STRIP, :] = jnp.concatenate([pieces[5][0], pieces[6][0]], axis=0)


def sample_kernel(pos_ref, row_ref, *refs):
    pieces, out_ref = refs[:7], refs[7]
    col_weight, row_weight, sampler, window = refs[8:]
    fill_factors(pos_ref, row_ref, col_weight, row_weight)
    fill_sampler(col_weight, row_weight, sampler)
    fill_window(pieces, window)
    result = dot_tn(window[...], sampler[...]).T.astype(bf16)
    width = window.shape[1]
    for tap in range(9):
        out_ref[0, :, tap * width : (tap + 1) * width] = result[tap * STRIP : (tap + 1) * STRIP]


def sample_back_kernel(pos_ref, row_ref, *refs):
    pieces, upstream_ref = refs[:7], refs[7]
    grads, pos_grad = refs[8:15], refs[15]
    (
        col_weight,
        row_weight,
        col_slope,
        row_slope,
        sampler,
        window,
        upstream,
        sampler_grad,
    ) = refs[16:]
    fill_factors(pos_ref, row_ref, col_weight, row_weight, col_slope, row_slope)
    fill_sampler(col_weight, row_weight, sampler)
    fill_window(pieces, window)
    width = window.shape[1]
    for tap in range(9):
        upstream[tap * STRIP : (tap + 1) * STRIP, :] = upstream_ref[
            0, :, tap * width : (tap + 1) * width
        ]
    upstream[QUERIES:LANES, :] = jnp.zeros((LANES - QUERIES, width), bf16)
    sampler_grad[...] = dot_nt(window[...], upstream[...])
    for index, grad in enumerate(grads[:5]):
        grad[0] = dot(sampler[index * STRIP : (index + 1) * STRIP, :], upstream[...]).astype(
            grad.dtype
        )
    last = dot(sampler[5 * STRIP :, :], upstream[...])
    grads[5][0] = last[: STRIP // 2].astype(bf16)
    grads[6][0] = last[STRIP // 2 :].astype(bf16)
    low = lax.broadcasted_iota(jnp.int32, (8, 128), 0) < 4

    def body(tile, carry):
        lanes = pl.ds(pl.multiple_of(tile * 128, 128), 128)
        zero = jnp.zeros((8, 128), f32)
        weights = [col_weight[8 * group : 8 * group + 8, lanes] for group in range(11)]
        middle_low = jnp.where(low, weights[5], 0.0)
        middle_high = jnp.where(low, 0.0, weights[5])
        row_total = zero
        col_totals = [zero] * 11
        for pair in range(12):
            first = row_weight[2 * pair : 2 * pair + 1, lanes]
            second = row_weight[2 * pair + 1 : 2 * pair + 2, lanes]
            mixed = jnp.where(low, first, second)
            first_sum = zero
            second_sum = zero
            for group in range(11):
                start = 88 * pair + 8 * group
                value = sampler_grad[start : start + 8, lanes]
                if group < 5:
                    first_sum = first_sum + value * weights[group]
                    col_totals[group] = col_totals[group] + value * first
                elif group > 5:
                    second_sum = second_sum + value * weights[group]
                    col_totals[group] = col_totals[group] + value * second
                else:
                    first_sum = first_sum + value * middle_low
                    second_sum = second_sum + value * middle_high
                    col_totals[group] = col_totals[group] + value * mixed
            row_total = (
                row_total
                + first_sum * row_slope[2 * pair : 2 * pair + 1, lanes]
                + second_sum * row_slope[2 * pair + 1 : 2 * pair + 2, lanes]
            )
        col_total = zero
        for group in range(11):
            col_total = col_total + col_totals[group] * col_slope[8 * group : 8 * group + 8, lanes]
        pos_grad[0, 0:1, lanes] = jnp.sum(row_total, axis=0, keepdims=True)
        pos_grad[0, 1:2, lanes] = jnp.sum(col_total, axis=0, keepdims=True)
        return carry

    lax.fori_loop(0, LANES // 128, body, 0)


def piece_specs(width):
    full = pl.BlockSpec((1, STRIP, width), lambda i: (i, 0, 0))
    half = pl.BlockSpec((1, STRIP // 2, width), lambda i: (i, 0, 0))
    return [full] * 5 + [half] * 2


def sampler_specs(width):
    return [
        pl.BlockSpec((1, 2, LANES), lambda i: (i, 0, 0)),
        pl.BlockSpec((len(ROW_ORDER), 1), lambda i: (0, 0)),
    ] + piece_specs(width)


def row_ids():
    return jnp.array(ROW_ORDER, f32)[:, None]


def sample(positions, pieces):
    images, _, width = pieces[0].shape
    return pl.pallas_call(
        sample_kernel,
        grid=(images,),
        in_specs=sampler_specs(width),
        out_specs=pl.BlockSpec((1, STRIP, 9 * width), lambda i: (i, 0, 0)),
        out_shape=jax.ShapeDtypeStruct((images, STRIP, 9 * width), bf16),
        scratch_shapes=[
            pltpu.VMEM((2 * COLS, LANES), f32),
            pltpu.VMEM((len(ROW_ORDER), LANES), f32),
            pltpu.VMEM((CELLS, LANES), bf16),
            pltpu.VMEM((CELLS, width), bf16),
        ],
        compiler_params=pltpu.CompilerParams(vmem_limit_bytes=40 * MIB),
        cost_estimate=pl.CostEstimate(
            flops=2 * images * CELLS * LANES * width,
            bytes_accessed=2 * images * (CELLS + QUERIES) * width,
            transcendentals=0,
        ),
        name="sample",
    )(positions, row_ids(), *pieces)


def sample_back(positions, pieces, upstream):
    images, _, width = pieces[0].shape
    full = (images, STRIP, width)
    half = (images, STRIP // 2, width)
    return pl.pallas_call(
        sample_back_kernel,
        grid=(images,),
        in_specs=sampler_specs(width)
        + [pl.BlockSpec((1, STRIP, 9 * width), lambda i: (i, 0, 0))],
        out_specs=piece_specs(width) + [pl.BlockSpec((1, 2, LANES), lambda i: (i, 0, 0))],
        out_shape=[jax.ShapeDtypeStruct(full, f32)]
        + [jax.ShapeDtypeStruct(full, bf16)] * 4
        + [jax.ShapeDtypeStruct(half, bf16)] * 2
        + [jax.ShapeDtypeStruct((images, 2, LANES), f32)],
        scratch_shapes=[
            pltpu.VMEM((2 * COLS, LANES), f32),
            pltpu.VMEM((len(ROW_ORDER), LANES), f32),
            pltpu.VMEM((2 * COLS, LANES), f32),
            pltpu.VMEM((len(ROW_ORDER), LANES), f32),
            pltpu.VMEM((CELLS, LANES), bf16),
            pltpu.VMEM((CELLS, width), bf16),
            pltpu.VMEM((LANES, width), bf16),
            pltpu.VMEM((CELLS, LANES), f32),
        ],
        compiler_params=pltpu.CompilerParams(vmem_limit_bytes=48 * MIB),
        cost_estimate=pl.CostEstimate(
            flops=4 * images * CELLS * LANES * width,
            bytes_accessed=4 * images * (CELLS + QUERIES) * width,
            transcendentals=0,
        ),
        name="sample_back",
    )(positions, row_ids(), *pieces, upstream)


def tap_slabs(above, own, below, padded, image):
    padded[8 : 8 + COLS, :] = above[image].astype(f32)
    padded[8 + COLS : 8 + COLS + STRIP, :] = own[image].astype(f32)
    padded[8 + COLS + STRIP : 8 + 2 * COLS + STRIP, :] = below[image].astype(f32)
    cols = lax.broadcasted_iota(jnp.int32, (STRIP, 1), 0) % COLS
    for tap in range(9):
        start = 8 + COLS * (tap // 3) + tap % 3 - 1
        slab = padded[start : start + STRIP, :]
        if tap % 3 == 0:
            slab = jnp.where(cols > 0, slab, 0.0)
        elif tap % 3 == 2:
            slab = jnp.where(cols < COLS - 1, slab, 0.0)
        yield tap, slab.astype(bf16)


def conv_kernel(above, own, below, weight, out_ref, slabs_ref, padded):
    width = own.shape[2]
    images = own.shape[0]
    for image in range(images):
        for tap, slab in tap_slabs(above, own, below, padded, image):
            slabs_ref[image, :, tap * width : (tap + 1) * width] = slab
    total = None
    for tap in range(9):
        lanes = slice(tap * width, (tap + 1) * width)
        part = dot(slabs_ref[:, :, lanes].reshape(images * STRIP, width), weight[lanes, :])
        total = part if total is None else total + part
    out_ref[...] = total.reshape(out_ref.shape)


def conv_back_kernel(above, own, below, weight, out_ref, padded, slabs):
    width = own.shape[2]
    images = own.shape[0]
    for image in range(images):
        for tap, slab in tap_slabs(above, own, below, padded, image):
            slabs[8 - tap, image * STRIP : (image + 1) * STRIP, :] = slab
    total = None
    for tap in range(9):
        part = dot_nt(slabs[tap], weight[tap * width : (tap + 1) * width, :])
        total = part if total is None else total + part
    out_ref[...] = total.reshape(out_ref.shape)


def conv_specs(images, width):
    rim = pl.BlockSpec((images, COLS, width), lambda i: (i, 0, 0))
    own = pl.BlockSpec((images, STRIP, width), lambda i: (i, 0, 0))
    return [rim, own, rim, pl.BlockSpec((9 * width, width), lambda i: (0, 0))]


def conv(above, own, below, weight):
    images, _, width = own.shape
    step = images // MB
    return pl.pallas_call(
        conv_kernel,
        grid=(MB,),
        in_specs=conv_specs(step, width),
        out_specs=[
            pl.BlockSpec((step, STRIP, width), lambda i: (i, 0, 0)),
            pl.BlockSpec((step, STRIP, 9 * width), lambda i: (i, 0, 0)),
        ],
        out_shape=[
            jax.ShapeDtypeStruct((images, STRIP, width), f32),
            jax.ShapeDtypeStruct((images, STRIP, 9 * width), bf16),
        ],
        scratch_shapes=[pltpu.VMEM((16 + 2 * COLS + STRIP, width), f32)],
        compiler_params=pltpu.CompilerParams(vmem_limit_bytes=40 * MIB),
        cost_estimate=pl.CostEstimate(
            flops=18 * images * STRIP * width * width,
            bytes_accessed=18 * width * width,
            transcendentals=0,
        ),
        name="conv",
    )(above, own, below, weight)


def conv_back(above, own, below, weight):
    images, _, width = own.shape
    step = images // MB
    return pl.pallas_call(
        conv_back_kernel,
        grid=(MB,),
        in_specs=conv_specs(step, width),
        out_specs=pl.BlockSpec((step, STRIP, width), lambda i: (i, 0, 0)),
        out_shape=jax.ShapeDtypeStruct((images, STRIP, width), f32),
        scratch_shapes=[
            pltpu.VMEM((16 + 2 * COLS + STRIP, width), f32),
            pltpu.VMEM((9, step * STRIP, width), bf16),
        ],
        compiler_params=pltpu.CompilerParams(vmem_limit_bytes=40 * MIB),
        cost_estimate=pl.CostEstimate(
            flops=18 * images * STRIP * width * width,
            bytes_accessed=18 * width * width,
            transcendentals=0,
        ),
        name="conv_back",
    )(above, own, below, weight)


def silu_slope(values):
    logistic = jax.nn.sigmoid(values)
    return logistic * (1.0 + values * (1.0 - logistic))


def box_weights(box_rows, box_cols, box_count, valid_mask, strip_rows, span_cols):
    row_ids_ = lax.axis_index("rows") * strip_rows + jnp.arange(strip_rows)
    col_ids = jnp.arange(span_cols)
    row_low = jnp.minimum(box_rows[..., 0], box_rows[..., 1])
    row_high = jnp.maximum(box_rows[..., 0], box_rows[..., 1])
    col_low = jnp.minimum(box_cols[..., 0], box_cols[..., 1])
    col_high = jnp.maximum(box_cols[..., 0], box_cols[..., 1])
    inside_rows = ((row_ids_ >= row_low[..., None]) & (row_ids_ <= row_high[..., None])).astype(f32)
    inside_cols = ((col_ids >= col_low[..., None]) & (col_ids <= col_high[..., None])).astype(f32)
    live_boxes = (jnp.arange(box_rows.shape[1])[None, :] < box_count[:, None]).astype(f32)
    covered = jnp.einsum("ib,ibh,ibw->ihw", live_boxes, inside_rows, inside_cols, precision=exact)
    return valid_mask.astype(f32) * (0.5 + covered / box_count.astype(f32)[:, None, None])


def per_batch(values):
    return values.reshape(MB, values.shape[0] // MB, values.shape[1])


def batch_totals(first, second):
    totals = all_sum(jnp.concatenate([jnp.sum(first, axis=1), jnp.sum(second, axis=1)], axis=0))
    return totals[:MB], totals[MB:]


class Norm:
    def __init__(self, values, gain, bias):
        values = per_batch(values)
        self.count = values.shape[1] * device_count()
        sums, squares = batch_totals(values, values * values)
        self.values = values
        self.center = (sums / self.count)[:, None, :]
        self.spread = lax.rsqrt(squares[:, None, :] / self.count - self.center * self.center + epsilon)
        self.gain = gain.astype(f32)
        self.bias = bias.astype(f32)

    def normed(self):
        return (self.values - self.center) * self.spread

    def forward(self):
        return self.normed() * self.gain + self.bias

    def backward(self, upstream):
        normed = self.normed()
        bias_sums, gain_sums = batch_totals(upstream, upstream * normed)
        self.gain_grad = jnp.sum(gain_sums, axis=0)
        self.bias_grad = jnp.sum(bias_sums, axis=0)
        result = (self.spread * self.gain) * (
            upstream
            - (bias_sums / self.count)[:, None, :]
            - normed * (gain_sums / self.count)[:, None, :]
        )
        return result.astype(bf16).reshape(-1, result.shape[-1])


def stacked_columns(weight, width):
    return jnp.concatenate(jnp.split(weight, weight.shape[1] // width, axis=1), axis=0)


def unstacked_columns(blocks, columns):
    count, stacked, width = blocks.shape
    parts = columns // width
    blocks = blocks.reshape(count, parts, stacked // parts, width).transpose(0, 2, 1, 3)
    return blocks.reshape(-1, columns)


def gather(pieces):
    whole = lax.all_gather(jnp.concatenate(pieces, axis=0), BOTH, axis=0)
    results = []
    start = 0
    for piece in pieces:
        results.append(whole[:, start : start + piece.shape[0]])
        start += piece.shape[0]
    return results


def to_width(flat, width):
    rows = -(-flat.shape[-1] // width)
    pad = rows * width - flat.shape[-1]
    return jnp.pad(flat, [(0, 0)] * (flat.ndim - 1) + [(0, pad)]).reshape(
        flat.shape[:-1] + (rows, width)
    )


def shifted(values, steps, columns):
    if steps == 0:
        return values
    cells = values.shape[-1]
    column = jnp.arange(cells) % columns
    pad = [(0, 0)] * (values.ndim - 1)
    if steps > 0:
        moved = jnp.pad(values[..., steps:], pad + [(0, steps)])
    else:
        moved = jnp.pad(values[..., :steps], pad + [(-steps, 0)])
    return jnp.where((column + steps >= 0) & (column + steps < columns), moved, 0)


def on_device(
    images_in,
    out_grad,
    box_rows,
    box_cols,
    box_count,
    valid_mask,
    reduce_one,
    offset_one,
    deform_one,
    expand_one,
    mid_gain_one,
    mid_bias_one,
    wide_gain_one,
    wide_bias_one,
    reduce_two,
    spatial_two,
    expand_two,
    mid_gain_two,
    mid_bias_two,
    wide_gain_two,
    wide_bias_two,
):
    images, strip_rows, span_cols, wide = images_in.shape
    mid = reduce_one.shape[1]
    assert strip_rows == STRIP_ROWS and span_cols == COLS
    count = device_count()
    pixels = images * STRIP

    vectors = jnp.concatenate(
        [mid_gain_one, mid_bias_one, mid_gain_two, mid_bias_two], axis=0
    ).reshape(-1)
    vectors = jnp.concatenate(
        [vectors, wide_gain_one, wide_bias_one, wide_gain_two, wide_bias_two]
    )
    vector_count = vectors.shape[0]
    offset_rows = offset_one.shape[0]
    offset_piece = to_width(offset_one.T, mid).transpose(1, 0, 2).reshape(-1, mid)
    reduce_all, offset_all, vector_all = gather(
        [reduce_one, offset_piece, to_width(vectors, mid)]
    )
    deform_all, expand_all = gather([deform_one, stacked_columns(expand_one, mid)])
    reduce_two_all, spatial_all, expand_two_all = gather(
        [reduce_two, spatial_two, stacked_columns(expand_two, mid)]
    )
    weight_reduce_one = reduce_all.reshape(wide, mid)
    weight_deform_one = deform_all.reshape(9 * mid, mid)
    weight_expand_one = unstacked_columns(expand_all, wide)
    weight_reduce_two = reduce_two_all.reshape(wide, mid)
    weight_spatial_two = spatial_all.reshape(9 * mid, mid)
    weight_expand_two = unstacked_columns(expand_two_all, wide)
    tap_weights = (
        offset_all.reshape(count, -1, 18, mid)
        .transpose(2, 0, 1, 3)
        .reshape(18, count, -1)[:, :, :offset_rows]
        .reshape(18, 9, wide)
        .transpose(1, 0, 2)
        .reshape(162, wide)
    )
    vector_all = vector_all.reshape(count, -1)[:, :vector_count]
    mid_part = mid // count
    wide_part = wide // count
    mid_vectors = (
        vector_all[:, : 8 * mid_part].reshape(count, 8, mid_part).transpose(1, 0, 2).reshape(8, mid)
    )
    wide_vectors = (
        vector_all[:, 8 * mid_part :].reshape(count, 4, wide_part).transpose(1, 0, 2).reshape(4, wide)
    )
    gain_mid_one, bias_mid_one = mid_vectors[0:2], mid_vectors[2:4]
    gain_mid_two, bias_mid_two = mid_vectors[4:6], mid_vectors[6:8]

    def maps(values):
        return values.reshape(images, STRIP, values.shape[-1])

    grad_weight = box_weights(box_rows, box_cols, box_count, valid_mask, strip_rows, span_cols)
    flat_inputs = images_in.reshape(pixels, wide)

    norm_a1 = Norm(dot(flat_inputs, weight_reduce_one), gain_mid_one[0], bias_mid_one[0])
    hidden = jax.nn.silu(norm_a1.forward()).astype(bf16).reshape(images, STRIP, mid)
    half = STRIP // 2
    pieces = [
        hidden,
        from_behind(hidden, -1),
        from_behind(hidden, 1),
        from_behind(hidden, -2),
        from_behind(hidden, 2),
        from_behind(hidden[:, :half], -3),
        from_behind(hidden[:, half:], 3),
    ]

    partial_offsets = dot_nt(tap_weights, flat_inputs).reshape(3, 54, images, STRIP)
    from_above = from_behind(partial_offsets[0, :, :, half:], 1)
    from_below = from_behind(partial_offsets[2, :, :, :half], -1)
    by_row = [
        jnp.concatenate([from_above, partial_offsets[0, :, :, :half]], axis=-1),
        partial_offsets[1],
        jnp.concatenate([partial_offsets[2, :, :, half:], from_below], axis=-1),
    ]
    offsets = 0.0
    for row in by_row:
        for col_tap in range(3):
            offsets = offsets + shifted(
                row[18 * col_tap : 18 * col_tap + 18], 2 * (col_tap - 1), COLS
            )
    squashed = jnp.tanh(offsets / CLIP)
    taps = jnp.arange(9)
    cells = jnp.arange(STRIP)
    row_base = ((taps // 3 - 1)[:, None] + (cells // COLS + HALO)[None, :]).astype(f32)
    col_base = ((taps % 3 - 1)[:, None] + (cells % COLS)[None, :]).astype(f32)
    base = jnp.stack([row_base, col_base])[:, :, None, :]
    positions = (CLIP * squashed).reshape(2, 9, images, STRIP) + base
    positions = positions.transpose(2, 0, 1, 3).reshape(images, 2, QUERIES)
    positions = jnp.pad(
        positions, ((0, 0), (0, 0), (0, LANES - QUERIES)), constant_values=-1000.0
    )
    sampled = sample(positions, pieces).reshape(pixels, 9 * mid)
    norm_a2 = Norm(dot(sampled, weight_deform_one), gain_mid_one[1], bias_mid_one[1])
    hidden_two = jax.nn.silu(norm_a2.forward()).astype(bf16).reshape(pixels, mid)
    norm_a3 = Norm(dot(hidden_two, weight_expand_one), wide_vectors[0], wide_vectors[1])
    joined_one = norm_a3.forward() + per_batch(flat_inputs).astype(f32)
    middle = jax.nn.silu(joined_one).astype(bf16).reshape(pixels, wide)

    norm_b1 = Norm(dot(middle, weight_reduce_two), gain_mid_two[0], bias_mid_two[0])
    inner_one = maps(jax.nn.silu(norm_b1.forward()).astype(bf16))
    fifth_conv, inner_slabs = conv(
        from_behind(inner_one[:, STRIP - COLS :], 1),
        inner_one,
        from_behind(inner_one[:, :COLS], -1),
        weight_spatial_two,
    )
    norm_b2 = Norm(fifth_conv.reshape(pixels, mid), gain_mid_two[1], bias_mid_two[1])
    inner_two = jax.nn.silu(norm_b2.forward()).astype(bf16).reshape(pixels, mid)
    norm_b3 = Norm(dot(inner_two, weight_expand_two), wide_vectors[2], wide_vectors[3])
    joined_two = norm_b3.forward() + per_batch(middle).astype(f32)
    block_out = jax.nn.silu(joined_two).astype(bf16).reshape(images_in.shape)

    upstream = per_batch(
        out_grad.reshape(pixels, wide)
    ).astype(f32) * grad_weight.reshape(MB, pixels // MB, 1)
    masked_six = upstream * silu_slope(joined_two)
    back_sixth = norm_b3.backward(masked_six)
    grad_expand_two = dot_tn(inner_two, back_sixth).astype(bf16)
    back_fifth = norm_b2.backward(
        per_batch(dot_nt(back_sixth, weight_expand_two)) * silu_slope(norm_b2.forward())
    )
    grad_spatial_two = dot_tn(inner_slabs.reshape(pixels, 9 * mid), back_fifth).astype(bf16)
    back_maps = maps(back_fifth)
    back_inner = conv_back(
        from_behind(back_maps[:, STRIP - COLS :], 1),
        back_maps,
        from_behind(back_maps[:, :COLS], -1),
        weight_spatial_two,
    ).reshape(pixels, mid)
    back_fourth = norm_b1.backward(per_batch(back_inner) * silu_slope(norm_b1.forward()))
    grad_reduce_two = dot_tn(middle, back_fourth).astype(bf16)

    def chunked(grad):
        return grad.reshape(count, -1, mid)

    def chunked_columns(grad):
        parts = grad.shape[1] // mid
        return (
            grad.reshape(count, -1, parts, mid).transpose(0, 2, 1, 3).reshape(count, -1, mid)
        )

    def unchunked_columns(shard):
        parts = wide // mid
        return shard.reshape(parts, -1, mid).transpose(1, 0, 2).reshape(-1, wide)

    def split_rows(shard, sizes):
        results = []
        start = 0
        for size in sizes:
            results.append(shard[start : start + size])
            start += size
        return results

    two_sizes = [reduce_two.shape[0], spatial_two.shape[0], expand_two.shape[0] * wide // mid]
    two_chunks = jnp.concatenate(
        [chunked(grad_reduce_two), chunked(grad_spatial_two), chunked_columns(grad_expand_two)],
        axis=1,
    )
    two_shards = split_rows(
        lax.psum_scatter(
            two_chunks.reshape(-1, mid), BOTH, scatter_dimension=0, tiled=True
        ).astype(f32),
        two_sizes,
    )

    back_middle = masked_six + per_batch(dot_nt(back_fourth, weight_reduce_two))
    masked_three = back_middle * silu_slope(joined_one)
    back_third = norm_a3.backward(masked_three)
    grad_expand_one = dot_tn(hidden_two, back_third).astype(bf16)
    back_second = norm_a2.backward(
        per_batch(dot_nt(back_third, weight_expand_one)) * silu_slope(norm_a2.forward())
    )
    grad_deform_one = dot_tn(sampled, back_second).astype(bf16)
    one_sizes = [deform_one.shape[0], expand_one.shape[0] * wide // mid]
    one_shards = split_rows(
        scatter_sum(
            jnp.concatenate([chunked(grad_deform_one), chunked_columns(grad_expand_one)], axis=1),
            (1, 4, 2, 8, 16),
        ),
        one_sizes,
    )
    back_sampled = dot_nt(back_second, weight_deform_one).astype(bf16).reshape(images, STRIP, -1)
    own, *others, position_grad = sample_back(positions, pieces, back_sampled)
    own = (
        own
        + from_behind(others[0], 1).astype(f32)
        + from_behind(others[1], -1).astype(f32)
        + from_behind(others[2], 2).astype(f32)
        + from_behind(others[3], -2).astype(f32)
        + jnp.concatenate(
            [from_behind(others[4], 3).astype(f32), from_behind(others[5], -3).astype(f32)], axis=1
        )
    )
    back_clipped = (
        position_grad[:, :, :QUERIES]
        .reshape(images, 2, 9, STRIP)
        .transpose(1, 2, 0, 3)
        .reshape(18, images, STRIP)
    )
    back_offsets = (back_clipped * (1.0 - squashed * squashed)).astype(bf16)
    rim_above = from_behind(back_offsets[:, :, half:], 1)
    rim_below = from_behind(back_offsets[:, :, :half], -1)
    by_row = [
        jnp.concatenate([back_offsets[:, :, half:], rim_below], axis=-1),
        back_offsets,
        jnp.concatenate([rim_above, back_offsets[:, :, :half]], axis=-1),
    ]
    stacked = jnp.concatenate(
        [shifted(row, -2 * (col_tap - 1), COLS) for row in by_row for col_tap in range(3)], axis=0
    ).reshape(162, pixels)
    grad_offset_one = dot(stacked, flat_inputs).astype(bf16)
    grad_offset_one = (
        grad_offset_one.reshape(9, 18, wide)
        .transpose(1, 0, 2)
        .reshape(18, count, offset_rows)
        .transpose(1, 0, 2)
    )
    offset_chunks = to_width(grad_offset_one, mid).transpose(0, 2, 1, 3).reshape(count, -1, mid)
    offset_to_images = dot_tn(stacked, tap_weights)

    back_first = norm_a1.backward(
        per_batch(own.reshape(pixels, mid)) * silu_slope(norm_a1.forward())
    )
    grad_reduce_one = dot_tn(flat_inputs, back_first).astype(bf16)
    grad_images = (
        masked_three.reshape(pixels, wide)
        + dot_nt(back_first, weight_reduce_one)
        + offset_to_images
    ).reshape(images_in.shape)
    last_shards = split_rows(
        scatter_sum(
            jnp.concatenate([chunked(grad_reduce_one), offset_chunks], axis=1), (1, 2, 4, 8, 16)
        ),
        [reduce_one.shape[0], offset_chunks.shape[1]],
    )
    offset_shard = (
        last_shards[1].reshape(-1, 18, mid).transpose(1, 0, 2).reshape(18, -1)[:, :offset_rows].T
    )

    me = lax.axis_index(BOTH)
    mid_grads = jnp.stack(
        [
            norm_a1.gain_grad,
            norm_a2.gain_grad,
            norm_a1.bias_grad,
            norm_a2.bias_grad,
            norm_b1.gain_grad,
            norm_b2.gain_grad,
            norm_b1.bias_grad,
            norm_b2.bias_grad,
        ]
    )
    mid_grads = lax.dynamic_slice_in_dim(mid_grads, me * mid_part, mid_part, 1)
    wide_grads = jnp.stack(
        [norm_a3.gain_grad, norm_a3.bias_grad, norm_b3.gain_grad, norm_b3.bias_grad]
    )
    wide_grads = lax.dynamic_slice_in_dim(wide_grads, me * wide_part, wide_part, 1)
    return (
        block_out,
        grad_images,
        last_shards[0],
        offset_shard,
        one_shards[0],
        unchunked_columns(one_shards[1]),
        mid_grads[0:2],
        mid_grads[2:4],
        wide_grads[0],
        wide_grads[1],
        two_shards[0],
        two_shards[1],
        unchunked_columns(two_shards[2]),
        mid_grads[4:6],
        mid_grads[6:8],
        wide_grads[2],
        wide_grads[3],
    )


def solution(mesh):
    whole = P(BOTH, None)
    part = P(None, BOTH)
    line = P(BOTH)
    maps = P("img", "rows", None, None)
    return jax.shard_map(
        on_device,
        mesh=mesh,
        in_specs=(
            maps,
            maps,
            P("img", None, None),
            P("img", None, None),
            P("img"),
            P("img", "rows", None),
            whole,
            whole,
            whole,
            whole,
            part,
            part,
            line,
            line,
            whole,
            whole,
            whole,
            part,
            part,
            line,
            line,
        ),
        out_specs=(
            maps,
            maps,
            whole,
            whole,
            whole,
            whole,
            part,
            part,
            line,
            line,
            whole,
            whole,
            whole,
            part,
            part,
            line,
            line,
        ),
        check_vma=False,
    )
```

time: 2470 us -> 864 us (0.35)
  blocking collectives: 766 us -> 0 us
  waiting for transfers between devices: 788 us -> 275 us
  local copies, waits for them, and re-layouts: 348 us -> 175 us
  other arithmetic: 192 us -> 60 us
  matrix products: 217 us -> 86.8 us
  starting transfers between devices: 124 us -> 186 us
  Pallas kernels: 0 us -> 54.9 us
    reduce_scatter x5 -> x1, waiting for transfers between devices: 578 us -> 0.01 us  [on_device(): lax.psum_scatter(two_chunks.reshape(-1, mid), BOTH, scatter_dimension=0,...]
    psum x12 -> x0, blocking collectives: 532 us -> none  [the longest x6 285 us: norm_backward(): lax.psum((jnp.sum(upstream, axis=0), jnp.sum(upstream * normed, axis=0)),...]
    all_gather x5 -> x0, blocking collectives: 197 us -> none  [the longest x1 46.7 us: on_device(): lax.all_gather(offset_one, ('rows', 'img'), axis=0, tiled=True)]
    ppermute x40 -> x114, waiting for transfers between devices: 66.8 us -> 226 us  [the longest x94 127 us: exchange(): lax.ppermute(value, BOTH, [(i, i ^ mask) for i in range(device_count())])]
    unnamed x15 -> x4, waiting for transfers between devices: 143 us -> 0.07 us
    dot_general x96 -> x19, matrix products: 217 us -> 86.5 us  [the longest x7 34.7 us: dot_tn(): lax.dot_general(left, right, (((0,), (0,)), ((), ())), preferred_element_...]
    reshape x57 -> x30, local copies, waits for them, and re-layouts: 168 us -> 51.2 us  [the longest x3 9.76 us: chunked_columns(): grad.reshape(count, -1, parts, mid).transpose(0, 2, 1, 3)]
    reduce_sum x6 -> x15, other arithmetic: 76.7 us -> 12.6 us  [the longest x7 10.5 us: batch_totals(): jnp.sum(first, axis=1)]
  transfers between devices with their start and end apart: 53 -> 118, of which waited for: 15 -> 62; matrix products, arithmetic and copies ran while one was open for 19% -> 29% of each run, Pallas kernels for 0% -> 6%
where the time goes in v1:
time: 864 us; the launch traced here: 853 us
  waiting for transfers between devices  275 us (32%)
  starting transfers between devices  186 us (22%)
  local copies, waits for them, and re-layouts  175 us (20%)
  matrix products  86.8 us (10%)
  other arithmetic  60 us (7%)
  Pallas kernels  54.9 us (6%)
  between operations  16.5 us (2%)
    ppermute x94, waiting for transfers between devices, exchange(): lax.ppermute(value, BOTH, [(i, i ^ mask) for i in range(device_count())])  127 us
    ppermute x94, starting transfers between devices, exchange(): lax.ppermute(value, BOTH, [(i, i ^ mask) for i in range(device_count())])  111 us
    ppermute x20, waiting for transfers between devices, from_behind(): lax.ppermute(value, 'rows', [(source, source + steps) for source in range...  99.6 us
    ppermute x20, starting transfers between devices, from_behind(): lax.ppermute(value, 'rows', [(source, source + steps) for source in range...  74.2 us
    all_gather x3, waiting for transfers between devices, gather(): whole = lax.all_gather(jnp.concatenate(pieces, axis=0), BOTH, axis=0)  48.3 us
    unnamed x252, local copies, waits for them, and re-layouts  43.5 us
    dot_general x7, matrix products, dot_tn(): lax.dot_general(left, right, (((0,), (0,)), ((), ())), preferred_element_...  34.7 us
    dot_general x6, matrix products, dot_nt(): lax.dot_general(left, right, (((1,), (1,)), ((), ())), preferred_element_...  31.5 us
  transfers between devices with their start and end apart: 118, of which 62 were waited for; matrix products, arithmetic and copies ran while one was open for 29% of the time, Pallas kernels for 6%

profile of v1, /device:TPU:0, one launch (start us, length us, event | category | flops | bytes accessed | tf_op | source)
XLA Modules:
  0.0 853.3 jit_solution(16444198009078506374)
XLA Ops:
  20.4 3.4 copy.197
  27.4 48.3 %all-gather.12.cloned.1.call-done = bf16[32,101,512]{2,1,0:T(8,128)(2,1)} async-done(((bf16[1,101,512]{2,1,0:T(8,128)(2,1)}), bf16[32,101,512]{2,1,0:T(8,128)(2,1)}) %all-gather.12.cloned.1.call-update) | async-done | bytes 3309584 | tf_op jit(solution)/shard_map/all_gather | solution.py:477
  103.2 5.2 collective-permute-start
  115.3 4.6 collective-permute-start.12
  130.9 30.5 %collective-permute-done.13.refs_5_ = bf16[4,88,512]{2,1,0:T(8,128)(2,1)S(1)} collective-permute-done((bf16[4,88,512]{2,1,0:T(8,128)(2,1)}, bf16[4,88,512]{2,1,0:T(8,128)(2,1)S(1)}, u32[]{:S(2)}, u32[]{:S(2)}) %collective-permute-start.13) | collective-permute-done | bytes 360480 | tf_op jit(solution)/shard_map/ppermute | solution.py:84
  161.4 20.6 %collective-permute-start.14 = (bf16[4,88,512]{2,1,0:T(8,128)(2,1)}, bf16[4,88,512]{2,1,0:T(8,128)(2,1)}, u32[]{:S(2)}, u32[]{:S(2)}) collective-permute-start(bf16[4,88,512]{2,1,0:T(8,128)(2,1)} %get-tuple-element.198), channel_id=1, source_target_pairs={{0,12},{4,16},{8,20},{12,24},{16,28},{1,13},{5,17},{9,21},{13,25},... | collective-permute-start | bytes 1081352 | tf_op jit(solution)/shard_map/ppermute | solution.py:84
  184.3 4.3 collective-permute-done.14.refs_6_
  188.7 16.6 %sample.1 = bf16[4,176,4608]{2,1,0:T(8,128)(2,1)S(1)} custom-call(f32[4,2,1664]{2,1,0:T(2,128)S(1)} %pad.64.pos_ref, f32[24,1]{1,0:T(8,128)S(1)} %copy-done.7, bf16[4,176,512]{2,1,0:T(8,128)(2,1)S(1)} %multiply_convert_fusion.11.refs_0_, bf16[4,176,512]{2,1,0:T(8,128)(2,1)} %collective-permute-done.9.refs_1_, ...), custom_call_target="tpu_custom_call" | custom-call | flops 7197425664 | bytes 10813440 | tf_op jit(solution)/shard_map/sample/pallas_call | solution.py:254
  210.8 3.4 copy-done.5
  214.2 4.6 fusion.106
  222.6 5.4 collective-permute-start.18
  228.1 3.7 collective-permute-start.19
  236.4 3.4 collective-permute-start.21
  246.8 6.7 fusion.99
  262.1 4.4 copy.206
  266.5 6.0 reshape.665
  273.0 4.5 collective-permute-done.28
  277.6 6.5 multiply_convert_fusion.3
  284.1 4.0 fusion.111
  301.0 4.2 collective-permute-done.35
  316.7 3.9 conv.1
  335.8 4.9 copy.254
  340.7 4.5 reshape.692
  346.9 4.1 fusion.98
  365.8 6.2 copy.212
  372.1 5.8 reshape.672
  378.1 8.9 %fusion.97 = (f32[2,2048]{1,0:T(2,128)S(1)}, f32[2,2048]{1,0:T(2,128)S(1)}, f32[2,352,2048]{2,1,0:T(8,128)S(1)}, bf16[2,352,2048]{2,1,0:T(8,128)(2,1)}) fusion(f32[2,2048]{1,0:T(2,128)S(1)} %get-tuple-element.225, f32[2,352,2048]{2,1,0:T(8,128)} %get-tuple-element.266, f32[2,2048]{1,0:T(2,128)S(1)} %get-tuple-element.226, ...), kind=kLoop, calls=%fused_computation.364 | loop fusion | flops 28827648 | bytes 23153408 | tf_op jit(solution)/shard_map/reduce_sum | solution.py:431
  400.0 3.4 collective-permute-done.58
  405.2 4.6 fusion.103
  420.8 4.5 collective-permute-done.65
  426.4 4.1 collective-permute-start.66
  432.1 5.8 collective-permute-done.66.above
  438.4 3.8 conv_back.1
  453.9 4.5 collective-permute-done.74
  460.6 7.9 fusion.96
  476.7 5.0 bitcast_convert_fusion
  481.7 4.5 reshape.654
  488.6 8.9 %convolution_convert_fusion.1 = bf16[4608,512]{1,0:T(8,128)(2,1)} fusion(bf16[704,4608]{1,0:T(8,128)(2,1)} %bitcast.291, bf16[704,512]{1,0:T(8,128)(2,1)S(1)} %bitcast.286), kind=kOutput, calls=%fused_computation.4 | convolution fusion | flops 3324248064 | bytes 11927552 | tf_op jit(solution)/shard_map/dot_general | solution.py:39
  499.5 5.8 fusion.101
  513.1 3.9 pad_maximum_fusion
  520.1 5.2 bitcast_convert_fusion.2
  525.3 3.3 reshape.647
  531.7 8.4 convolution_convert_fusion
  540.1 30.6 %sample_back.1 = (f32[4,176,512]{2,1,0:T(8,128)}, bf16[4,176,512]{2,1,0:T(8,128)(2,1)}, bf16[4,176,512]{2,1,0:T(8,128)(2,1)}, bf16[4,176,512]{2,1,0:T(8,128)(2,1...) custom-call(f32[4,2,1664]{2,1,0:T(2,128)S(1)} %pad.64.pos_ref, ...), custom_call_target="tpu_custom_call" | custom-call | flops 14394851328 | bytes 21626880 | tf_op jit(solution)/shard_map/sample_back/pallas_call | solution.py:280
  574.9 7.2 collective-permute-start.91
  585.9 7.1 convolution_convert_fusion.2
  598.8 8.5 collective-permute-start.103
  607.7 11.2 %collective-permute-done.103 = bf16[18,4,88]{2,1,0:T(4,128)(2,1)S(1)} collective-permute-done((bf16[18,4,88]{2,1,0:T(4,128)(2,1)S(1)}, bf16[18,4,88]{2,1,0:T(4,128)(2,1)S(1)}, u32[]{:S(2)}, u32[]{:S(2)}) %collective-permute-start.103) | collective-permute-done | bytes 12704 | tf_op jit(solution)/shard_map/ppermute | solution.py:84
  621.8 41.6 %collective-permute-done.94 = bf16[4,88,512]{2,1,0:T(8,128)(2,1)S(1)} collective-permute-done((bf16[4,88,512]{2,1,0:T(8,128)(2,1)S(1)}, bf16[4,88,512]{2,1,0:T(8,128)(2,1)S(1)}, u32[]{:S(2)}, u32[]{:S(2)}) %collective-permute-start.94) | collective-permute-done | bytes 360480 | tf_op jit(solution)/shard_map/ppermute | solution.py:84
  663.5 3.7 multiply_multiply_fusion.2
  668.3 12.6 %collective-permute-start.96 = (f32[4,512]{1,0:T(4,128)S(1)}, f32[4,512]{1,0:T(4,128)S(1)}, u32[]{:S(2)}, u32[]{:S(2)}) collective-permute-start(f32[4,512]{1,0:T(4,128)S(1)} %pad_maximum_fusion.15), channel_id=1, source_target_pairs={{0,2},{1,3},{2,0},{3,1},{4,6},{5,7},{6,4},{7,5},{8,10},{9,11},{10,... | collective-permute-start | bytes 24584 | tf_op jit(solution)/shard_map/ppermute | solution.py:47
  684.1 5.3 collective-permute-start.98
  705.5 3.7 concatenate.116
  709.2 3.1 copy.217
  715.5 3.1 fusion.6
  724.2 3.8 collective-permute-done.104
  739.2 4.5 reshape.633
  743.7 5.9 copy.229
  757.0 29.1 %collective-permute-done.106 = bf16[2,2,100,512]{3,2,1,0:T(8,128)(2,1)S(1)} collective-permute-done((bf16[2,2,100,512]{3,2,1,0:T(8,128)(2,1)S(1)}, bf16[2,2,100,512]{3,2,1,0:T(8,128)(2,1)S(1)}, u32[]{:S(2)}, u32[]{:S(2)}) %collective-permute-start.106) | collective-permute-done | bytes 409632 | tf_op jit(solution)/shard_map/ppermute | solution.py:47
  793.1 3.5 fusion.1
  800.7 11.3 %collective-permute-done.111 = bf16[2,2,208,512]{3,2,0,1:T(8,128)(2,1)} collective-permute-done((bf16[2,2,208,512]{3,2,0,1:T(8,128)(2,1)S(1)}, bf16[2,2,208,512]{3,2,0,1:T(8,128)(2,1)}, u32[]{:S(2)}, u32[]{:S(2)}) %collective-permute-start.111) | collective-permute-done | bytes 852000 | tf_op jit(solution)/shard_map/ppermute | solution.py:47
  814.4 5.8 reshape.640
  820.2 9.0 %copy.230 = f32[4,4,44,2048]{3,1,2,0:T(4,128)} copy(f32[4,4,44,2048]{3,2,1,0:T(8,128)} %reshape.640) | data formatting | bytes 11534336
  833.9 7.1 collective-permute-done.113
  (711 shorter events, 306.6 us)
Async XLA Ops:
  7.2 68.6 %all-gather.12.cloned.1.call-start = ((), (), s32[]{:S(2)}) async-start(), calls=%async_computation.4 | async-start | bytes 3514368 | tf_op jit(solution)/shard_map/all_gather | solution.py:477
  13.2 194.8 %all-gather.8.cloned.1.call-start = ((), (), s32[]{:S(2)}) async-start(), calls=%async_computation.2 | async-start | bytes 7028736 | tf_op jit(solution)/shard_map/all_gather | solution.py:477
  17.7 266.4 %all-gather.10.cloned.1.call-start = ((), (), s32[]{:S(2)}) async-start(), calls=%async_computation.3 | async-start | bytes 9191424 | tf_op jit(solution)/shard_map/all_gather | solution.py:477
  20.4 822.3 %reduce-scatter.2.cloned.1.call-start = ((), (), s32[]{:S(2)}) async-start(), calls=%async_computation.1 | async-start | bytes 9191424 | tf_op jit(solution)/shard_map/reduce_scatter | solution.py:690
  80.1 12.0 %collective-permute-start.2 = (f32[4,512]{1,0:T(4,128)S(1)}, f32[4,512]{1,0:T(4,128)S(1)}, u32[]{:S(2)}, u32[]{:S(2)}) collective-permute-start(f32[4,512]{1,0:T(4,128)S(1)} %pad_maximum_fusion.8), channel_id=1, source_target_pairs={{0,1},{1,0},{2,3},{3,2},{4,5},{5,4},{6,7},{7,6},{8,9},{9,8},{10,11... | collective-permute-start | bytes 24584 | tf_op jit(solution)/shard_map/ppermute | solution.py:47
  80.4 11.7 %collective-permute-start.3 = (f32[4,512]{1,0:T(4,128)S(1)}, f32[4,512]{1,0:T(4,128)S(1)}, u32[]{:S(2)}, u32[]{:S(2)}) collective-permute-start(f32[4,512]{1,0:T(4,128)S(1)} %pad_maximum_fusion.8), channel_id=1, source_target_pairs={{0,2},{1,3},{2,0},{3,1},{4,6},{5,7},{6,4},{7,5},{8,10},{9,11},{10,... | collective-permute-start | bytes 24584 | tf_op jit(solution)/shard_map/ppermute | solution.py:47
  81.7 10.5 %collective-permute-start.4 = (f32[4,512]{1,0:T(4,128)S(1)}, f32[4,512]{1,0:T(4,128)S(1)}, u32[]{:S(2)}, u32[]{:S(2)}) collective-permute-start(f32[4,512]{1,0:T(4,128)S(1)} %pad_maximum_fusion.8), channel_id=1, source_target_pairs={{0,3},{1,2},{2,1},{3,0},{4,7},{5,6},{6,5},{7,4},{8,11},{9,10},{10,... | collective-permute-start | bytes 24584 | tf_op jit(solution)/shard_map/ppermute | solution.py:47
  92.2 5.6 collective-permute-start.5
  99.1 9.3 %collective-permute-start.8 = (f32[4,512]{1,0:T(4,128)S(1)}, f32[4,512]{1,0:T(4,128)S(1)}, u32[]{:S(2)}, u32[]{:S(2)}) collective-permute-start(f32[4,512]{1,0:T(4,128)S(1)} %add_add_fusion.23), channel_id=1, source_target_pairs={{0,16},{1,17},{2,18},{3,19},{4,20},{5,21},{6,22},{7,23},{8,24},{9,... | collective-permute-start | bytes 24584 | tf_op jit(solution)/shard_map/ppermute | solution.py:47
  101.9 18.0 %collective-permute-start.1 = (f32[54,4,88]{2,1,0:T(4,128)}, f32[54,4,88]{2,1,0:T(4,128)}, u32[]{:S(2)}, u32[]{:S(2)}) collective-permute-start(f32[54,4,88]{2,1,0:T(4,128)} %get-tuple-element.201), channel_id=1, source_target_pairs={{4,0},{8,4},{12,8},{16,12},{20,16},{24,20},{28,24},{5,1},{9,5},{13... | collective-permute-start | bytes 228104 | tf_op jit(solution)/shard_map/ppermute | solution.py:84
  103.2 18.0 %collective-permute-start = (f32[54,4,88]{2,1,0:T(4,128)}, f32[54,4,88]{2,1,0:T(4,128)}, u32[]{:S(2)}, u32[]{:S(2)}) collective-permute-start(f32[54,4,88]{2,1,0:T(4,128)} %get-tuple-element.200), channel_id=1, source_target_pairs={{0,4},{4,8},{8,12},{12,16},{16,20},{20,24},{24,28},{1,5},{5,9},{9,... | collective-permute-start | bytes 228104 | tf_op jit(solution)/shard_map/ppermute | solution.py:84
  111.2 77.4 %collective-permute-start.10 = (bf16[4,176,512]{2,1,0:T(8,128)(2,1)S(1)}, bf16[4,176,512]{2,1,0:T(8,128)(2,1)S(1)}, u32[]{:S(2)}, u32[]{:S(2)}) collective-permute-start(bf16[4,176,512]{2,1,0:T(8,128)(2,1)S(1)} %multiply_convert_fusion.11.refs_0_), channel_id=1, source_target_pairs={{0,4},{4,8},{8,12},{12,16},{16,20},{20,24},{24,28},{1,5},{5,9},{9,... | collective-permute-start | bytes 2162696 | tf_op jit(solution)/shard_map/ppermute | solution.py:84
  114.0 74.6 %collective-permute-start.11 = (bf16[4,176,512]{2,1,0:T(8,128)(2,1)S(1)}, bf16[4,176,512]{2,1,0:T(8,128)(2,1)S(1)}, u32[]{:S(2)}, u32[]{:S(2)}) collective-permute-start(bf16[4,176,512]{2,1,0:T(8,128)(2,1)S(1)} %multiply_convert_fusion.11.refs_0_), channel_id=1, source_target_pairs={{8,0},{12,4},{16,8},{20,12},{24,16},{28,20},{9,1},{13,5},{17,9},{2... | collective-permute-start | bytes 2162696 | tf_op jit(solution)/shard_map/ppermute | solution.py:84
  115.3 73.3 %collective-permute-start.12 = (bf16[4,176,512]{2,1,0:T(8,128)(2,1)S(1)}, bf16[4,176,512]{2,1,0:T(8,128)(2,1)S(1)}, u32[]{:S(2)}, u32[]{:S(2)}) collective-permute-start(bf16[4,176,512]{2,1,0:T(8,128)(2,1)S(1)} %multiply_convert_fusion.11.refs_0_), channel_id=1, source_target_pairs={{0,8},{4,12},{8,16},{12,20},{16,24},{20,28},{1,9},{5,13},{9,17},{1... | collective-permute-start | bytes 2162696 | tf_op jit(solution)/shard_map/ppermute | solution.py:84
  119.9 68.7 %collective-permute-start.9 = (bf16[4,176,512]{2,1,0:T(8,128)(2,1)S(1)}, bf16[4,176,512]{2,1,0:T(8,128)(2,1)}, u32[]{:S(2)}, u32[]{:S(2)}) collective-permute-start(bf16[4,176,512]{2,1,0:T(8,128)(2,1)S(1)} %multiply_convert_fusion.11.refs_0_), channel_id=1, source_target_pairs={{4,0},{8,4},{12,8},{16,12},{20,16},{24,20},{28,24},{5,1},{9,5},{13... | collective-permute-start | bytes 2162696 | tf_op jit(solution)/shard_map/ppermute | solution.py:84
  121.2 40.2 %collective-permute-start.13 = (bf16[4,88,512]{2,1,0:T(8,128)(2,1)}, bf16[4,88,512]{2,1,0:T(8,128)(2,1)S(1)}, u32[]{:S(2)}, u32[]{:S(2)}) collective-permute-start(bf16[4,88,512]{2,1,0:T(8,128)(2,1)} %get-tuple-element.199), channel_id=1, source_target_pairs={{12,0},{16,4},{20,8},{24,12},{28,16},{13,1},{17,5},{21,9},{25,13},... | collective-permute-start | bytes 1081352 | tf_op jit(solution)/shard_map/ppermute | solution.py:84
  161.4 27.2 %collective-permute-start.14 = (bf16[4,88,512]{2,1,0:T(8,128)(2,1)}, bf16[4,88,512]{2,1,0:T(8,128)(2,1)}, u32[]{:S(2)}, u32[]{:S(2)}) collective-permute-start(bf16[4,88,512]{2,1,0:T(8,128)(2,1)} %get-tuple-element.198), channel_id=1, source_target_pairs={{0,12},{4,16},{8,20},{12,24},{16,28},{1,13},{5,17},{9,21},{13,25},... | collective-permute-start | bytes 1081352 | tf_op jit(solution)/shard_map/ppermute | solution.py:84
  222.6 9.1 %collective-permute-start.18 = (f32[4,512]{1,0:T(4,128)S(1)}, f32[4,512]{1,0:T(4,128)S(1)}, u32[]{:S(2)}, u32[]{:S(2)}) collective-permute-start(f32[4,512]{1,0:T(4,128)S(1)} %add_add_fusion.22), channel_id=1, source_target_pairs={{0,4},{1,5},{2,6},{3,7},{4,0},{5,1},{6,2},{7,3},{8,12},{9,13},{10,... | collective-permute-start | bytes 24584 | tf_op jit(solution)/shard_map/ppermute | solution.py:47
  228.1 5.3 collective-permute-start.19
  231.8 4.7 collective-permute-start.20
  236.4 10.3 %collective-permute-start.21 = (f32[4,512]{1,0:T(4,128)S(1)}, f32[4,512]{1,0:T(4,128)S(1)}, u32[]{:S(2)}, u32[]{:S(2)}) collective-permute-start(f32[4,512]{1,0:T(4,128)S(1)} %add_add_fusion.21), channel_id=1, source_target_pairs={{0,16},{1,17},{2,18},{3,19},{4,20},{5,21},{6,22},{7,23},{8,24},{9,... | collective-permute-start | bytes 24584 | tf_op jit(solution)/shard_map/ppermute | solution.py:47
  258.6 14.0 %collective-permute-start.25 = (f32[4,2048]{1,0:T(4,128)S(1)}, f32[4,2048]{1,0:T(4,128)S(1)}, u32[]{:S(2)}, u32[]{:S(2)}) collective-permute-start(f32[4,2048]{1,0:T(4,128)S(1)} %add_add_fusion.8), channel_id=1, source_target_pairs={{0,4},{1,5},{2,6},{3,7},{4,0},{5,1},{6,2},{7,3},{8,12},{9,13},{10,... | collective-permute-start | bytes 98312 | tf_op jit(solution)/shard_map/ppermute | solution.py:47
  260.6 12.0 %collective-permute-start.26 = (f32[4,2048]{1,0:T(4,128)S(1)}, f32[4,2048]{1,0:T(4,128)S(1)}, u32[]{:S(2)}, u32[]{:S(2)}) collective-permute-start(f32[4,2048]{1,0:T(4,128)S(1)} %add_add_fusion.8), channel_id=1, source_target_pairs={{0,8},{1,9},{2,10},{3,11},{4,12},{5,13},{6,14},{7,15},{8,0},{9,1},... | collective-permute-start | bytes 98312 | tf_op jit(solution)/shard_map/ppermute | solution.py:47
  260.6 11.9 %collective-permute-start.27 = (f32[4,2048]{1,0:T(4,128)S(1)}, f32[4,2048]{1,0:T(4,128)S(1)}, u32[]{:S(2)}, u32[]{:S(2)}) collective-permute-start(f32[4,2048]{1,0:T(4,128)S(1)} %add_add_fusion.8), channel_id=1, source_target_pairs={{0,12},{1,13},{2,14},{3,15},{4,8},{5,9},{6,10},{7,11},{8,4},{9,5},... | collective-permute-start | bytes 98312 | tf_op jit(solution)/shard_map/ppermute | solution.py:47
  272.6 4.9 collective-permute-start.28
  305.7 8.4 collective-permute-start.36
  308.8 7.9 collective-permute-start.37
  335.5 9.7 %collective-permute-start.44 = (f32[4,512]{1,0:T(4,128)S(1)}, f32[4,512]{1,0:T(4,128)S(1)}, u32[]{:S(2)}, u32[]{:S(2)}) collective-permute-start(f32[4,512]{1,0:T(4,128)S(1)} %add_add_fusion.17), channel_id=1, source_target_pairs={{0,16},{1,17},{2,18},{3,19},{4,20},{5,21},{6,22},{7,23},{8,24},{9,... | collective-permute-start | bytes 24584 | tf_op jit(solution)/shard_map/ppermute | solution.py:47
  357.7 4.8 collective-permute-start.50
  362.6 15.5 %collective-permute-start.51 = (f32[4,2048]{1,0:T(4,128)S(1)}, f32[4,2048]{1,0:T(4,128)S(1)}, u32[]{:S(2)}, u32[]{:S(2)}) collective-permute-start(f32[4,2048]{1,0:T(4,128)S(1)} %add_add_fusion.5), channel_id=1, source_target_pairs={{0,16},{1,17},{2,18},{3,19},{4,20},{5,21},{6,22},{7,23},{8,24},{9,... | collective-permute-start | bytes 98312 | tf_op jit(solution)/shard_map/ppermute | solution.py:47
  393.7 4.8 collective-permute-start.57
  398.5 4.9 collective-permute-start.58
  426.4 11.5 %collective-permute-start.66 = (bf16[4,44,512]{2,1,0:T(8,128)(2,1)S(1)}, bf16[4,44,512]{2,1,0:T(8,128)(2,1)S(1)}, u32[]{:S(2)}, u32[]{:S(2)}) collective-permute-start(bf16[4,44,512]{2,1,0:T(8,128)(2,1)S(1)} %get-tuple-element.195), channel_id=1, source_target_pairs={{0,4},{4,8},{8,12},{12,16},{16,20},{20,24},{24,28},{1,5},{5,9},{9,... | collective-permute-start | bytes 540680 | tf_op jit(solution)/shard_map/ppermute | solution.py:84
  430.5 7.8 collective-permute-start.67
  473.1 15.3 %collective-permute-start.78 = (f32[4,2048]{1,0:T(4,128)S(1)}, f32[4,2048]{1,0:T(4,128)S(1)}, u32[]{:S(2)}, u32[]{:S(2)}) collective-permute-start(f32[4,2048]{1,0:T(4,128)S(1)} %add_add_fusion.2), channel_id=1, source_target_pairs={{0,4},{1,5},{2,6},{3,7},{4,0},{5,1},{6,2},{7,3},{8,12},{9,13},{10,... | collective-permute-start | bytes 98312 | tf_op jit(solution)/shard_map/ppermute | solution.py:47
  473.9 14.6 %collective-permute-start.79 = (f32[4,2048]{1,0:T(4,128)S(1)}, f32[4,2048]{1,0:T(4,128)S(1)}, u32[]{:S(2)}, u32[]{:S(2)}) collective-permute-start(f32[4,2048]{1,0:T(4,128)S(1)} %add_add_fusion.2), channel_id=1, source_target_pairs={{0,8},{1,9},{2,10},{3,11},{4,12},{5,13},{6,14},{7,15},{8,0},{9,1},... | collective-permute-start | bytes 98312 | tf_op jit(solution)/shard_map/ppermute | solution.py:47
  475.3 13.2 %collective-permute-start.80 = (f32[4,2048]{1,0:T(4,128)S(1)}, f32[4,2048]{1,0:T(4,128)S(1)}, u32[]{:S(2)}, u32[]{:S(2)}) collective-permute-start(f32[4,2048]{1,0:T(4,128)S(1)} %add_add_fusion.2), channel_id=1, source_target_pairs={{0,12},{1,13},{2,14},{3,15},{4,8},{5,9},{6,10},{7,11},{8,4},{9,5},... | collective-permute-start | bytes 98312 | tf_op jit(solution)/shard_map/ppermute | solution.py:47
  488.5 9.1 %collective-permute-start.81 = (f32[4,2048]{1,0:T(4,128)S(1)}, f32[4,2048]{1,0:T(4,128)S(1)}, u32[]{:S(2)}, u32[]{:S(2)}) collective-permute-start(f32[4,2048]{1,0:T(4,128)S(1)} %add_add_fusion.1), channel_id=1, source_target_pairs={{0,16},{1,17},{2,18},{3,19},{4,20},{5,21},{6,22},{7,23},{8,24},{9,... | collective-permute-start | bytes 98312 | tf_op jit(solution)/shard_map/ppermute | solution.py:47
  509.6 7.5 collective-permute-start.85
  510.6 6.5 collective-permute-start.86
  512.2 4.9 collective-permute-start.87
  517.1 13.5 %collective-permute-start.88 = (f32[4,512]{1,0:T(4,128)S(1)}, f32[4,512]{1,0:T(4,128)S(1)}, u32[]{:S(2)}, u32[]{:S(2)}) collective-permute-start(f32[4,512]{1,0:T(4,128)S(1)} %add_add_fusion.11), channel_id=1, source_target_pairs={{0,16},{1,17},{2,18},{3,19},{4,20},{5,21},{6,22},{7,23},{8,24},{9,... | collective-permute-start | bytes 24584 | tf_op jit(solution)/shard_map/ppermute | solution.py:47
  570.7 92.8 %collective-permute-start.89 = (bf16[4,176,512]{2,1,0:T(8,128)(2,1)}, bf16[4,176,512]{2,1,0:T(8,128)(2,1)S(1)}, u32[]{:S(2)}, u32[]{:S(2)}) collective-permute-start(bf16[4,176,512]{2,1,0:T(8,128)(2,1)} %get-tuple-element.29), channel_id=1, source_target_pairs={{0,4},{4,8},{8,12},{12,16},{16,20},{20,24},{24,28},{1,5},{5,9},{9,... | collective-permute-start | bytes 2162696 | tf_op jit(solution)/shard_map/ppermute | solution.py:84
  573.6 89.8 %collective-permute-start.90 = (bf16[4,176,512]{2,1,0:T(8,128)(2,1)}, bf16[4,176,512]{2,1,0:T(8,128)(2,1)}, u32[]{:S(2)}, u32[]{:S(2)}) collective-permute-start(bf16[4,176,512]{2,1,0:T(8,128)(2,1)} %get-tuple-element.30), channel_id=1, source_target_pairs={{4,0},{8,4},{12,8},{16,12},{20,16},{24,20},{28,24},{5,1},{9,5},{13... | collective-permute-start | bytes 2162696 | tf_op jit(solution)/shard_map/ppermute | solution.py:84
  574.9 88.5 %collective-permute-start.91 = (bf16[4,176,512]{2,1,0:T(8,128)(2,1)S(1)}, bf16[4,176,512]{2,1,0:T(8,128)(2,1)}, u32[]{:S(2)}, u32[]{:S(2)}) collective-permute-start(bf16[4,176,512]{2,1,0:T(8,128)(2,1)S(1)} %get-tuple-element.31), channel_id=1, source_target_pairs={{0,8},{4,12},{8,16},{12,20},{16,24},{20,28},{1,9},{5,13},{9,17},{1... | collective-permute-start | bytes 2162696 | tf_op jit(solution)/shard_map/ppermute | solution.py:84
  582.1 38.1 %collective-permute-start.93 = (bf16[4,88,512]{2,1,0:T(8,128)(2,1)}, bf16[4,88,512]{2,1,0:T(8,128)(2,1)}, u32[]{:S(2)}, u32[]{:S(2)}) collective-permute-start(bf16[4,88,512]{2,1,0:T(8,128)(2,1)} %get-tuple-element.33), channel_id=1, source_target_pairs={{0,12},{4,16},{8,20},{12,24},{16,28},{1,13},{5,17},{9,21},{13,25},... | collective-permute-start | bytes 1081352 | tf_op jit(solution)/shard_map/ppermute | solution.py:84
  584.5 14.3 %collective-permute-start.102 = (bf16[18,4,88]{2,1,0:T(4,128)(2,1)S(1)}, bf16[18,4,88]{2,1,0:T(4,128)(2,1)S(1)}, u32[]{:S(2)}, u32[]{:S(2)}) collective-permute-start(bf16[18,4,88]{2,1,0:T(4,128)(2,1)S(1)} %get-tuple-element.215), channel_id=1, source_target_pairs={{4,0},{8,4},{12,8},{16,12},{20,16},{24,20},{28,24},{5,1},{9,5},{13... | collective-permute-start | bytes 38024 | tf_op jit(solution)/shard_map/ppermute | solution.py:84
  598.8 20.1 %collective-permute-start.103 = (bf16[18,4,88]{2,1,0:T(4,128)(2,1)S(1)}, bf16[18,4,88]{2,1,0:T(4,128)(2,1)S(1)}, u32[]{:S(2)}, u32[]{:S(2)}) collective-permute-start(bf16[18,4,88]{2,1,0:T(4,128)(2,1)S(1)} %get-tuple-element.216), channel_id=1, source_target_pairs={{0,4},{4,8},{8,12},{12,16},{16,20},{20,24},{24,28},{1,5},{5,9},{9,... | collective-permute-start | bytes 38024 | tf_op jit(solution)/shard_map/ppermute | solution.py:84
  618.9 44.6 %collective-permute-start.92 = (bf16[4,176,512]{2,1,0:T(8,128)(2,1)S(1)}, bf16[4,176,512]{2,1,0:T(8,128)(2,1)S(1)}, u32[]{:S(2)}, u32[]{:S(2)}) collective-permute-start(bf16[4,176,512]{2,1,0:T(8,128)(2,1)S(1)} %get-tuple-element.32), channel_id=1, source_target_pairs={{8,0},{12,4},{16,8},{20,12},{24,16},{28,20},{9,1},{13,5},{17,9},{2... | collective-permute-start | bytes 2162696 | tf_op jit(solution)/shard_map/ppermute | solution.py:84
  620.3 43.2 %collective-permute-start.94 = (bf16[4,88,512]{2,1,0:T(8,128)(2,1)S(1)}, bf16[4,88,512]{2,1,0:T(8,128)(2,1)S(1)}, u32[]{:S(2)}, u32[]{:S(2)}) collective-permute-start(bf16[4,88,512]{2,1,0:T(8,128)(2,1)S(1)} %get-tuple-element.34), channel_id=1, source_target_pairs={{12,0},{16,4},{20,8},{24,12},{28,16},{13,1},{17,5},{21,9},{25,13},... | collective-permute-start | bytes 1081352 | tf_op jit(solution)/shard_map/ppermute | solution.py:84
  663.4 69.9 %collective-permute-start.109 = (bf16[2,2,2,2,208,512]{5,4,0,1,3,2:T(8,128)(2,1)}, bf16[2,2,2,2,208,512]{5,4,0,1,3,2:T(8,128)(2,1)}, u32[]{:S(2)}, u32[]{:S(2)}) collective-permute-start(bf16[2,2,2,2,208,512]{5,4,0,1,3,2:T(8,128)(2,1)} %bitcast.264), channel_id=1, source_target_pairs={{0,1},{1,0},{2,3},{3,2},{4,5},{5,4},{6,7},{7,6},{8,9},{9,8},{10,11... | collective-permute-start | bytes 10223624 | tf_op jit(solution)/shard_map/ppermute | solution.py:47
  667.8 13.3 %collective-permute-start.95 = (f32[4,512]{1,0:T(4,128)S(1)}, f32[4,512]{1,0:T(4,128)S(1)}, u32[]{:S(2)}, u32[]{:S(2)}) collective-permute-start(f32[4,512]{1,0:T(4,128)S(1)} %pad_maximum_fusion.15), channel_id=1, source_target_pairs={{0,1},{1,0},{2,3},{3,2},{4,5},{5,4},{6,7},{7,6},{8,9},{9,8},{10,11... | collective-permute-start | bytes 24584 | tf_op jit(solution)/shard_map/ppermute | solution.py:47
  668.3 14.2 %collective-permute-start.96 = (f32[4,512]{1,0:T(4,128)S(1)}, f32[4,512]{1,0:T(4,128)S(1)}, u32[]{:S(2)}, u32[]{:S(2)}) collective-permute-start(f32[4,512]{1,0:T(4,128)S(1)} %pad_maximum_fusion.15), channel_id=1, source_target_pairs={{0,2},{1,3},{2,0},{3,1},{4,6},{5,7},{6,4},{7,5},{8,10},{9,11},{10,... | collective-permute-start | bytes 24584 | tf_op jit(solution)/shard_map/ppermute | solution.py:47
  684.1 7.2 collective-permute-start.100
  684.1 7.1 collective-permute-start.98
  693.1 19.2 %collective-permute-start.101 = (f32[4,512]{1,0:T(4,128)S(1)}, f32[4,512]{1,0:T(4,128)S(1)}, u32[]{:S(2)}, u32[]{:S(2)}) collective-permute-start(f32[4,512]{1,0:T(4,128)S(1)} %add_add_fusion.9), channel_id=1, source_target_pairs={{0,16},{1,17},{2,18},{3,19},{4,20},{5,21},{6,22},{7,23},{8,24},{9,... | collective-permute-start | bytes 24584 | tf_op jit(solution)/shard_map/ppermute | solution.py:47
  731.8 20.6 %collective-permute-start.105 = (bf16[2,2,2,100,512]{4,2,3,1,0:T(2,128)(2,1)}, bf16[2,2,2,100,512]{4,2,3,1,0:T(2,128)(2,1)}, u32[]{:S(2)}, u32[]{:S(2)}) collective-permute-start(bf16[2,2,2,100,512]{4,2,3,1,0:T(2,128)(2,1)} %copy.220), channel_id=1, source_target_pairs={{0,2},{1,3},{2,0},{3,1},{4,6},{5,7},{6,4},{7,5},{8,10},{9,11},{10,... | collective-permute-start | bytes 2457608 | tf_op jit(solution)/shard_map/ppermute | solution.py:47
  737.8 50.9 %collective-permute-start.110 = (bf16[2,2,2,208,512]{4,3,0,1,2:T(8,128)(2,1)}, bf16[2,2,2,208,512]{4,3,0,1,2:T(8,128)(2,1)}, u32[]{:S(2)}, u32[]{:S(2)}) collective-permute-start(bf16[2,2,2,208,512]{4,3,0,1,2:T(8,128)(2,1)} %dynamic-slice_bitcast_fusion), channel_id=1, source_target_pairs={{0,4},{1,5},{2,6},{3,7},{4,0},{5,1},{6,2},{7,3},{8,12},{9,13},{10,... | collective-permute-start | bytes 5111816 | tf_op jit(solution)/shard_map/ppermute | solution.py:47
  753.9 32.2 %collective-permute-start.106 = (bf16[2,2,100,512]{3,2,1,0:T(8,128)(2,1)S(1)}, bf16[2,2,100,512]{3,2,1,0:T(8,128)(2,1)S(1)}, u32[]{:S(2)}, u32[]{:S(2)}) collective-permute-start(bf16[2,2,100,512]{3,2,1,0:T(8,128)(2,1)S(1)} %dynamic-slice_bitcast_fusion.4), channel_id=1, source_target_pairs={{0,4},{1,5},{2,6},{3,7},{4,0},{5,1},{6,2},{7,3},{8,12},{9,13},{10,... | collective-permute-start | bytes 1228808 | tf_op jit(solution)/shard_map/ppermute | solution.py:47
  787.0 9.7 %collective-permute-start.107 = (bf16[2,100,512]{2,1,0:T(8,128)(2,1)}, bf16[2,100,512]{2,1,0:T(8,128)(2,1)}, u32[]{:S(2)}, u32[]{:S(2)}) collective-permute-start(bf16[2,100,512]{2,1,0:T(8,128)(2,1)} %dynamic-slice_bitcast_fusion.6), channel_id=1, source_target_pairs={{0,8},{1,9},{2,10},{3,11},{4,12},{5,13},{6,14},{7,15},{8,0},{9,1},... | collective-permute-start | bytes 614408 | tf_op jit(solution)/shard_map/ppermute | solution.py:47
  792.1 20.0 %collective-permute-start.111 = (bf16[2,2,208,512]{3,2,0,1:T(8,128)(2,1)S(1)}, bf16[2,2,208,512]{3,2,0,1:T(8,128)(2,1)}, u32[]{:S(2)}, u32[]{:S(2)}) collective-permute-start(bf16[2,2,208,512]{3,2,0,1:T(8,128)(2,1)S(1)} %dynamic-slice_bitcast_fusion.1), channel_id=1, source_target_pairs={{0,2},{1,3},{2,0},{3,1},{4,6},{5,7},{6,4},{7,5},{8,10},{9,11},{10,... | collective-permute-start | bytes 2555912 | tf_op jit(solution)/shard_map/ppermute | solution.py:47
  797.8 31.5 %collective-permute-start.108 = (bf16[100,512]{1,0:T(8,128)(2,1)S(1)}, bf16[100,512]{1,0:T(8,128)(2,1)S(1)}, u32[]{:S(2)}, u32[]{:S(2)}) collective-permute-start(bf16[100,512]{1,0:T(8,128)(2,1)S(1)} %dynamic-slice_bitcast_fusion.7), channel_id=1, source_target_pairs={{0,16},{1,17},{2,18},{3,19},{4,20},{5,21},{6,22},{7,23},{8,24},{9,... | collective-permute-start | bytes 307208 | tf_op jit(solution)/shard_map/ppermute | solution.py:47
  813.5 16.6 %collective-permute-start.112 = (bf16[2,208,512]{2,1,0:T(8,128)(2,1)S(1)}, bf16[2,208,512]{2,1,0:T(8,128)(2,1)S(1)}, u32[]{:S(2)}, u32[]{:S(2)}) collective-permute-start(bf16[2,208,512]{2,1,0:T(8,128)(2,1)S(1)} %dynamic-slice_bitcast_fusion.3), channel_id=1, source_target_pairs={{0,8},{1,9},{2,10},{3,11},{4,12},{5,13},{6,14},{7,15},{8,0},{9,1},... | collective-permute-start | bytes 1277960 | tf_op jit(solution)/shard_map/ppermute | solution.py:47
  830.3 10.8 %collective-permute-start.113 = (bf16[208,512]{1,0:T(8,128)(2,1)S(1)}, bf16[208,512]{1,0:T(8,128)(2,1)S(1)}, u32[]{:S(2)}, u32[]{:S(2)}) collective-permute-start(bf16[208,512]{1,0:T(8,128)(2,1)S(1)} %dynamic-slice_bitcast_fusion.5), channel_id=1, source_target_pairs={{0,16},{1,17},{2,18},{3,19},{4,20},{5,21},{6,22},{7,23},{8,24},{9,... | collective-permute-start | bytes 638984 | tf_op jit(solution)/shard_map/ppermute | solution.py:47
  (171 other events, 2154.4 us)
Sparse Core Ops, SparseCore 0:
  13.3 62.3 all-gather.11
  79.2 105.4 all-gather.7
  188.1 75.6 all-gather.9
  517.2 157.9 reduce-scatter.1

commit v2 on v1

--- a/solution.py
+++ b/solution.py
@@ -25,6 +25,9 @@
 LANES = 1664
 CELLS = (STRIP_ROWS + 2 * HALO) * COLS
 ROW_ORDER = (10, 11, 12, 13, 14, 15, 16, 17, 6, 7, 8, 9, 18, 19, 20, 21, 2, 3, 4, 5, 22, 23, 0, 1)
+
+
+SMALL = pl.CostEstimate(flops=1, bytes_accessed=1, transcendentals=0)
 
 
 def dot(left, right):
@@ -59,23 +62,83 @@
     return value
 
 
-def scatter_sum(chunks, order):
-    count = device_count()
-    me = lax.axis_index(BOTH)
-    bits = [1 << k for k in range(count.bit_length() - 1)][::-1]
-    value = chunks.reshape((2,) * len(bits) + chunks.shape[1:])
-    order = [b for b in order if b in bits] + [b for b in bits[::-1] if b not in order]
-    left = list(bits)
-    for position, bit in enumerate(order):
-        axis = left.index(bit)
-        mine = (me // bit) % 2
-        keep = lax.dynamic_index_in_dim(value, mine, axis, keepdims=False)
-        send = lax.dynamic_index_in_dim(value, 1 - mine, axis, keepdims=False)
-        value = keep.astype(f32) + exchange(send, bit).astype(f32)
-        if position < len(order) - 1:
-            value = value.astype(bf16)
-        left.pop(axis)
-    return value
+def bits_of(order):
+    bits = [1 << k for k in range(device_count().bit_length() - 1)]
+    return [b for b in order if b in bits] + [b for b in bits if b not in order]
+
+
+def tie(value, *others):
+    return lax.optimization_barrier((value,) + others)[0]
+
+
+def meet(*values):
+    return lax.optimization_barrier(values)
+
+
+class Scatter:
+    def __init__(self, pieces, order):
+        self.order = bits_of(order)
+        bits = sorted(self.order, reverse=True)
+        count = len(bits)
+        axes = [bits.index(b) for b in self.order] + [count, count + 1]
+        self.value = jnp.concatenate(
+            [piece.reshape((2,) * count + piece.shape[1:]).transpose(axes) for piece in pieces],
+            axis=-2,
+        )
+
+    def step(self):
+        bit = self.order.pop(0)
+        mine = (lax.axis_index(BOTH) // bit) % 2
+        keep = lax.dynamic_index_in_dim(self.value, mine, 0, keepdims=False)
+        send = lax.dynamic_index_in_dim(self.value, 1 - mine, 0, keepdims=False)
+        total = keep.astype(f32) + exchange(send, bit).astype(f32)
+        self.value = total.astype(bf16) if self.order else total
+        return self.value
+
+    def finish(self):
+        while self.order:
+            self.step()
+        return self.value
+
+
+class Gather:
+    def __init__(self, piece, groups):
+        bits = bits_of(())
+        self.groups = [tuple(b for b in group if b in bits) for group in groups]
+        self.groups += [(b,) for b in bits if not any(b in group for group in self.groups)]
+        self.done = []
+        self.piece = piece
+        self.value = piece
+
+    def step(self):
+        group = self.groups.pop(0)
+        by_mask = {0: self.value}
+        for bit in group:
+            for mask in sub_masks(group, bit):
+                by_mask[bit + mask] = exchange(self.value, bit + mask)
+        for bit in group:
+            mine = (lax.axis_index(BOTH) // bit) % 2 == 1
+            self.done = sorted(self.done + [bit], reverse=True)
+            axis = self.done.index(bit)
+            merged = {}
+            for mask, part in by_mask.items():
+                if not mask & bit:
+                    other = by_mask[mask + bit]
+                    merged[mask] = jnp.stack(
+                        [jnp.where(mine, other, part), jnp.where(mine, part, other)], axis=axis
+                    )
+            by_mask = merged
+        (self.value,) = by_mask.values()
+
+    def result(self):
+        return self.value.reshape((-1,) + self.piece.shape)
+
+
+def sub_masks(group, bit):
+    masks = [0]
+    for other in group[: group.index(bit)]:
+        masks = masks + [mask + other for mask in masks]
+    return masks
 
 
 def from_behind(value, steps):
@@ -232,17 +295,17 @@
     lax.fori_loop(0, LANES // 128, body, 0)
 
 
-def piece_specs(width):
-    full = pl.BlockSpec((1, STRIP, width), lambda i: (i, 0, 0))
-    half = pl.BlockSpec((1, STRIP // 2, width), lambda i: (i, 0, 0))
+def piece_specs(width, first=0):
+    full = pl.BlockSpec((1, STRIP, width), lambda i: (i + first, 0, 0))
+    half = pl.BlockSpec((1, STRIP // 2, width), lambda i: (i + first, 0, 0))
     return [full] * 5 + [half] * 2
 
 
-def sampler_specs(width):
+def sampler_specs(width, first=0):
     return [
-        pl.BlockSpec((1, 2, LANES), lambda i: (i, 0, 0)),
+        pl.BlockSpec((1, 2, LANES), lambda i: (i + first, 0, 0)),
         pl.BlockSpec((len(ROW_ORDER), 1), lambda i: (0, 0)),
-    ] + piece_specs(width)
+    ] + piece_specs(width, first)
 
 
 def row_ids():
@@ -263,25 +326,21 @@
             pltpu.VMEM((CELLS, LANES), bf16),
             pltpu.VMEM((CELLS, width), bf16),
         ],
-        compiler_params=pltpu.CompilerParams(vmem_limit_bytes=40 * MIB),
-        cost_estimate=pl.CostEstimate(
-            flops=2 * images * CELLS * LANES * width,
-            bytes_accessed=2 * images * (CELLS + QUERIES) * width,
-            transcendentals=0,
-        ),
+        compiler_params=pltpu.CompilerParams(vmem_limit_bytes=60 * MIB),
+        cost_estimate=SMALL,
         name="sample",
     )(positions, row_ids(), *pieces)
 
 
-def sample_back(positions, pieces, upstream):
-    images, _, width = pieces[0].shape
+def sample_back(positions, pieces, upstream, first, images):
+    width = pieces[0].shape[2]
     full = (images, STRIP, width)
     half = (images, STRIP // 2, width)
     return pl.pallas_call(
         sample_back_kernel,
         grid=(images,),
-        in_specs=sampler_specs(width)
-        + [pl.BlockSpec((1, STRIP, 9 * width), lambda i: (i, 0, 0))],
+        in_specs=sampler_specs(width, first)
+        + [pl.BlockSpec((1, STRIP, 9 * width), lambda i: (i + first, 0, 0))],
         out_specs=piece_specs(width) + [pl.BlockSpec((1, 2, LANES), lambda i: (i, 0, 0))],
         out_shape=[jax.ShapeDtypeStruct(full, f32)]
         + [jax.ShapeDtypeStruct(full, bf16)] * 4
@@ -297,12 +356,8 @@
             pltpu.VMEM((LANES, width), bf16),
             pltpu.VMEM((CELLS, LANES), f32),
         ],
-        compiler_params=pltpu.CompilerParams(vmem_limit_bytes=48 * MIB),
-        cost_estimate=pl.CostEstimate(
-            flops=4 * images * CELLS * LANES * width,
-            bytes_accessed=4 * images * (CELLS + QUERIES) * width,
-            transcendentals=0,
-        ),
+        compiler_params=pltpu.CompilerParams(vmem_limit_bytes=34 * MIB),
+        cost_estimate=SMALL,
         name="sample_back",
     )(positions, row_ids(), *pieces, upstream)
 
@@ -371,12 +426,8 @@
             jax.ShapeDtypeStruct((images, STRIP, 9 * width), bf16),
         ],
         scratch_shapes=[pltpu.VMEM((16 + 2 * COLS + STRIP, width), f32)],
-        compiler_params=pltpu.CompilerParams(vmem_limit_bytes=40 * MIB),
-        cost_estimate=pl.CostEstimate(
-            flops=18 * images * STRIP * width * width,
-            bytes_accessed=18 * width * width,
-            transcendentals=0,
-        ),
+        compiler_params=pltpu.CompilerParams(vmem_limit_bytes=24 * MIB),
+        cost_estimate=SMALL,
         name="conv",
     )(above, own, below, weight)
 
@@ -394,14 +445,249 @@
             pltpu.VMEM((16 + 2 * COLS + STRIP, width), f32),
             pltpu.VMEM((9, step * STRIP, width), bf16),
         ],
-        compiler_params=pltpu.CompilerParams(vmem_limit_bytes=40 * MIB),
-        cost_estimate=pl.CostEstimate(
-            flops=18 * images * STRIP * width * width,
-            bytes_accessed=18 * width * width,
-            transcendentals=0,
-        ),
+        compiler_params=pltpu.CompilerParams(vmem_limit_bytes=24 * MIB),
+        cost_estimate=SMALL,
         name="conv_back",
     )(above, own, below, weight)
+
+
+TAP = 32
+
+
+def offset_spans(device, rows, wide):
+    spans = []
+    start = device * rows
+    while start < (device + 1) * rows:
+        tap, column = divmod(start, wide)
+        size = min((device + 1) * rows - start, wide - column)
+        spans.append((tap, column, start - device * rows, size))
+        start += size
+    return spans
+
+
+def offset_stack(strip, extra, width):
+    rows = strip.shape[-1]
+    lead = [(0, 0)] * (strip.ndim - 2)
+    strip = jnp.pad(strip, lead + [(0, TAP - 18), (0, 0)])
+    full = rows // width * width
+    blocks = [strip[..., start : start + width] for start in range(0, full, width)]
+    rest = strip[..., full:]
+    rest = jnp.concatenate([rest[..., :16, :], rest[..., 16:, :]], axis=-1)
+    pad = width - rest.shape[-1] - extra.shape[-1]
+    assert pad >= 0
+    blocks.append(jnp.pad(jnp.concatenate([rest, extra], axis=-1), lead + [(0, 0), (0, pad)]))
+    return jnp.concatenate(blocks, axis=-2)
+
+
+def spread_rows(values, images, take):
+    parts = []
+    for image in range(images):
+        parts += take(image)
+    return jnp.concatenate(parts, axis=1)
+
+
+def own_lanes(values, image, start):
+    first = image * STRIP + start
+    return values[:, first : first + STRIP // 2]
+
+
+def rim_lanes(values, image):
+    return values[:, image * STRIP // 2 : (image + 1) * STRIP // 2]
+
+
+def down_two(own, above, images):
+    return spread_rows(own, images, lambda i: [rim_lanes(above, i), own_lanes(own, i, 0)])
+
+
+def up_two(own, below, images):
+    return spread_rows(own, images, lambda i: [own_lanes(own, i, STRIP // 2), rim_lanes(below, i)])
+
+
+def beside(values, steps):
+    if steps == 0:
+        return values
+    rows, cells = values.shape
+    column = lax.broadcasted_iota(jnp.int32, (1, cells), 1) % COLS
+    empty = jnp.zeros((rows, abs(steps)), values.dtype)
+    if steps > 0:
+        moved = jnp.concatenate([values[:, steps:], empty], axis=1)
+    else:
+        moved = jnp.concatenate([empty, values[:, :steps]], axis=1)
+    return jnp.where((column + steps >= 0) & (column + steps < COLS), moved, 0.0)
+
+
+def offset_conv_kernel(rows, small_ref, input_ref, taps_ref, partial_ref, last_ref, first_ref):
+    count, _, width = small_ref.shape
+    wide = input_ref.shape[1]
+    images = input_ref.shape[0] // STRIP
+    full = rows // width
+    rest = rows - full * width
+    for device in range(count):
+        blocks = [small_ref[device, TAP * i : TAP * (i + 1), :] for i in range(full)]
+        if rest:
+            block = small_ref[device, TAP * full : TAP * full + 16, :]
+            blocks.append(
+                jnp.concatenate([block[:, :rest], block[:, rest : 2 * rest]], axis=0)
+            )
+        strip = jnp.concatenate(blocks, axis=1)
+        for tap, column, local, size in offset_spans(device, rows, wide):
+            taps_ref[TAP * tap : TAP * (tap + 1), column : column + size] = strip[
+                :, local : local + size
+            ]
+    partial = dot_nt(taps_ref[...], input_ref[...])
+    partial_ref[...] = partial
+    half = STRIP // 2
+    for image in range(images):
+        lanes = slice(image * half, (image + 1) * half)
+        last_ref[:, lanes] = own_lanes(partial[: 3 * TAP], image, half)
+        first_ref[:, lanes] = own_lanes(partial[6 * TAP :], image, 0)
+
+
+def offset_conv(small_all, rows, inputs):
+    pixels, wide = inputs.shape
+    rim = (3 * TAP, pixels // 2)
+    return pl.pallas_call(
+        partial(offset_conv_kernel, rows),
+        out_shape=[
+            jax.ShapeDtypeStruct((9 * TAP, wide), bf16),
+            jax.ShapeDtypeStruct((9 * TAP, pixels), f32),
+            jax.ShapeDtypeStruct(rim, f32),
+            jax.ShapeDtypeStruct(rim, f32),
+        ],
+        compiler_params=pltpu.CompilerParams(vmem_limit_bytes=24 * MIB),
+        name="offset_conv",
+    )(small_all, inputs)
+
+
+def positions_kernel(partial_ref, above_ref, below_ref, squashed_ref, positions_ref):
+    images = positions_ref.shape[0]
+    rows = [
+        down_two(partial_ref[: 3 * TAP, :], above_ref[...], images),
+        partial_ref[3 * TAP : 6 * TAP, :],
+        up_two(partial_ref[6 * TAP :, :], below_ref[...], images),
+    ]
+    offsets = None
+    for row in rows:
+        for col_tap in range(3):
+            part = beside(row[TAP * col_tap : TAP * (col_tap + 1)], 2 * (col_tap - 1))
+            offsets = part if offsets is None else offsets + part
+    squashed = jnp.tanh(offsets / CLIP)
+    squashed_ref[...] = squashed
+    clipped = CLIP * squashed
+    cells = images * STRIP
+    lane = lax.broadcasted_iota(jnp.int32, (9, cells), 1) % STRIP
+    tap = lax.broadcasted_iota(jnp.int32, (9, cells), 0)
+    row_position = clipped[:9] + (tap // 3 - 1 + HALO + lane // COLS).astype(f32)
+    col_position = clipped[9:18] + (tap % 3 - 1 + lane % COLS).astype(f32)
+    positions_ref[:, :, QUERIES:] = jnp.full((images, 2, LANES - QUERIES), -1000.0, f32)
+    for image in range(images):
+        lanes = slice(image * STRIP, (image + 1) * STRIP)
+        for t in range(9):
+            place = slice(t * STRIP, (t + 1) * STRIP)
+            positions_ref[image, 0:1, place] = row_position[t : t + 1, lanes]
+            positions_ref[image, 1:2, place] = col_position[t : t + 1, lanes]
+
+
+def sample_positions(partial_offsets, above, below):
+    cells = partial_offsets.shape[1]
+    return pl.pallas_call(
+        positions_kernel,
+        out_shape=[
+            jax.ShapeDtypeStruct((TAP, cells), f32),
+            jax.ShapeDtypeStruct((cells // STRIP, 2, LANES), f32),
+        ],
+        name="sample_positions",
+    )(partial_offsets, above, below)
+
+
+def offset_slope_kernel(position_grad_ref, squashed_ref, back_ref, last_ref, first_ref, flat):
+    images = position_grad_ref.shape[0]
+    flat[...] = jnp.zeros_like(flat)
+    for image in range(images):
+        lanes = slice(image * STRIP, (image + 1) * STRIP)
+        for t in range(9):
+            place = slice(t * STRIP, (t + 1) * STRIP)
+            flat[t : t + 1, lanes] = position_grad_ref[image, 0:1, place]
+            flat[9 + t : 10 + t, lanes] = position_grad_ref[image, 1:2, place]
+    squashed = squashed_ref[...]
+    back = (flat[...] * (1.0 - squashed * squashed)).astype(bf16)
+    back_ref[...] = back
+    half = STRIP // 2
+    wider = back.astype(f32)
+    for image in range(images):
+        lanes = slice(image * half, (image + 1) * half)
+        last_ref[:, lanes] = own_lanes(wider, image, half).astype(bf16)
+        first_ref[:, lanes] = own_lanes(wider, image, 0).astype(bf16)
+
+
+def offset_slope(position_grad, squashed):
+    cells = squashed.shape[1]
+    rim = jax.ShapeDtypeStruct((TAP, cells // 2), bf16)
+    return pl.pallas_call(
+        offset_slope_kernel,
+        out_shape=[jax.ShapeDtypeStruct((TAP, cells), bf16), rim, rim],
+        scratch_shapes=[pltpu.VMEM((TAP, cells), f32)],
+        name="offset_slope",
+    )(position_grad, squashed)
+
+
+def offset_back_kernel(rows, back_ref, above_ref, below_ref, input_ref, stacked_ref, chunks_ref):
+    count, _, width = chunks_ref.shape
+    wide = input_ref.shape[1]
+    images = input_ref.shape[0] // STRIP
+    own = back_ref[...].astype(f32)
+    by_row = [
+        up_two(own, below_ref[...].astype(f32), images),
+        own,
+        down_two(own, above_ref[...].astype(f32), images),
+    ]
+    for tap in range(9):
+        moved = beside(by_row[tap // 3], -2 * (tap % 3 - 1))
+        stacked_ref[TAP * tap : TAP * (tap + 1), :] = moved.astype(bf16)
+    grad = dot(stacked_ref[...], input_ref[...])
+    full = rows // width
+    rest = rows - full * width
+    chunks_ref[...] = jnp.zeros(chunks_ref.shape, bf16)
+    for device in range(count):
+        strip = jnp.concatenate(
+            [
+                grad[TAP * tap : TAP * (tap + 1), column : column + size]
+                for tap, column, _, size in offset_spans(device, rows, wide)
+            ],
+            axis=1,
+        ).astype(bf16)
+        for i in range(full):
+            chunks_ref[device, TAP * i : TAP * (i + 1), :] = strip[:, width * i : width * (i + 1)]
+        if rest:
+            tail = strip[:, width * full :]
+            chunks_ref[device, TAP * full :, : 2 * rest] = jnp.concatenate(
+                [tail[:16], tail[16:]], axis=1
+            )
+
+
+def offset_back(back, above, below, inputs, count, rows, width):
+    pixels, wide = inputs.shape
+    stack_rows = rows // width * TAP + (16 if rows % width else 0)
+    return pl.pallas_call(
+        partial(offset_back_kernel, rows),
+        out_shape=[
+            jax.ShapeDtypeStruct((9 * TAP, pixels), bf16),
+            jax.ShapeDtypeStruct((count, stack_rows, width), bf16),
+        ],
+        compiler_params=pltpu.CompilerParams(vmem_limit_bytes=24 * MIB),
+        name="offset_back",
+    )(back, above, below, inputs)
+
+
+def offset_unstack(shard, rows):
+    width = shard.shape[1]
+    full = rows // width
+    rest = rows - full * width
+    blocks = [shard[TAP * i : TAP * i + 18] for i in range(full)]
+    if rest:
+        tail = shard[TAP * full :]
+        blocks.append(jnp.concatenate([tail[:, :rest], tail[:2, rest : 2 * rest]], axis=0))
+    return jnp.concatenate(blocks, axis=1).T
 
 
 def silu_slope(values):
@@ -467,10 +753,9 @@
 
 
 def unstacked_columns(blocks, columns):
-    count, stacked, width = blocks.shape
-    parts = columns // width
-    blocks = blocks.reshape(count, parts, stacked // parts, width).transpose(0, 2, 1, 3)
-    return blocks.reshape(-1, columns)
+    width = blocks.shape[2]
+    parts = jnp.split(blocks, columns // width, axis=1)
+    return jnp.concatenate([part.reshape(-1, width) for part in parts], axis=1)
 
 
 def gather(pieces):
@@ -489,6 +774,15 @@
     return jnp.pad(flat, [(0, 0)] * (flat.ndim - 1) + [(0, pad)]).reshape(
         flat.shape[:-1] + (rows, width)
     )
+
+
+def widths(values, width):
+    pieces = []
+    for start in range(0, values.shape[-1], width):
+        piece = values[..., start : start + width]
+        pad = width - piece.shape[-1]
+        pieces.append(jnp.pad(piece, [(0, 0)] * (values.ndim - 1) + [(0, pad)]))
+    return pieces
 
 
 def shifted(values, steps, columns):
@@ -533,45 +827,41 @@
     count = device_count()
     pixels = images * STRIP
 
+    mid_part = mid // count
+    wide_part = wide // count
+    vector_rows = [mid_gain_one, mid_bias_one, mid_gain_two, mid_bias_two] + [
+        vector[None] for vector in (wide_gain_one, wide_bias_one, wide_gain_two, wide_bias_two)
+    ]
+    extent = max(mid_part, wide_part)
     vectors = jnp.concatenate(
-        [mid_gain_one, mid_bias_one, mid_gain_two, mid_bias_two], axis=0
-    ).reshape(-1)
-    vectors = jnp.concatenate(
-        [vectors, wide_gain_one, wide_bias_one, wide_gain_two, wide_bias_two]
-    )
-    vector_count = vectors.shape[0]
+        [jnp.pad(rows, ((0, 0), (0, extent - rows.shape[1]))) for rows in vector_rows]
+        + [jnp.zeros((4, extent), bf16)],
+        axis=0,
+    )
     offset_rows = offset_one.shape[0]
-    offset_piece = to_width(offset_one.T, mid).transpose(1, 0, 2).reshape(-1, mid)
-    reduce_all, offset_all, vector_all = gather(
-        [reduce_one, offset_piece, to_width(vectors, mid)]
-    )
+    small = offset_stack(offset_one.T, vectors, mid)
+    flat_inputs = images_in.reshape(pixels, wide)
+    flat_out_grad = out_grad.reshape(pixels, wide)
+    reduce_gather = Gather(reduce_one, ((8, 16), (4,), (2,), (1,)))
+    small_gather = Gather(small, ((8, 16), (2,), (4,), (1,)))
+    while reduce_gather.groups:
+        reduce_gather.step()
+        small_gather.step()
+        if len(reduce_gather.groups) == 1:
+            reduce_gather.value, small_gather.value, flat_inputs = meet(
+                reduce_gather.value, small_gather.value, flat_inputs
+            )
+        else:
+            reduce_gather.value, small_gather.value = meet(reduce_gather.value, small_gather.value)
+    reduce_all, small_all = reduce_gather.result(), small_gather.result()
     deform_all, expand_all = gather([deform_one, stacked_columns(expand_one, mid)])
-    reduce_two_all, spatial_all, expand_two_all = gather(
-        [reduce_two, spatial_two, stacked_columns(expand_two, mid)]
-    )
     weight_reduce_one = reduce_all.reshape(wide, mid)
     weight_deform_one = deform_all.reshape(9 * mid, mid)
     weight_expand_one = unstacked_columns(expand_all, wide)
-    weight_reduce_two = reduce_two_all.reshape(wide, mid)
-    weight_spatial_two = spatial_all.reshape(9 * mid, mid)
-    weight_expand_two = unstacked_columns(expand_two_all, wide)
-    tap_weights = (
-        offset_all.reshape(count, -1, 18, mid)
-        .transpose(2, 0, 1, 3)
-        .reshape(18, count, -1)[:, :, :offset_rows]
-        .reshape(18, 9, wide)
-        .transpose(1, 0, 2)
-        .reshape(162, wide)
-    )
-    vector_all = vector_all.reshape(count, -1)[:, :vector_count]
-    mid_part = mid // count
-    wide_part = wide // count
-    mid_vectors = (
-        vector_all[:, : 8 * mid_part].reshape(count, 8, mid_part).transpose(1, 0, 2).reshape(8, mid)
-    )
-    wide_vectors = (
-        vector_all[:, 8 * mid_part :].reshape(count, 4, wide_part).transpose(1, 0, 2).reshape(4, wide)
-    )
+    vector_start = 2 * (offset_rows % mid)
+    vector_all = small_all[:, small.shape[0] - 16 :, vector_start : vector_start + extent]
+    mid_vectors = vector_all[:, :8, :mid_part].transpose(1, 0, 2).reshape(8, mid)
+    wide_vectors = vector_all[:, 8:12, :wide_part].transpose(1, 0, 2).reshape(4, wide)
     gain_mid_one, bias_mid_one = mid_vectors[0:2], mid_vectors[2:4]
     gain_mid_two, bias_mid_two = mid_vectors[4:6], mid_vectors[6:8]
 
@@ -579,11 +869,17 @@
         return values.reshape(images, STRIP, values.shape[-1])
 
     grad_weight = box_weights(box_rows, box_cols, box_count, valid_mask, strip_rows, span_cols)
-    flat_inputs = images_in.reshape(pixels, wide)
-
-    norm_a1 = Norm(dot(flat_inputs, weight_reduce_one), gain_mid_one[0], bias_mid_one[0])
+
+    first_conv = dot(flat_inputs, weight_reduce_one)
+    first_conv, small_all = meet(first_conv, small_all)
+    norm_a1 = Norm(first_conv, gain_mid_one[0], bias_mid_one[0])
+    tap_weights, partial_offsets, last_rim, first_rim = offset_conv(
+        small_all, offset_rows, flat_inputs
+    )
     hidden = jax.nn.silu(norm_a1.forward()).astype(bf16).reshape(images, STRIP, mid)
+    hidden, rim_above, rim_below = meet(hidden, from_behind(last_rim, 1), from_behind(first_rim, -1))
     half = STRIP // 2
+    squashed, positions = sample_positions(partial_offsets, rim_above, rim_below)
     pieces = [
         hidden,
         from_behind(hidden, -1),
@@ -593,32 +889,15 @@
         from_behind(hidden[:, :half], -3),
         from_behind(hidden[:, half:], 3),
     ]
-
-    partial_offsets = dot_nt(tap_weights, flat_inputs).reshape(3, 54, images, STRIP)
-    from_above = from_behind(partial_offsets[0, :, :, half:], 1)
-    from_below = from_behind(partial_offsets[2, :, :, :half], -1)
-    by_row = [
-        jnp.concatenate([from_above, partial_offsets[0, :, :, :half]], axis=-1),
-        partial_offsets[1],
-        jnp.concatenate([partial_offsets[2, :, :, half:], from_below], axis=-1),
-    ]
-    offsets = 0.0
-    for row in by_row:
-        for col_tap in range(3):
-            offsets = offsets + shifted(
-                row[18 * col_tap : 18 * col_tap + 18], 2 * (col_tap - 1), COLS
-            )
-    squashed = jnp.tanh(offsets / CLIP)
-    taps = jnp.arange(9)
-    cells = jnp.arange(STRIP)
-    row_base = ((taps // 3 - 1)[:, None] + (cells // COLS + HALO)[None, :]).astype(f32)
-    col_base = ((taps % 3 - 1)[:, None] + (cells % COLS)[None, :]).astype(f32)
-    base = jnp.stack([row_base, col_base])[:, :, None, :]
-    positions = (CLIP * squashed).reshape(2, 9, images, STRIP) + base
-    positions = positions.transpose(2, 0, 1, 3).reshape(images, 2, QUERIES)
-    positions = jnp.pad(
-        positions, ((0, 0), (0, 0), (0, LANES - QUERIES)), constant_values=-1000.0
-    )
+    positions, reduce_two_, flat_out_grad, *pieces = meet(
+        positions, reduce_two, flat_out_grad, *pieces
+    )
+    reduce_two_all, spatial_all, expand_two_all = gather(
+        [reduce_two_, spatial_two, stacked_columns(expand_two, mid)]
+    )
+    weight_reduce_two = reduce_two_all.reshape(wide, mid)
+    weight_spatial_two = spatial_all.reshape(9 * mid, mid)
+    weight_expand_two = unstacked_columns(expand_two_all, wide)
     sampled = sample(positions, pieces).reshape(pixels, 9 * mid)
     norm_a2 = Norm(dot(sampled, weight_deform_one), gain_mid_one[1], bias_mid_one[1])
     hidden_two = jax.nn.silu(norm_a2.forward()).astype(bf16).reshape(pixels, mid)
@@ -640,9 +919,7 @@
     joined_two = norm_b3.forward() + per_batch(middle).astype(f32)
     block_out = jax.nn.silu(joined_two).astype(bf16).reshape(images_in.shape)
 
-    upstream = per_batch(
-        out_grad.reshape(pixels, wide)
-    ).astype(f32) * grad_weight.reshape(MB, pixels // MB, 1)
+    upstream = per_batch(flat_out_grad).astype(f32) * grad_weight.reshape(MB, pixels // MB, 1)
     masked_six = upstream * silu_slope(joined_two)
     back_sixth = norm_b3.backward(masked_six)
     grad_expand_two = dot_tn(inner_two, back_sixth).astype(bf16)
@@ -650,6 +927,40 @@
         per_batch(dot_nt(back_sixth, weight_expand_two)) * silu_slope(norm_b2.forward())
     )
     grad_spatial_two = dot_tn(inner_slabs.reshape(pixels, 9 * mid), back_fifth).astype(bf16)
+    def chunked(grad):
+        return grad.reshape(count, -1, mid)
+
+    def chunked_columns(grad):
+        return [part.reshape(count, -1, mid) for part in jnp.split(grad, grad.shape[1] // mid, axis=1)]
+
+    def unchunked_columns(shard):
+        return jnp.concatenate(jnp.split(shard, wide // mid, axis=0), axis=1)
+
+    def split_rows(shard, sizes):
+        results = []
+        start = 0
+        for size in sizes:
+            results.append(shard[start : start + size])
+            start += size
+        return results
+
+    column_rows = expand_two.shape[0] * wide // mid
+    spatial_chunks = chunked(grad_spatial_two)
+    cut = spatial_two.shape[0] * 7 // 9
+    two_left = Scatter([spatial_chunks[:, :cut]], (1, 2, 4, 8, 16))
+    two_right = Scatter(
+        [spatial_chunks[:, cut:]] + chunked_columns(grad_expand_two), (1, 4, 2, 8, 16)
+    )
+
+    def beside_steps(value, *scatters):
+        for scatter in scatters:
+            scatter.step()
+        value, *sums = meet(value, *[scatter.value for scatter in scatters])
+        for scatter, total in zip(scatters, sums):
+            scatter.value = total
+        return value
+
+    back_fifth = beside_steps(back_fifth, two_left, two_right)
     back_maps = maps(back_fifth)
     back_inner = conv_back(
         from_behind(back_maps[:, STRIP - COLS :], 1),
@@ -658,114 +969,89 @@
         weight_spatial_two,
     ).reshape(pixels, mid)
     back_fourth = norm_b1.backward(per_batch(back_inner) * silu_slope(norm_b1.forward()))
+    back_fourth = beside_steps(back_fourth, two_left, two_right)
     grad_reduce_two = dot_tn(middle, back_fourth).astype(bf16)
-
-    def chunked(grad):
-        return grad.reshape(count, -1, mid)
-
-    def chunked_columns(grad):
-        parts = grad.shape[1] // mid
-        return (
-            grad.reshape(count, -1, parts, mid).transpose(0, 2, 1, 3).reshape(count, -1, mid)
-        )
-
-    def unchunked_columns(shard):
-        parts = wide // mid
-        return shard.reshape(parts, -1, mid).transpose(1, 0, 2).reshape(-1, wide)
-
-    def split_rows(shard, sizes):
-        results = []
-        start = 0
-        for size in sizes:
-            results.append(shard[start : start + size])
-            start += size
-        return results
-
-    two_sizes = [reduce_two.shape[0], spatial_two.shape[0], expand_two.shape[0] * wide // mid]
-    two_chunks = jnp.concatenate(
-        [chunked(grad_reduce_two), chunked(grad_spatial_two), chunked_columns(grad_expand_two)],
-        axis=1,
-    )
-    two_shards = split_rows(
-        lax.psum_scatter(
-            two_chunks.reshape(-1, mid), BOTH, scatter_dimension=0, tiled=True
-        ).astype(f32),
-        two_sizes,
-    )
 
     back_middle = masked_six + per_batch(dot_nt(back_fourth, weight_reduce_two))
     masked_three = back_middle * silu_slope(joined_one)
     back_third = norm_a3.backward(masked_three)
+    back_third = beside_steps(back_third, two_left, two_right)
     grad_expand_one = dot_tn(hidden_two, back_third).astype(bf16)
     back_second = norm_a2.backward(
         per_batch(dot_nt(back_third, weight_expand_one)) * silu_slope(norm_a2.forward())
     )
+    back_second = beside_steps(back_second, two_left, two_right)
     grad_deform_one = dot_tn(sampled, back_second).astype(bf16)
-    one_sizes = [deform_one.shape[0], expand_one.shape[0] * wide // mid]
-    one_shards = split_rows(
-        scatter_sum(
-            jnp.concatenate([chunked(grad_deform_one), chunked_columns(grad_expand_one)], axis=1),
-            (1, 4, 2, 8, 16),
-        ),
-        one_sizes,
+    one_left = Scatter([chunked(grad_deform_one)], (1, 2, 4, 8, 16))
+    one_right = Scatter(
+        chunked_columns(grad_expand_one) + [chunked(grad_reduce_two)], (1, 4, 2, 8, 16)
+    )
+    back_second, one_left.value, one_right.value = meet(
+        back_second, one_left.value, one_right.value
     )
     back_sampled = dot_nt(back_second, weight_deform_one).astype(bf16).reshape(images, STRIP, -1)
-    own, *others, position_grad = sample_back(positions, pieces, back_sampled)
-    own = (
-        own
-        + from_behind(others[0], 1).astype(f32)
-        + from_behind(others[1], -1).astype(f32)
-        + from_behind(others[2], 2).astype(f32)
-        + from_behind(others[3], -2).astype(f32)
-        + jnp.concatenate(
-            [from_behind(others[4], 3).astype(f32), from_behind(others[5], -3).astype(f32)], axis=1
+    back_sampled = beside_steps(back_sampled, one_left, one_right, two_left, two_right)
+
+    def returned(upstream, first):
+        own, *others, position_grad = sample_back(
+            positions, pieces, upstream, first, images // MB
         )
-    )
-    back_clipped = (
-        position_grad[:, :, :QUERIES]
-        .reshape(images, 2, 9, STRIP)
-        .transpose(1, 2, 0, 3)
-        .reshape(18, images, STRIP)
-    )
-    back_offsets = (back_clipped * (1.0 - squashed * squashed)).astype(bf16)
-    rim_above = from_behind(back_offsets[:, :, half:], 1)
-    rim_below = from_behind(back_offsets[:, :, :half], -1)
-    by_row = [
-        jnp.concatenate([back_offsets[:, :, half:], rim_below], axis=-1),
+        half_sum = jnp.concatenate([from_behind(others[4], 3), from_behind(others[5], -3)], axis=1)
+        own = (
+            own
+            + from_behind(others[0], 1).astype(f32)
+            + from_behind(others[1], -1).astype(f32)
+            + from_behind(others[2], 2).astype(f32)
+            + from_behind(others[3], -2).astype(f32)
+            + half_sum.astype(f32)
+        )
+        return own, position_grad
+
+    backs = [returned(back_sampled, 0)]
+    back_sampled = beside_steps(back_sampled, one_left, one_right)
+    backs.append(returned(back_sampled, images // MB))
+    own = jnp.concatenate([pair[0] for pair in backs], axis=0)
+    own = beside_steps(own, one_left, one_right)
+    position_grad = jnp.concatenate([pair[1] for pair in backs], axis=0)
+    back_offsets, last_rim, first_rim = offset_slope(position_grad, squashed)
+    stacked, offset_chunks = offset_back(
         back_offsets,
-        jnp.concatenate([rim_above, back_offsets[:, :, :half]], axis=-1),
-    ]
-    stacked = jnp.concatenate(
-        [shifted(row, -2 * (col_tap - 1), COLS) for row in by_row for col_tap in range(3)], axis=0
-    ).reshape(162, pixels)
-    grad_offset_one = dot(stacked, flat_inputs).astype(bf16)
-    grad_offset_one = (
-        grad_offset_one.reshape(9, 18, wide)
-        .transpose(1, 0, 2)
-        .reshape(18, count, offset_rows)
-        .transpose(1, 0, 2)
-    )
-    offset_chunks = to_width(grad_offset_one, mid).transpose(0, 2, 1, 3).reshape(count, -1, mid)
+        from_behind(last_rim, 1),
+        from_behind(first_rim, -1),
+        flat_inputs,
+        count,
+        offset_rows,
+        mid,
+    )
     offset_to_images = dot_tn(stacked, tap_weights)
 
     back_first = norm_a1.backward(
         per_batch(own.reshape(pixels, mid)) * silu_slope(norm_a1.forward())
     )
+    offset_sum = Scatter([offset_chunks], (1, 4, 2, 8, 16))
+    back_first = beside_steps(back_first, one_left, one_right, offset_sum)
     grad_reduce_one = dot_tn(flat_inputs, back_first).astype(bf16)
+    half_rows = reduce_one.shape[0] // 2
+    last_chunks = chunked(grad_reduce_one)
+    last_left = Scatter([last_chunks[:, :half_rows]], (1, 2, 4, 8, 16))
+    last_right = Scatter([last_chunks[:, half_rows:]], (1, 4, 2, 8, 16))
+    back_first = beside_steps(back_first, last_left, last_right)
     grad_images = (
         masked_three.reshape(pixels, wide)
         + dot_nt(back_first, weight_reduce_one)
         + offset_to_images
-    ).reshape(images_in.shape)
-    last_shards = split_rows(
-        scatter_sum(
-            jnp.concatenate([chunked(grad_reduce_one), offset_chunks], axis=1), (1, 2, 4, 8, 16)
-        ),
-        [reduce_one.shape[0], offset_chunks.shape[1]],
-    )
-    offset_shard = (
-        last_shards[1].reshape(-1, 18, mid).transpose(1, 0, 2).reshape(18, -1)[:, :offset_rows].T
-    )
+    )
+    grad_images = beside_steps(grad_images, last_left, last_right).reshape(images_in.shape)
+    reduce_shard = jnp.concatenate([last_left.finish(), last_right.finish()], axis=0)
+    offset_shard = offset_unstack(offset_sum.finish(), offset_rows)
+    deform_shard = one_left.finish()
+    expand_shard, reduce_two_shard = split_rows(
+        one_right.finish(), [column_rows, reduce_two.shape[0]]
+    )
+    two_rest, expand_two_shard = split_rows(
+        two_right.finish(), [spatial_two.shape[0] - cut, column_rows]
+    )
+    spatial_shard = jnp.concatenate([two_left.finish(), two_rest], axis=0)
 
     me = lax.axis_index(BOTH)
     mid_grads = jnp.stack(
@@ -788,17 +1074,17 @@
     return (
         block_out,
         grad_images,
-        last_shards[0],
+        reduce_shard,
         offset_shard,
-        one_shards[0],
-        unchunked_columns(one_shards[1]),
+        deform_shard,
+        unchunked_columns(expand_shard),
         mid_grads[0:2],
         mid_grads[2:4],
         wide_grads[0],
         wide_grads[1],
-        two_shards[0],
-        two_shards[1],
-        unchunked_columns(two_shards[2]),
+        reduce_two_shard,
+        spatial_shard,
+        unchunked_columns(expand_two_shard),
         mid_grads[4:6],
         mid_grads[6:8],
         wide_grads[2],

time: 864 us -> 793 us (0.918)
  waiting for transfers between devices: 275 us -> 194 us
  local copies, waits for them, and re-layouts: 175 us -> 112 us
  starting transfers between devices: 186 us -> 238 us
  other arithmetic: 60 us -> 86.1 us
  matrix products: 86.8 us -> 69.1 us
  Pallas kernels: 54.9 us -> 65.1 us
    ppermute x20 -> x26, waiting for transfers between devices: 99.6 us -> 38.5 us  [from_behind(): lax.ppermute(value, 'rows', [(source, source + steps) for source in range...]
    ppermute x94 -> x131, starting transfers between devices: 111 us -> 160 us  [exchange(): lax.ppermute(value, BOTH, [(i, i ^ mask) for i in range(device_count())])]
    all_gather x3 -> x2, waiting for transfers between devices: 48.3 us -> 4.05 us  [gather(): whole = lax.all_gather(jnp.concatenate(pieces, axis=0), BOTH, axis=0)]
    reshape x28 -> x2, local copies, waits for them, and re-layouts: 44.5 us -> 10.2 us  [the longest x1 5.86 us: on_device(): beside_steps(grad_images, last_left, last_right).reshape(images_in.shape)]
    convert_element_type x5 -> x0, local copies, waits for them, and re-layouts: 25.4 us -> none  [the longest x2 12.1 us: on_device(): upstream = per_batch(out_grad.reshape(pixels, wide)).astype(f32) * grad_w...]
    ppermute x94 -> x131, waiting for transfers between devices: 127 us -> 152 us  [exchange(): lax.ppermute(value, BOTH, [(i, i ^ mask) for i in range(device_count())])]
    convert_element_type x12 -> x29, other arithmetic: 11.7 us -> 27.9 us  [the longest x28 27.5 us: step(): self.value = total.astype(bf16) if self.order else total]
    unnamed x252 -> x351, local copies, waits for them, and re-layouts: 43.5 us -> 54.5 us
  transfers between devices with their start and end apart: 118 -> 159, of which waited for: 62 -> 86; matrix products, arithmetic and copies ran while one was open for 29% -> 22% of each run, Pallas kernels for 6% -> 7%
where the time goes in v2:
time: 793 us; the launch traced here: 783 us
  starting transfers between devices  238 us (30%)
  waiting for transfers between devices  194 us (24%)
  local copies, waits for them, and re-layouts  112 us (14%)
  other arithmetic  86.1 us (11%)
  matrix products  69.1 us (9%)
  Pallas kernels  65.1 us (8%)
  between operations  17.7 us (2%)
    ppermute x131, starting transfers between devices, exchange(): lax.ppermute(value, BOTH, [(i, i ^ mask) for i in range(device_count())])  160 us
    ppermute x131, waiting for transfers between devices, exchange(): lax.ppermute(value, BOTH, [(i, i ^ mask) for i in range(device_count())])  152 us
    ppermute x26, starting transfers between devices, from_behind(): lax.ppermute(value, 'rows', [(source, source + steps) for source in range...  77.5 us
    unnamed x351, local copies, waits for them, and re-layouts  54.5 us
    ppermute x26, waiting for transfers between devices, from_behind(): lax.ppermute(value, 'rows', [(source, source + steps) for source in range...  38.5 us
    pallas_call x2, Pallas kernels, sample_back(): pl.pallas_call(sample_back_kernel, grid=(images,), in_specs=sampler_specs...  32.4 us
    dot_general x7, matrix products, dot_tn(): lax.dot_general(left, right, (((0,), (0,)), ((), ())), preferred_element_...  27.7 us
    convert_element_type x28, other arithmetic, step(): self.value = total.astype(bf16) if self.order else total  27.5 us
  transfers between devices with their start and end apart: 159, of which 86 were waited for; matrix products, arithmetic and copies ran while one was open for 22% of the time, Pallas kernels for 7%

profile of v2, /device:TPU:0, one launch (start us, length us, event | category | flops | bytes accessed | tf_op | source)
XLA Modules:
  0.0 782.7 jit_solution(13517495637368205225)
XLA Ops:
  16.8 3.1 collective-permute-start.5
  26.9 6.1 collective-permute-done.4
  33.0 4.6 collective-permute-done.1
  40.9 3.5 collective-permute-done.7
  45.2 4.4 collective-permute-done.6
  52.3 3.3 copy.84
  84.4 3.9 collective-permute-start.18
  108.5 5.5 collective-permute-start.22
  115.2 5.4 collective-permute-start.24
  120.6 5.6 collective-permute-start.26
  126.2 3.3 copy.87
  129.5 4.3 reshape.691
  136.4 9.3 %collective-permute-done.26.refs_6_ = bf16[4,88,512]{2,1,0:T(8,128)(2,1)} collective-permute-done((bf16[4,88,512]{2,1,0:T(8,128)(2,1)}, bf16[4,88,512]{2,1,0:T(8,128)(2,1)}, u32[]{:S(2)}, u32[]{:S(2)}) %collective-permute-start.26) | collective-permute-done | bytes 360480 | tf_op jit(solution)/shard_map/ppermute | solution.py:147
  154.9 17.5 %sample.1 = bf16[4,176,4608]{2,1,0:T(8,128)(2,1)} custom-call(f32[4,2,1664]{2,1,0:T(2,128)} %get-tuple-element.124.pos_ref, f32[24,1]{1,0:T(8,128)} %constant.539.row_ref, bf16[4,176,512]{2,1,0:T(8,128)(2,1)} %multiply_convert_fusion.10.refs_0_, bf16[4,176,512]{2,1,0:T(8,128)(2,1)} %collective-permute-done.21.refs_1_, ...), custom_call_target="tpu_custom_call" | custom-call | flops 1 | bytes 1 | tf_op jit(solution)/shard_map/sample/pallas_call | solution.py:317
  177.8 4.6 fusion.111
  186.9 7.6 collective-permute-start.30
  194.5 8.2 %collective-permute-start.31 = (f32[4,512]{1,0:T(4,128)S(1)}, f32[4,512]{1,0:T(4,128)S(1)}, u32[]{:S(2)}, u32[]{:S(2)}) collective-permute-start(f32[4,512]{1,0:T(4,128)S(1)} %add_add_fusion.21), channel_id=1, source_target_pairs={{0,8},{1,9},{2,10},{3,11},{4,12},{5,13},{6,14},{7,15},{8,0},{9,1},... | collective-permute-start | bytes 24584 | tf_op jit(solution)/shard_map/ppermute | solution.py:50
  213.7 3.9 fusion.104
  219.6 3.1 collective-permute-done.35
  228.6 3.2 collective-permute-done.38
  234.7 5.0 collective-permute-done.40
  240.4 5.6 multiply_convert_fusion.3
  246.0 4.1 all-gather.7.cloned.1.call-done
  268.1 3.5 collective-permute-done.47
  274.2 3.0 collective-permute-start.48
  284.7 4.1 conv.1
  310.4 4.9 fusion.103
  332.0 8.2 %fusion.102 = (f32[2,2048]{1,0:T(2,128)S(1)}, f32[2,2048]{1,0:T(2,128)S(1)}, f32[2,352,2048]{2,1,0:T(8,128)S(1)}, bf16[2,352,2048]{2,1,0:T(8,128)(2,1)}) fusion(f32[2,2048]{1,0:T(2,128)S(1)} %get-tuple-element.370, f32[2,352,2048]{2,1,0:T(8,128)} %get-tuple-element.405, f32[2,2048]{1,0:T(2,128)S(1)} %get-tuple-element.371, ...), kind=kLoop, calls=%fused_computation.414 | loop fusion | flops 30269440 | bytes 20269824 | tf_op jit(solution)/shard_map/reduce_sum | solution.py:717
  353.6 3.7 collective-permute-done.70
  359.8 3.3 fusion.108
  371.0 4.1 bitcast_convert_fusion
  376.5 3.4 collective-permute-done.77
  380.3 7.4 convolution_convert_fusion.2
  395.2 3.6 fusion.5
  398.7 3.4 fusion.4
  406.2 3.4 collective-permute-done.80.above
  409.6 4.6 collective-permute-done.81.below
  417.6 3.8 conv_back.1
  435.2 12.4 %collective-permute-done.85 = f32[4,512]{1,0:T(4,128)S(1)} collective-permute-done((f32[4,512]{1,0:T(4,128)S(1)}, f32[4,512]{1,0:T(4,128)S(1)}, u32[]{:S(2)}, u32[]{:S(2)}) %collective-permute-start.85) | collective-permute-done | bytes 8224 | tf_op jit(solution)/shard_map/ppermute | solution.py:50
  447.6 3.0 collective-permute-start.88
  457.8 7.7 fusion.101
  480.2 3.2 convolution_convert_fusion.4
  499.8 4.3 collective-permute-done.104
  510.1 4.6 convolution_convert_fusion.1
  522.6 9.0 %convolution_convert_fusion = bf16[704,4608]{1,0:T(8,128)(2,1)} fusion(bf16[704,512]{1,0:T(8,128)(2,1)} %bitcast.521, bf16[4608,512]{1,0:T(8,128)(2,1)} %bitcast.497), kind=kOutput, calls=%fused_computation | convolution fusion | flops 3325132800 | bytes 11927552 | tf_op jit(solution)/shard_map/dot_general | solution.py:38
  535.8 3.2 fusion.2
  543.1 4.3 reshape.704
  547.4 5.8 copy.105
  556.7 16.3 %sample_back.2 = (f32[2,176,512]{2,1,0:T(8,128)S(1)}, bf16[2,176,512]{2,1,0:T(8,128)(2,1)}, bf16[2,176,512]{2,1,0:T(8,128)(2,1)}, bf16[2,176,512]{2,1,0:T(8,128)...) custom-call(f32[4,2,1664]{2,1,0:T(2,128)S(1)} %copy-done.20, ...), custom_call_target="tpu_custom_call" | custom-call | flops 1 | bytes 1 | tf_op jit(solution)/shard_map/sample_back/pallas_call | solution.py:339
  573.8 4.0 collective-permute-start.113
  579.1 4.7 collective-permute-start.115
  589.7 4.1 collective-permute-done.117
  599.1 16.1 %sample_back.3 = (f32[2,176,512]{2,1,0:T(8,128)S(1)}, bf16[2,176,512]{2,1,0:T(8,128)(2,1)S(1)}, bf16[2,176,512]{2,1,0:T(8,128)(2,1)}, bf16[2,176,512]{2,1,0:T(8,...) custom-call(f32[4,2,1664]{2,1,0:T(2,128)S(1)} %copy-done.20, ...), custom_call_target="tpu_custom_call" | custom-call | flops 1 | bytes 1 | tf_op jit(solution)/shard_map/sample_back/pallas_call | solution.py:339
  616.9 11.0 %collective-permute-start.125 = (bf16[2,88,512]{2,1,0:T(8,128)(2,1)}, bf16[2,88,512]{2,1,0:T(8,128)(2,1)}, u32[]{:S(2)}, u32[]{:S(2)}) collective-permute-start(bf16[2,88,512]{2,1,0:T(8,128)(2,1)} %get-tuple-element.167), channel_id=1, source_target_pairs={{0,12},{4,16},{8,20},{12,24},{16,28},{1,13},{5,17},{9,21},{13,25},... | collective-permute-start | bytes 540680 | tf_op jit(solution)/shard_map/ppermute | solution.py:147
  635.6 5.2 collective-permute-start.121
  642.1 6.9 collective-permute-start.123
  653.9 8.2 %collective-permute-done.126 = bf16[2,88,512]{2,1,0:T(8,128)(2,1)S(1)} collective-permute-done((bf16[2,88,512]{2,1,0:T(8,128)(2,1)S(1)}, bf16[2,88,512]{2,1,0:T(8,128)(2,1)S(1)}, u32[]{:S(2)}, u32[]{:S(2)}) %collective-permute-start.126) | collective-permute-done | bytes 180256 | tf_op jit(solution)/shard_map/ppermute | solution.py:147
  664.7 8.4 %collective-permute-start.127 = (bf16[2,2,144,512]{3,2,1,0:T(8,128)(2,1)S(1)}, bf16[2,2,144,512]{3,2,1,0:T(8,128)(2,1)S(1)}, u32[]{:S(2)}, u32[]{:S(2)}) collective-permute-start(bf16[2,2,144,512]{3,2,1,0:T(8,128)(2,1)S(1)} %dynamic-slice_bitcast_fusion.8), channel_id=1, source_target_pairs={{0,4},{1,5},{2,6},{3,7},{4,0},{5,1},{6,2},{7,3},{8,12},{9,13},{10,... | collective-permute-start | bytes 1769480 | tf_op jit(solution)/shard_map/ppermute | solution.py:50
  675.5 8.3 %collective-permute-done.127 = bf16[2,2,144,512]{3,2,1,0:T(8,128)(2,1)S(1)} collective-permute-done((bf16[2,2,144,512]{3,2,1,0:T(8,128)(2,1)S(1)}, bf16[2,2,144,512]{3,2,1,0:T(8,128)(2,1)S(1)}, u32[]{:S(2)}, u32[]{:S(2)}) %collective-permute-start.127) | collective-permute-done | bytes 589856 | tf_op jit(solution)/shard_map/ppermute | solution.py:50
  719.2 3.5 collective-permute-done.156
  730.6 3.4 collective-permute-done.152
  738.9 4.7 fusion.1
  747.8 5.9 reshape.724
  753.6 9.0 %copy.106 = f32[4,4,44,2048]{3,1,2,0:T(4,128)} copy(f32[4,4,44,2048]{3,2,1,0:T(8,128)} %reshape.724) | data formatting | bytes 11534336
  (895 shorter events, 398.7 us)
Async XLA Ops:
  7.2 165.2 %all-gather.5.cloned.1.call-start = ((), (), s32[]{:S(2)}) async-start(), calls=%async_computation | async-start | bytes 7028736 | tf_op jit(solution)/shard_map/all_gather | solution.py:762
  11.8 238.3 %all-gather.7.cloned.1.call-start = ((), (), s32[]{:S(2)}) async-start(), calls=%async_computation.1 | async-start | bytes 9191424 | tf_op jit(solution)/shard_map/all_gather | solution.py:762
  16.8 8.9 %collective-permute-start.5 = (bf16[48,512]{1,0:T(8,128)(2,1)S(1)}, bf16[48,512]{1,0:T(8,128)(2,1)S(1)}, u32[]{:S(2)}, u32[]{:S(2)}) collective-permute-start(bf16[48,512]{1,0:T(8,128)(2,1)S(1)} %pad_maximum_fusion.21), channel_id=1, source_target_pairs={{0,8},{1,9},{2,10},{3,11},{4,12},{5,13},{6,14},{7,15},{8,0},{9,1},... | collective-permute-start | bytes 147464 | tf_op jit(solution)/shard_map/ppermute | solution.py:50
  22.3 10.6 %collective-permute-start.4 = (bf16[48,512]{1,0:T(8,128)(2,1)S(1)}, bf16[48,512]{1,0:T(8,128)(2,1)S(1)}, u32[]{:S(2)}, u32[]{:S(2)}) collective-permute-start(bf16[48,512]{1,0:T(8,128)(2,1)S(1)} %pad_maximum_fusion.21), channel_id=1, source_target_pairs={{0,16},{1,17},{2,18},{3,19},{4,20},{5,21},{6,22},{7,23},{8,24},{9,... | collective-permute-start | bytes 147464 | tf_op jit(solution)/shard_map/ppermute | solution.py:50
  22.4 10.6 %collective-permute-start = (bf16[64,512]{1,0:T(8,128)(2,1)}, bf16[64,512]{1,0:T(8,128)(2,1)S(1)}, u32[]{:S(2)}, u32[]{:S(2)}) collective-permute-start(bf16[64,512]{1,0:T(8,128)(2,1)} %param.30), channel_id=1, source_target_pairs={{0,24},{1,25},{2,26},{3,27},{4,28},{5,29},{6,30},{7,31},{8,16},{9,... | collective-permute-start | bytes 196616 | tf_op jit(solution)/shard_map/ppermute | solution.py:50
  25.4 12.3 %collective-permute-start.1 = (bf16[64,512]{1,0:T(8,128)(2,1)}, bf16[64,512]{1,0:T(8,128)(2,1)S(1)}, u32[]{:S(2)}, u32[]{:S(2)}) collective-permute-start(bf16[64,512]{1,0:T(8,128)(2,1)} %param.30), channel_id=1, source_target_pairs={{0,16},{1,17},{2,18},{3,19},{4,20},{5,21},{6,22},{7,23},{8,24},{9,... | collective-permute-start | bytes 196616 | tf_op jit(solution)/shard_map/ppermute | solution.py:50
  39.4 10.2 %collective-permute-start.6 = (bf16[2,2,64,512]{3,2,1,0:T(8,128)(2,1)S(1)}, bf16[2,2,64,512]{3,2,1,0:T(8,128)(2,1)S(1)}, u32[]{:S(2)}, u32[]{:S(2)}) collective-permute-start(bf16[2,2,64,512]{3,2,1,0:T(8,128)(2,1)S(1)} %pad_maximum_fusion.11), channel_id=1, source_target_pairs={{0,4},{1,5},{2,6},{3,7},{4,0},{5,1},{6,2},{7,3},{8,12},{9,13},{10,... | collective-permute-start | bytes 786440 | tf_op jit(solution)/shard_map/ppermute | solution.py:50
  49.8 9.0 %collective-permute-start.9 = (bf16[2,2,2,48,512]{4,3,1,0,2:T(8,128)(2,1)}, bf16[2,2,2,48,512]{4,3,1,0,2:T(8,128)(2,1)}, u32[]{:S(2)}, u32[]{:S(2)}) collective-permute-start(bf16[2,2,2,48,512]{4,3,1,0,2:T(8,128)(2,1)} %pad_maximum_fusion.7), channel_id=1, source_target_pairs={{0,4},{1,5},{2,6},{3,7},{4,0},{5,1},{6,2},{7,3},{8,12},{9,13},{10,... | collective-permute-start | bytes 1179656 | tf_op jit(solution)/shard_map/ppermute | solution.py:50
  52.3 11.1 %collective-permute-start.8 = (bf16[2,2,2,64,512]{4,3,2,1,0:T(8,128)(2,1)S(1)}, bf16[2,2,2,64,512]{4,3,2,1,0:T(8,128)(2,1)}, u32[]{:S(2)}, u32[]{:S(2)}) collective-permute-start(bf16[2,2,2,64,512]{4,3,2,1,0:T(8,128)(2,1)S(1)} %pad_maximum_fusion.6), channel_id=1, source_target_pairs={{0,2},{1,3},{2,0},{3,1},{4,6},{5,7},{6,4},{7,5},{8,10},{9,11},{10,... | collective-permute-start | bytes 1572872 | tf_op jit(solution)/shard_map/ppermute | solution.py:50
  84.4 13.8 %collective-permute-start.18 = (f32[4,512]{1,0:T(4,128)S(1)}, f32[4,512]{1,0:T(4,128)S(1)}, u32[]{:S(2)}, u32[]{:S(2)}) collective-permute-start(f32[4,512]{1,0:T(4,128)S(1)} %add_add_fusion.22), channel_id=1, source_target_pairs={{0,16},{1,17},{2,18},{3,19},{4,20},{5,21},{6,22},{7,23},{8,24},{9,... | collective-permute-start | bytes 24584 | tf_op jit(solution)/shard_map/ppermute | solution.py:50
  94.4 8.0 %collective-permute-start.19 = (f32[96,352]{1,0:T(8,128)S(1)}, f32[96,352]{1,0:T(8,128)S(1)}, u32[]{:S(2)}, u32[]{:S(2)}) collective-permute-start(f32[96,352]{1,0:T(8,128)S(1)} %get-tuple-element.118), channel_id=1, source_target_pairs={{0,4},{4,8},{8,12},{12,16},{16,20},{20,24},{24,28},{1,5},{5,9},{9,... | collective-permute-start | bytes 405512 | tf_op jit(solution)/shard_map/ppermute | solution.py:147
  105.9 14.8 %collective-permute-start.25 = (bf16[4,88,512]{2,1,0:T(8,128)(2,1)S(1)}, bf16[4,88,512]{2,1,0:T(8,128)(2,1)S(1)}, u32[]{:S(2)}, u32[]{:S(2)}) collective-permute-start(bf16[4,88,512]{2,1,0:T(8,128)(2,1)S(1)} %get-tuple-element.337), channel_id=1, source_target_pairs={{12,0},{16,4},{20,8},{24,12},{28,16},{13,1},{17,5},{21,9},{25,13},... | collective-permute-start | bytes 1081352 | tf_op jit(solution)/shard_map/ppermute | solution.py:147
  107.2 38.5 %collective-permute-start.21 = (bf16[4,176,512]{2,1,0:T(8,128)(2,1)}, bf16[4,176,512]{2,1,0:T(8,128)(2,1)}, u32[]{:S(2)}, u32[]{:S(2)}) collective-permute-start(bf16[4,176,512]{2,1,0:T(8,128)(2,1)} %multiply_convert_fusion.10.refs_0_), channel_id=1, source_target_pairs={{4,0},{8,4},{12,8},{16,12},{20,16},{24,20},{28,24},{5,1},{9,5},{13... | collective-permute-start | bytes 2162696 | tf_op jit(solution)/shard_map/ppermute | solution.py:147
  108.5 40.0 %collective-permute-start.22 = (bf16[4,176,512]{2,1,0:T(8,128)(2,1)}, bf16[4,176,512]{2,1,0:T(8,128)(2,1)}, u32[]{:S(2)}, u32[]{:S(2)}) collective-permute-start(bf16[4,176,512]{2,1,0:T(8,128)(2,1)} %multiply_convert_fusion.10.refs_0_), channel_id=1, source_target_pairs={{0,4},{4,8},{8,12},{12,16},{16,20},{20,24},{24,28},{1,5},{5,9},{9,... | collective-permute-start | bytes 2162696 | tf_op jit(solution)/shard_map/ppermute | solution.py:147
  113.9 35.6 %collective-permute-start.23 = (bf16[4,176,512]{2,1,0:T(8,128)(2,1)}, bf16[4,176,512]{2,1,0:T(8,128)(2,1)}, u32[]{:S(2)}, u32[]{:S(2)}) collective-permute-start(bf16[4,176,512]{2,1,0:T(8,128)(2,1)} %multiply_convert_fusion.10.refs_0_), channel_id=1, source_target_pairs={{8,0},{12,4},{16,8},{20,12},{24,16},{28,20},{9,1},{13,5},{17,9},{2... | collective-permute-start | bytes 2162696 | tf_op jit(solution)/shard_map/ppermute | solution.py:147
  115.2 34.3 %collective-permute-start.24 = (bf16[4,176,512]{2,1,0:T(8,128)(2,1)}, bf16[4,176,512]{2,1,0:T(8,128)(2,1)}, u32[]{:S(2)}, u32[]{:S(2)}) collective-permute-start(bf16[4,176,512]{2,1,0:T(8,128)(2,1)} %multiply_convert_fusion.10.refs_0_), channel_id=1, source_target_pairs={{0,8},{4,12},{8,16},{12,20},{16,24},{20,28},{1,9},{5,13},{9,17},{1... | collective-permute-start | bytes 2162696 | tf_op jit(solution)/shard_map/ppermute | solution.py:147
  120.6 25.0 %collective-permute-start.26 = (bf16[4,88,512]{2,1,0:T(8,128)(2,1)}, bf16[4,88,512]{2,1,0:T(8,128)(2,1)}, u32[]{:S(2)}, u32[]{:S(2)}) collective-permute-start(bf16[4,88,512]{2,1,0:T(8,128)(2,1)} %get-tuple-element.336), channel_id=1, source_target_pairs={{0,12},{4,16},{8,20},{12,24},{16,28},{1,13},{5,17},{9,21},{13,25},... | collective-permute-start | bytes 1081352 | tf_op jit(solution)/shard_map/ppermute | solution.py:147
  186.9 17.3 %collective-permute-start.30 = (f32[4,512]{1,0:T(4,128)S(1)}, f32[4,512]{1,0:T(4,128)S(1)}, u32[]{:S(2)}, u32[]{:S(2)}) collective-permute-start(f32[4,512]{1,0:T(4,128)S(1)} %add_add_fusion.21), channel_id=1, source_target_pairs={{0,4},{1,5},{2,6},{3,7},{4,0},{5,1},{6,2},{7,3},{8,12},{9,13},{10,... | collective-permute-start | bytes 24584 | tf_op jit(solution)/shard_map/ppermute | solution.py:50
  194.5 9.8 %collective-permute-start.31 = (f32[4,512]{1,0:T(4,128)S(1)}, f32[4,512]{1,0:T(4,128)S(1)}, u32[]{:S(2)}, u32[]{:S(2)}) collective-permute-start(f32[4,512]{1,0:T(4,128)S(1)} %add_add_fusion.21), channel_id=1, source_target_pairs={{0,8},{1,9},{2,10},{3,11},{4,12},{5,13},{6,14},{7,15},{8,0},{9,1},... | collective-permute-start | bytes 24584 | tf_op jit(solution)/shard_map/ppermute | solution.py:50
  274.2 8.3 %collective-permute-start.48 = (bf16[4,44,512]{2,1,0:T(8,128)(2,1)S(1)}, bf16[4,44,512]{2,1,0:T(8,128)(2,1)S(1)}, u32[]{:S(2)}, u32[]{:S(2)}) collective-permute-start(bf16[4,44,512]{2,1,0:T(8,128)(2,1)S(1)} %get-tuple-element.335), channel_id=1, source_target_pairs={{0,4},{4,8},{8,12},{12,16},{16,20},{20,24},{24,28},{1,5},{5,9},{9,... | collective-permute-start | bytes 540680 | tf_op jit(solution)/shard_map/ppermute | solution.py:147
  404.9 9.3 %collective-permute-start.81 = (bf16[4,44,512]{2,1,0:T(8,128)(2,1)S(1)}, bf16[4,44,512]{2,1,0:T(8,128)(2,1)S(1)}, u32[]{:S(2)}, u32[]{:S(2)}) collective-permute-start(bf16[4,44,512]{2,1,0:T(8,128)(2,1)S(1)} %get-tuple-element.332), channel_id=1, source_target_pairs={{4,0},{8,4},{12,8},{16,12},{20,16},{24,20},{28,24},{5,1},{9,5},{13... | collective-permute-start | bytes 540680 | tf_op jit(solution)/shard_map/ppermute | solution.py:147
  426.3 28.3 %collective-permute-start.90 = (bf16[2,2,2,96,512]{4,3,2,1,0:T(8,128)(2,1)}, bf16[2,2,2,96,512]{4,3,2,1,0:T(8,128)(2,1)}, u32[]{:S(2)}, u32[]{:S(2)}) collective-permute-start(bf16[2,2,2,96,512]{4,3,2,1,0:T(8,128)(2,1)} %dynamic-slice_bitcast_fusion.7), channel_id=1, source_target_pairs={{0,4},{1,5},{2,6},{3,7},{4,0},{5,1},{6,2},{7,3},{8,12},{9,13},{10,... | collective-permute-start | bytes 2359304 | tf_op jit(solution)/shard_map/ppermute | solution.py:50
  429.0 18.6 %collective-permute-start.85 = (f32[4,512]{1,0:T(4,128)S(1)}, f32[4,512]{1,0:T(4,128)S(1)}, u32[]{:S(2)}, u32[]{:S(2)}) collective-permute-start(f32[4,512]{1,0:T(4,128)S(1)} %add_add_fusion.13), channel_id=1, source_target_pairs={{0,4},{1,5},{2,6},{3,7},{4,0},{5,1},{6,2},{7,3},{8,12},{9,13},{10,... | collective-permute-start | bytes 24584 | tf_op jit(solution)/shard_map/ppermute | solution.py:50
  430.3 17.3 %collective-permute-start.86 = (f32[4,512]{1,0:T(4,128)S(1)}, f32[4,512]{1,0:T(4,128)S(1)}, u32[]{:S(2)}, u32[]{:S(2)}) collective-permute-start(f32[4,512]{1,0:T(4,128)S(1)} %add_add_fusion.13), channel_id=1, source_target_pairs={{0,8},{1,9},{2,10},{3,11},{4,12},{5,13},{6,14},{7,15},{8,0},{9,1},... | collective-permute-start | bytes 24584 | tf_op jit(solution)/shard_map/ppermute | solution.py:50
  432.4 15.2 %collective-permute-start.87 = (f32[4,512]{1,0:T(4,128)S(1)}, f32[4,512]{1,0:T(4,128)S(1)}, u32[]{:S(2)}, u32[]{:S(2)}) collective-permute-start(f32[4,512]{1,0:T(4,128)S(1)} %add_add_fusion.13), channel_id=1, source_target_pairs={{0,12},{1,13},{2,14},{3,15},{4,8},{5,9},{6,10},{7,11},{8,4},{9,5},... | collective-permute-start | bytes 24584 | tf_op jit(solution)/shard_map/ppermute | solution.py:50
  434.1 22.2 %collective-permute-start.89 = (bf16[2,2,2,112,512]{4,3,0,1,2:T(8,128)(2,1)}, bf16[2,2,2,112,512]{4,3,0,1,2:T(8,128)(2,1)}, u32[]{:S(2)}, u32[]{:S(2)}) collective-permute-start(bf16[2,2,2,112,512]{4,3,0,1,2:T(8,128)(2,1)} %dynamic-slice_bitcast_fusion.6), channel_id=1, source_target_pairs={{0,2},{1,3},{2,0},{3,1},{4,6},{5,7},{6,4},{7,5},{8,10},{9,11},{10,... | collective-permute-start | bytes 2752520 | tf_op jit(solution)/shard_map/ppermute | solution.py:50
  467.5 17.7 %collective-permute-start.99 = (bf16[2,2,96,512]{3,2,1,0:T(8,128)(2,1)S(1)}, bf16[2,2,96,512]{3,2,1,0:T(8,128)(2,1)S(1)}, u32[]{:S(2)}, u32[]{:S(2)}) collective-permute-start(bf16[2,2,96,512]{3,2,1,0:T(8,128)(2,1)S(1)} %dynamic-slice_bitcast_fusion.13), channel_id=1, source_target_pairs={{0,2},{1,3},{2,0},{3,1},{4,6},{5,7},{6,4},{7,5},{8,10},{9,11},{10,... | collective-permute-start | bytes 1179656 | tf_op jit(solution)/shard_map/ppermute | solution.py:50
  474.4 12.5 %collective-permute-start.98 = (bf16[2,2,112,512]{3,2,0,1:T(8,128)(2,1)S(1)}, bf16[2,2,112,512]{3,2,0,1:T(8,128)(2,1)S(1)}, u32[]{:S(2)}, u32[]{:S(2)}) collective-permute-start(bf16[2,2,112,512]{3,2,0,1:T(8,128)(2,1)S(1)} %dynamic-slice_bitcast_fusion.11), channel_id=1, source_target_pairs={{0,4},{1,5},{2,6},{3,7},{4,0},{5,1},{6,2},{7,3},{8,12},{9,13},{10,... | collective-permute-start | bytes 1376264 | tf_op jit(solution)/shard_map/ppermute | solution.py:50
  491.7 18.2 %collective-permute-start.108 = (bf16[2,96,512]{2,1,0:T(8,128)(2,1)S(1)}, bf16[2,96,512]{2,1,0:T(8,128)(2,1)S(1)}, u32[]{:S(2)}, u32[]{:S(2)}) collective-permute-start(bf16[2,96,512]{2,1,0:T(8,128)(2,1)S(1)} %dynamic-slice_bitcast_fusion.20), channel_id=1, source_target_pairs={{0,8},{1,9},{2,10},{3,11},{4,12},{5,13},{6,14},{7,15},{8,0},{9,1},... | collective-permute-start | bytes 589832 | tf_op jit(solution)/shard_map/ppermute | solution.py:50
  493.3 16.7 %collective-permute-start.107 = (bf16[2,112,512]{2,1,0:T(8,128)(2,1)S(1)}, bf16[2,112,512]{2,1,0:T(8,128)(2,1)S(1)}, u32[]{:S(2)}, u32[]{:S(2)}) collective-permute-start(bf16[2,112,512]{2,1,0:T(8,128)(2,1)S(1)} %dynamic-slice_bitcast_fusion.18), channel_id=1, source_target_pairs={{0,8},{1,9},{2,10},{3,11},{4,12},{5,13},{6,14},{7,15},{8,0},{9,1},... | collective-permute-start | bytes 688136 | tf_op jit(solution)/shard_map/ppermute | solution.py:50
  516.8 16.7 %collective-permute-start.110 = (bf16[2,2,2,2,128,512]{5,4,3,2,1,0:T(8,128)(2,1)}, bf16[2,2,2,2,128,512]{5,4,3,2,1,0:T(8,128)(2,1)}, u32[]{:S(2)}, u32[]{:S(2)}) collective-permute-start(bf16[2,2,2,2,128,512]{5,4,3,2,1,0:T(8,128)(2,1)} %dynamic-slice_bitcast_fusion.1), channel_id=1, source_target_pairs={{0,1},{1,0},{2,3},{3,2},{4,5},{5,4},{6,7},{7,6},{8,9},{9,8},{10,11... | collective-permute-start | bytes 6291464 | tf_op jit(solution)/shard_map/ppermute | solution.py:50
  519.5 16.2 %collective-permute-start.109 = (bf16[2,2,2,2,144,512]{5,4,3,2,1,0:T(8,128)(2,1)}, bf16[2,2,2,2,144,512]{5,4,3,2,1,0:T(8,128)(2,1)}, u32[]{:S(2)}, u32[]{:S(2)}) collective-permute-start(bf16[2,2,2,2,144,512]{5,4,3,2,1,0:T(8,128)(2,1)} %dynamic-slice_bitcast_fusion), channel_id=1, source_target_pairs={{0,1},{1,0},{2,3},{3,2},{4,5},{5,4},{6,7},{7,6},{8,9},{9,8},{10,11... | collective-permute-start | bytes 7077896 | tf_op jit(solution)/shard_map/ppermute | solution.py:50
  519.5 12.0 %collective-permute-start.112 = (bf16[96,512]{1,0:T(8,128)(2,1)S(1)}, bf16[96,512]{1,0:T(8,128)(2,1)S(1)}, u32[]{:S(2)}, u32[]{:S(2)}) collective-permute-start(bf16[96,512]{1,0:T(8,128)(2,1)S(1)} %dynamic-slice_bitcast_fusion.27), channel_id=1, source_target_pairs={{0,16},{1,17},{2,18},{3,19},{4,20},{5,21},{6,22},{7,23},{8,24},{9,... | collective-permute-start | bytes 294920 | tf_op jit(solution)/shard_map/ppermute | solution.py:50
  521.2 11.5 %collective-permute-start.111 = (bf16[112,512]{1,0:T(8,128)(2,1)S(1)}, bf16[112,512]{1,0:T(8,128)(2,1)S(1)}, u32[]{:S(2)}, u32[]{:S(2)}) collective-permute-start(bf16[112,512]{1,0:T(8,128)(2,1)S(1)} %dynamic-slice_bitcast_fusion.25), channel_id=1, source_target_pairs={{0,16},{1,17},{2,18},{3,19},{4,20},{5,21},{6,22},{7,23},{8,24},{9,... | collective-permute-start | bytes 344072 | tf_op jit(solution)/shard_map/ppermute | solution.py:50
  540.1 44.4 %collective-permute-start.120 = (bf16[2,2,2,128,512]{4,3,2,1,0:T(8,128)(2,1)}, bf16[2,2,2,128,512]{4,3,2,1,0:T(8,128)(2,1)}, u32[]{:S(2)}, u32[]{:S(2)}) collective-permute-start(bf16[2,2,2,128,512]{4,3,2,1,0:T(8,128)(2,1)} %dynamic-slice_bitcast_fusion.5), channel_id=1, source_target_pairs={{0,4},{1,5},{2,6},{3,7},{4,0},{5,1},{6,2},{7,3},{8,12},{9,13},{10,... | collective-permute-start | bytes 3145736 | tf_op jit(solution)/shard_map/ppermute | solution.py:50
  542.0 53.1 %collective-permute-start.119 = (bf16[2,2,2,144,512]{4,3,2,1,0:T(8,128)(2,1)}, bf16[2,2,2,144,512]{4,3,2,1,0:T(8,128)(2,1)}, u32[]{:S(2)}, u32[]{:S(2)}) collective-permute-start(bf16[2,2,2,144,512]{4,3,2,1,0:T(8,128)(2,1)} %dynamic-slice_bitcast_fusion.4), channel_id=1, source_target_pairs={{0,2},{1,3},{2,0},{3,1},{4,6},{5,7},{6,4},{7,5},{8,10},{9,11},{10,... | collective-permute-start | bytes 3538952 | tf_op jit(solution)/shard_map/ppermute | solution.py:50
  573.8 56.5 %collective-permute-start.113 = (bf16[2,176,512]{2,1,0:T(8,128)(2,1)}, bf16[2,176,512]{2,1,0:T(8,128)(2,1)}, u32[]{:S(2)}, u32[]{:S(2)}) collective-permute-start(bf16[2,176,512]{2,1,0:T(8,128)(2,1)} %get-tuple-element.153), channel_id=1, source_target_pairs={{0,4},{4,8},{8,12},{12,16},{16,20},{20,24},{24,28},{1,5},{5,9},{9,... | collective-permute-start | bytes 1081352 | tf_op jit(solution)/shard_map/ppermute | solution.py:147
  577.8 54.8 %collective-permute-start.114 = (bf16[2,176,512]{2,1,0:T(8,128)(2,1)}, bf16[2,176,512]{2,1,0:T(8,128)(2,1)}, u32[]{:S(2)}, u32[]{:S(2)}) collective-permute-start(bf16[2,176,512]{2,1,0:T(8,128)(2,1)} %get-tuple-element.154), channel_id=1, source_target_pairs={{4,0},{8,4},{12,8},{16,12},{20,16},{24,20},{28,24},{5,1},{9,5},{13... | collective-permute-start | bytes 1081352 | tf_op jit(solution)/shard_map/ppermute | solution.py:147
  579.1 56.5 %collective-permute-start.115 = (bf16[2,176,512]{2,1,0:T(8,128)(2,1)}, bf16[2,176,512]{2,1,0:T(8,128)(2,1)}, u32[]{:S(2)}, u32[]{:S(2)}) collective-permute-start(bf16[2,176,512]{2,1,0:T(8,128)(2,1)} %get-tuple-element.155), channel_id=1, source_target_pairs={{0,8},{4,12},{8,16},{12,20},{16,24},{20,28},{1,9},{5,13},{9,17},{1... | collective-permute-start | bytes 1081352 | tf_op jit(solution)/shard_map/ppermute | solution.py:147
  584.5 9.3 %collective-permute-start.117 = (bf16[2,88,512]{2,1,0:T(8,128)(2,1)S(1)}, bf16[2,88,512]{2,1,0:T(8,128)(2,1)S(1)}, u32[]{:S(2)}, u32[]{:S(2)}) collective-permute-start(bf16[2,88,512]{2,1,0:T(8,128)(2,1)S(1)} %get-tuple-element.157), channel_id=1, source_target_pairs={{0,12},{4,16},{8,20},{12,24},{16,28},{1,13},{5,17},{9,21},{13,25},... | collective-permute-start | bytes 540680 | tf_op jit(solution)/shard_map/ppermute | solution.py:147
  593.9 46.9 %collective-permute-start.116 = (bf16[2,176,512]{2,1,0:T(8,128)(2,1)S(1)}, bf16[2,176,512]{2,1,0:T(8,128)(2,1)}, u32[]{:S(2)}, u32[]{:S(2)}) collective-permute-start(bf16[2,176,512]{2,1,0:T(8,128)(2,1)S(1)} %get-tuple-element.156), channel_id=1, source_target_pairs={{8,0},{12,4},{16,8},{20,12},{24,16},{28,20},{9,1},{13,5},{17,9},{2... | collective-permute-start | bytes 1081352 | tf_op jit(solution)/shard_map/ppermute | solution.py:147
  595.2 21.8 %collective-permute-start.118 = (bf16[2,88,512]{2,1,0:T(8,128)(2,1)S(1)}, bf16[2,88,512]{2,1,0:T(8,128)(2,1)S(1)}, u32[]{:S(2)}, u32[]{:S(2)}) collective-permute-start(bf16[2,88,512]{2,1,0:T(8,128)(2,1)S(1)} %get-tuple-element.158), channel_id=1, source_target_pairs={{12,0},{16,4},{20,8},{24,12},{28,16},{13,1},{17,5},{21,9},{25,13},... | collective-permute-start | bytes 540680 | tf_op jit(solution)/shard_map/ppermute | solution.py:147
  616.9 33.4 %collective-permute-start.125 = (bf16[2,88,512]{2,1,0:T(8,128)(2,1)}, bf16[2,88,512]{2,1,0:T(8,128)(2,1)}, u32[]{:S(2)}, u32[]{:S(2)}) collective-permute-start(bf16[2,88,512]{2,1,0:T(8,128)(2,1)} %get-tuple-element.167), channel_id=1, source_target_pairs={{0,12},{4,16},{8,20},{12,24},{16,28},{1,13},{5,17},{9,21},{13,25},... | collective-permute-start | bytes 540680 | tf_op jit(solution)/shard_map/ppermute | solution.py:147
  630.3 11.8 %collective-permute-start.138 = (bf16[32,352]{1,0:T(8,128)(2,1)}, bf16[32,352]{1,0:T(8,128)(2,1)S(1)}, u32[]{:S(2)}, u32[]{:S(2)}) collective-permute-start(bf16[32,352]{1,0:T(8,128)(2,1)} %get-tuple-element.178), channel_id=1, source_target_pairs={{0,4},{4,8},{8,12},{12,16},{16,20},{20,24},{24,28},{1,5},{5,9},{9,... | collective-permute-start | bytes 67592 | tf_op jit(solution)/shard_map/ppermute | solution.py:147
  632.6 16.4 %collective-permute-start.139 = (bf16[32,352]{1,0:T(8,128)(2,1)}, bf16[32,352]{1,0:T(8,128)(2,1)S(1)}, u32[]{:S(2)}, u32[]{:S(2)}) collective-permute-start(bf16[32,352]{1,0:T(8,128)(2,1)} %get-tuple-element.179), channel_id=1, source_target_pairs={{4,0},{8,4},{12,8},{16,12},{20,16},{24,20},{28,24},{5,1},{9,5},{13... | collective-permute-start | bytes 67592 | tf_op jit(solution)/shard_map/ppermute | solution.py:147
  635.6 29.1 %collective-permute-start.121 = (bf16[2,176,512]{2,1,0:T(8,128)(2,1)}, bf16[2,176,512]{2,1,0:T(8,128)(2,1)S(1)}, u32[]{:S(2)}, u32[]{:S(2)}) collective-permute-start(bf16[2,176,512]{2,1,0:T(8,128)(2,1)} %copy-done.24), channel_id=1, source_target_pairs={{0,4},{4,8},{8,12},{12,16},{16,20},{20,24},{24,28},{1,5},{5,9},{9,... | collective-permute-start | bytes 1081352 | tf_op jit(solution)/shard_map/ppermute | solution.py:147
  640.8 32.3 %collective-permute-start.122 = (bf16[2,176,512]{2,1,0:T(8,128)(2,1)}, bf16[2,176,512]{2,1,0:T(8,128)(2,1)S(1)}, u32[]{:S(2)}, u32[]{:S(2)}) collective-permute-start(bf16[2,176,512]{2,1,0:T(8,128)(2,1)} %get-tuple-element.164), channel_id=1, source_target_pairs={{4,0},{8,4},{12,8},{16,12},{20,16},{24,20},{28,24},{5,1},{9,5},{13... | collective-permute-start | bytes 1081352 | tf_op jit(solution)/shard_map/ppermute | solution.py:147
  642.1 31.0 %collective-permute-start.123 = (bf16[2,176,512]{2,1,0:T(8,128)(2,1)}, bf16[2,176,512]{2,1,0:T(8,128)(2,1)S(1)}, u32[]{:S(2)}, u32[]{:S(2)}) collective-permute-start(bf16[2,176,512]{2,1,0:T(8,128)(2,1)} %get-tuple-element.165), channel_id=1, source_target_pairs={{0,8},{4,12},{8,16},{12,20},{16,24},{20,28},{1,9},{5,13},{9,17},{1... | collective-permute-start | bytes 1081352 | tf_op jit(solution)/shard_map/ppermute | solution.py:147
  649.0 24.1 %collective-permute-start.124 = (bf16[2,176,512]{2,1,0:T(8,128)(2,1)}, bf16[2,176,512]{2,1,0:T(8,128)(2,1)S(1)}, u32[]{:S(2)}, u32[]{:S(2)}) collective-permute-start(bf16[2,176,512]{2,1,0:T(8,128)(2,1)} %get-tuple-element.166), channel_id=1, source_target_pairs={{8,0},{12,4},{16,8},{20,12},{24,16},{28,20},{9,1},{13,5},{17,9},{2... | collective-permute-start | bytes 1081352 | tf_op jit(solution)/shard_map/ppermute | solution.py:147
  650.3 11.8 %collective-permute-start.126 = (bf16[2,88,512]{2,1,0:T(8,128)(2,1)S(1)}, bf16[2,88,512]{2,1,0:T(8,128)(2,1)S(1)}, u32[]{:S(2)}, u32[]{:S(2)}) collective-permute-start(bf16[2,88,512]{2,1,0:T(8,128)(2,1)S(1)} %get-tuple-element.168), channel_id=1, source_target_pairs={{12,0},{16,4},{20,8},{24,12},{28,16},{13,1},{17,5},{21,9},{25,13},... | collective-permute-start | bytes 540680 | tf_op jit(solution)/shard_map/ppermute | solution.py:147
  662.2 12.4 %collective-permute-start.128 = (bf16[2,2,128,512]{3,2,1,0:T(8,128)(2,1)S(1)}, bf16[2,2,128,512]{3,2,1,0:T(8,128)(2,1)S(1)}, u32[]{:S(2)}, u32[]{:S(2)}) collective-permute-start(bf16[2,2,128,512]{3,2,1,0:T(8,128)(2,1)S(1)} %dynamic-slice_bitcast_fusion.10), channel_id=1, source_target_pairs={{0,2},{1,3},{2,0},{3,1},{4,6},{5,7},{6,4},{7,5},{8,10},{9,11},{10,... | collective-permute-start | bytes 1572872 | tf_op jit(solution)/shard_map/ppermute | solution.py:50
  664.7 19.1 %collective-permute-start.127 = (bf16[2,2,144,512]{3,2,1,0:T(8,128)(2,1)S(1)}, bf16[2,2,144,512]{3,2,1,0:T(8,128)(2,1)S(1)}, u32[]{:S(2)}, u32[]{:S(2)}) collective-permute-start(bf16[2,2,144,512]{3,2,1,0:T(8,128)(2,1)S(1)} %dynamic-slice_bitcast_fusion.8), channel_id=1, source_target_pairs={{0,4},{1,5},{2,6},{3,7},{4,0},{5,1},{6,2},{7,3},{8,12},{9,13},{10,... | collective-permute-start | bytes 1769480 | tf_op jit(solution)/shard_map/ppermute | solution.py:50
  691.2 14.6 %collective-permute-start.140 = (bf16[2,2,2,2,48,512]{5,4,3,2,1,0:T(8,128)(2,1)}, bf16[2,2,2,2,48,512]{5,4,3,2,1,0:T(8,128)(2,1)}, u32[]{:S(2)}, u32[]{:S(2)}) collective-permute-start(bf16[2,2,2,2,48,512]{5,4,3,2,1,0:T(8,128)(2,1)} %bitcast.443), channel_id=1, source_target_pairs={{0,1},{1,0},{2,3},{3,2},{4,5},{5,4},{6,7},{7,6},{8,9},{9,8},{10,11... | collective-permute-start | bytes 2359304 | tf_op jit(solution)/shard_map/ppermute | solution.py:50
  695.9 11.6 %collective-permute-start.137 = (bf16[2,128,512]{2,1,0:T(8,128)(2,1)}, bf16[2,128,512]{2,1,0:T(8,128)(2,1)}, u32[]{:S(2)}, u32[]{:S(2)}) collective-permute-start(bf16[2,128,512]{2,1,0:T(8,128)(2,1)} %dynamic-slice_bitcast_fusion.17), channel_id=1, source_target_pairs={{0,8},{1,9},{2,10},{3,11},{4,12},{5,13},{6,14},{7,15},{8,0},{9,1},... | collective-permute-start | bytes 786440 | tf_op jit(solution)/shard_map/ppermute | solution.py:50
  698.7 11.6 %collective-permute-start.136 = (bf16[2,144,512]{2,1,0:T(8,128)(2,1)}, bf16[2,144,512]{2,1,0:T(8,128)(2,1)}, u32[]{:S(2)}, u32[]{:S(2)}) collective-permute-start(bf16[2,144,512]{2,1,0:T(8,128)(2,1)} %dynamic-slice_bitcast_fusion.14), channel_id=1, source_target_pairs={{0,8},{1,9},{2,10},{3,11},{4,12},{5,13},{6,14},{7,15},{8,0},{9,1},... | collective-permute-start | bytes 884744 | tf_op jit(solution)/shard_map/ppermute | solution.py:50
  711.4 11.3 %collective-permute-start.156 = (bf16[128,512]{1,0:T(8,128)(2,1)S(1)}, bf16[128,512]{1,0:T(8,128)(2,1)S(1)}, u32[]{:S(2)}, u32[]{:S(2)}) collective-permute-start(bf16[128,512]{1,0:T(8,128)(2,1)S(1)} %dynamic-slice_bitcast_fusion.22), channel_id=1, source_target_pairs={{0,16},{1,17},{2,18},{3,19},{4,20},{5,21},{6,22},{7,23},{8,24},{9,... | collective-permute-start | bytes 393224 | tf_op jit(solution)/shard_map/ppermute | solution.py:50
  713.1 12.2 %collective-permute-start.155 = (bf16[144,512]{1,0:T(8,128)(2,1)S(1)}, bf16[144,512]{1,0:T(8,128)(2,1)S(1)}, u32[]{:S(2)}, u32[]{:S(2)}) collective-permute-start(bf16[144,512]{1,0:T(8,128)(2,1)S(1)} %dynamic-slice_bitcast_fusion.21), channel_id=1, source_target_pairs={{0,16},{1,17},{2,18},{3,19},{4,20},{5,21},{6,22},{7,23},{8,24},{9,... | collective-permute-start | bytes 442376 | tf_op jit(solution)/shard_map/ppermute | solution.py:50
  714.5 11.6 %collective-permute-start.151 = (bf16[2,2,2,48,512]{4,3,2,1,0:T(8,128)(2,1)S(1)}, bf16[2,2,2,48,512]{4,3,2,1,0:T(8,128)(2,1)S(1)}, u32[]{:S(2)}, u32[]{:S(2)}) collective-permute-start(bf16[2,2,2,48,512]{4,3,2,1,0:T(8,128)(2,1)S(1)} %dynamic-slice_bitcast_fusion.12), channel_id=1, source_target_pairs={{0,4},{1,5},{2,6},{3,7},{4,0},{5,1},{6,2},{7,3},{8,12},{9,13},{10,... | collective-permute-start | bytes 1179656 | tf_op jit(solution)/shard_map/ppermute | solution.py:50
  718.5 9.0 %collective-permute-start.142 = (bf16[2,2,2,2,32,512]{5,4,3,2,1,0:T(8,128)(2,1)S(1)}, bf16[2,2,2,2,32,512]{5,4,3,2,1,0:T(8,128)(2,1)S(1)}, u32[]{:S(2)}, u32[]{:S(2)}) collective-permute-start(bf16[2,2,2,2,32,512]{5,4,3,2,1,0:T(8,128)(2,1)S(1)} %bitcast.522), channel_id=1, source_target_pairs={{0,1},{1,0},{2,3},{3,2},{4,5},{5,4},{6,7},{7,6},{8,9},{9,8},{10,11... | collective-permute-start | bytes 1572872 | tf_op jit(solution)/shard_map/ppermute | solution.py:50
  718.6 8.7 %collective-permute-start.141 = (bf16[2,2,2,2,32,512]{5,4,0,1,2,3:T(8,128)(2,1)S(1)}, bf16[2,2,2,2,32,512]{5,4,0,1,2,3:T(8,128)(2,1)S(1)}, u32[]{:S(2)}, u32[]{:S(2)}) collective-permute-start(bf16[2,2,2,2,32,512]{5,4,0,1,2,3:T(8,128)(2,1)S(1)} %dynamic-slice_bitcast_fusion.9), channel_id=1, source_target_pairs={{0,1},{1,0},{2,3},{3,2},{4,5},{5,4},{6,7},{7,6},{8,9},{9,8},{10,11... | collective-permute-start | bytes 1572872 | tf_op jit(solution)/shard_map/ppermute | solution.py:50
  727.7 16.6 %collective-permute-start.144 = (bf16[2,2,2,32,512]{4,3,2,1,0:T(8,128)(2,1)S(1)}, bf16[2,2,2,32,512]{4,3,2,1,0:T(8,128)(2,1)S(1)}, u32[]{:S(2)}, u32[]{:S(2)}) collective-permute-start(bf16[2,2,2,32,512]{4,3,2,1,0:T(8,128)(2,1)S(1)} %dynamic-slice_bitcast_fusion.15), channel_id=1, source_target_pairs={{0,4},{1,5},{2,6},{3,7},{4,0},{5,1},{6,2},{7,3},{8,12},{9,13},{10,... | collective-permute-start | bytes 786440 | tf_op jit(solution)/shard_map/ppermute | solution.py:50
  729.5 14.9 %collective-permute-start.143 = (bf16[2,2,2,32,512]{4,3,0,1,2:T(8,128)(2,1)S(1)}, bf16[2,2,2,32,512]{4,3,0,1,2:T(8,128)(2,1)S(1)}, u32[]{:S(2)}, u32[]{:S(2)}) collective-permute-start(bf16[2,2,2,32,512]{4,3,0,1,2:T(8,128)(2,1)S(1)} %dynamic-slice_bitcast_fusion.16), channel_id=1, source_target_pairs={{0,2},{1,3},{2,0},{3,1},{4,6},{5,7},{6,4},{7,5},{8,10},{9,11},{10,... | collective-permute-start | bytes 786440 | tf_op jit(solution)/shard_map/ppermute | solution.py:50
  744.5 18.1 %collective-permute-start.145 = (bf16[2,2,32,512]{3,2,0,1:T(8,128)(2,1)S(1)}, bf16[2,2,32,512]{3,2,0,1:T(8,128)(2,1)S(1)}, u32[]{:S(2)}, u32[]{:S(2)}) collective-permute-start(bf16[2,2,32,512]{3,2,0,1:T(8,128)(2,1)S(1)} %dynamic-slice_bitcast_fusion.24), channel_id=1, source_target_pairs={{0,4},{1,5},{2,6},{3,7},{4,0},{5,1},{6,2},{7,3},{8,12},{9,13},{10,... | collective-permute-start | bytes 393224 | tf_op jit(solution)/shard_map/ppermute | solution.py:50
  746.7 16.8 %collective-permute-start.148 = (bf16[2,2,32,512]{3,2,1,0:T(8,128)(2,1)S(1)}, bf16[2,2,32,512]{3,2,1,0:T(8,128)(2,1)S(1)}, u32[]{:S(2)}, u32[]{:S(2)}) collective-permute-start(bf16[2,2,32,512]{3,2,1,0:T(8,128)(2,1)S(1)} %dynamic-slice_bitcast_fusion.23), channel_id=1, source_target_pairs={{0,2},{1,3},{2,0},{3,1},{4,6},{5,7},{6,4},{7,5},{8,10},{9,11},{10,... | collective-permute-start | bytes 393224 | tf_op jit(solution)/shard_map/ppermute | solution.py:50
  (260 other events, 1940.4 us)
Sparse Core Ops, SparseCore 0:
  11.9 82.9 all-gather.4
  155.0 94.9 all-gather.6

commit v3 on v2

--- a/solution.py
+++ b/solution.py
@@ -99,6 +99,19 @@
         while self.order:
             self.step()
         return self.value
+
+
+def scatter_chips(scatter):
+    count = device_count()
+    groups = [[i for i in range(count) if i % 2 == side] for side in range(2)]
+    value = scatter.value
+    return lax.psum_scatter(
+        value.reshape(-1, value.shape[-1]),
+        BOTH,
+        scatter_dimension=0,
+        axis_index_groups=groups,
+        tiled=True,
+    ).astype(f32)
 
 
 class Gather:
@@ -829,14 +842,13 @@
 
     mid_part = mid // count
     wide_part = wide // count
-    vector_rows = [mid_gain_one, mid_bias_one, mid_gain_two, mid_bias_two] + [
-        vector[None] for vector in (wide_gain_one, wide_bias_one, wide_gain_two, wide_bias_two)
-    ]
     extent = max(mid_part, wide_part)
-    vectors = jnp.concatenate(
-        [jnp.pad(rows, ((0, 0), (0, extent - rows.shape[1]))) for rows in vector_rows]
-        + [jnp.zeros((4, extent), bf16)],
-        axis=0,
+    mid_rows = jnp.concatenate([mid_gain_one, mid_bias_one, mid_gain_two, mid_bias_two], axis=0)
+    wide_rows = jnp.concatenate(
+        [v[None] for v in (wide_gain_one, wide_bias_one, wide_gain_two, wide_bias_two)], axis=0
+    )
+    vectors = jnp.pad(mid_rows, ((0, 8), (0, extent - mid_part))) + jnp.pad(
+        wide_rows, ((8, 4), (0, extent - wide_part))
     )
     offset_rows = offset_one.shape[0]
     small = offset_stack(offset_one.T, vectors, mid)
@@ -889,11 +901,11 @@
         from_behind(hidden[:, :half], -3),
         from_behind(hidden[:, half:], 3),
     ]
-    positions, reduce_two_, flat_out_grad, *pieces = meet(
-        positions, reduce_two, flat_out_grad, *pieces
+    positions, flat_out_grad, reduce_two, spatial_two, expand_two, *pieces = meet(
+        positions, flat_out_grad, reduce_two, spatial_two, expand_two, *pieces
     )
     reduce_two_all, spatial_all, expand_two_all = gather(
-        [reduce_two_, spatial_two, stacked_columns(expand_two, mid)]
+        [reduce_two, spatial_two, stacked_columns(expand_two, mid)]
     )
     weight_reduce_two = reduce_two_all.reshape(wide, mid)
     weight_spatial_two = spatial_all.reshape(9 * mid, mid)
@@ -945,12 +957,7 @@
         return results
 
     column_rows = expand_two.shape[0] * wide // mid
-    spatial_chunks = chunked(grad_spatial_two)
-    cut = spatial_two.shape[0] * 7 // 9
-    two_left = Scatter([spatial_chunks[:, :cut]], (1, 2, 4, 8, 16))
-    two_right = Scatter(
-        [spatial_chunks[:, cut:]] + chunked_columns(grad_expand_two), (1, 4, 2, 8, 16)
-    )
+    two_sum = Scatter([chunked(grad_spatial_two)] + chunked_columns(grad_expand_two), (1, 16, 8, 4, 2))
 
     def beside_steps(value, *scatters):
         for scatter in scatters:
@@ -960,7 +967,8 @@
             scatter.value = total
         return value
 
-    back_fifth = beside_steps(back_fifth, two_left, two_right)
+    back_fifth = beside_steps(back_fifth, two_sum)
+    two_shard = scatter_chips(two_sum)
     back_maps = maps(back_fifth)
     back_inner = conv_back(
         from_behind(back_maps[:, STRIP - COLS :], 1),
@@ -969,18 +977,15 @@
         weight_spatial_two,
     ).reshape(pixels, mid)
     back_fourth = norm_b1.backward(per_batch(back_inner) * silu_slope(norm_b1.forward()))
-    back_fourth = beside_steps(back_fourth, two_left, two_right)
     grad_reduce_two = dot_tn(middle, back_fourth).astype(bf16)
 
     back_middle = masked_six + per_batch(dot_nt(back_fourth, weight_reduce_two))
     masked_three = back_middle * silu_slope(joined_one)
     back_third = norm_a3.backward(masked_three)
-    back_third = beside_steps(back_third, two_left, two_right)
     grad_expand_one = dot_tn(hidden_two, back_third).astype(bf16)
     back_second = norm_a2.backward(
         per_batch(dot_nt(back_third, weight_expand_one)) * silu_slope(norm_a2.forward())
     )
-    back_second = beside_steps(back_second, two_left, two_right)
     grad_deform_one = dot_tn(sampled, back_second).astype(bf16)
     one_left = Scatter([chunked(grad_deform_one)], (1, 2, 4, 8, 16))
     one_right = Scatter(
@@ -990,7 +995,7 @@
         back_second, one_left.value, one_right.value
     )
     back_sampled = dot_nt(back_second, weight_deform_one).astype(bf16).reshape(images, STRIP, -1)
-    back_sampled = beside_steps(back_sampled, one_left, one_right, two_left, two_right)
+    back_sampled = beside_steps(back_sampled, one_left, one_right)
 
     def returned(upstream, first):
         own, *others, position_grad = sample_back(
@@ -1009,9 +1014,9 @@
 
     backs = [returned(back_sampled, 0)]
     back_sampled = beside_steps(back_sampled, one_left, one_right)
+    back_sampled, two_shard = meet(back_sampled, two_shard)
     backs.append(returned(back_sampled, images // MB))
     own = jnp.concatenate([pair[0] for pair in backs], axis=0)
-    own = beside_steps(own, one_left, one_right)
     position_grad = jnp.concatenate([pair[1] for pair in backs], axis=0)
     back_offsets, last_rim, first_rim = offset_slope(position_grad, squashed)
     stacked, offset_chunks = offset_back(
@@ -1048,10 +1053,7 @@
     expand_shard, reduce_two_shard = split_rows(
         one_right.finish(), [column_rows, reduce_two.shape[0]]
     )
-    two_rest, expand_two_shard = split_rows(
-        two_right.finish(), [spatial_two.shape[0] - cut, column_rows]
-    )
-    spatial_shard = jnp.concatenate([two_left.finish(), two_rest], axis=0)
+    spatial_shard, expand_two_shard = split_rows(two_shard, [spatial_two.shape[0], column_rows])
 
     me = lax.axis_index(BOTH)
     mid_grads = jnp.stack(

time: 793 us -> 765 us (0.965)
  starting transfers between devices: 238 us -> 217 us
  other arithmetic: 86.1 us -> 76.5 us
    ppermute x131 -> x122, starting transfers between devices: 160 us -> 140 us  [exchange(): lax.ppermute(value, BOTH, [(i, i ^ mask) for i in range(device_count())])]
    convert_element_type x28 -> x21, other arithmetic: 27.5 us -> 21.1 us  [step(): self.value = total.astype(bf16) if self.order else total]
    unnamed x351 -> x305, local copies, waits for them, and re-layouts: 54.5 us -> 55.2 us
    ppermute x131 -> x122, waiting for transfers between devices: 152 us -> 152 us  [exchange(): lax.ppermute(value, BOTH, [(i, i ^ mask) for i in range(device_count())])]
  transfers between devices with their start and end apart: 159 -> 151, of which waited for: 86 -> 92; matrix products, arithmetic and copies ran while one was open for 22% -> 23% of each run, Pallas kernels for 7% -> 7%
where the time goes in v3:
time: 765 us; the launch traced here: 755 us
  starting transfers between devices  217 us (28%)
  waiting for transfers between devices  199 us (26%)
  local copies, waits for them, and re-layouts  107 us (14%)
  other arithmetic  76.5 us (10%)
  matrix products  73.7 us (10%)
  Pallas kernels  64.4 us (8%)
  between operations  17.2 us (2%)
    ppermute x122, waiting for transfers between devices, exchange(): lax.ppermute(value, BOTH, [(i, i ^ mask) for i in range(device_count())])  152 us
    ppermute x122, starting transfers between devices, exchange(): lax.ppermute(value, BOTH, [(i, i ^ mask) for i in range(device_count())])  140 us
    ppermute x26, starting transfers between devices, from_behind(): lax.ppermute(value, 'rows', [(source, source + steps) for source in range...  77.2 us
    unnamed x305, local copies, waits for them, and re-layouts  55.2 us
    ppermute x26, waiting for transfers between devices, from_behind(): lax.ppermute(value, 'rows', [(source, source + steps) for source in range...  42.3 us
    pallas_call x2, Pallas kernels, sample_back(): pl.pallas_call(sample_back_kernel, grid=(images,), in_specs=sampler_specs...  31.4 us
    dot_general x7, matrix products, dot_tn(): lax.dot_general(left, right, (((0,), (0,)), ((), ())), preferred_element_...  28 us
    dot_general x5, matrix products, dot_nt(): lax.dot_general(left, right, (((1,), (1,)), ((), ())), preferred_element_...  26 us
  transfers between devices with their start and end apart: 151, of which 92 were waited for; matrix products, arithmetic and copies ran while one was open for 23% of the time, Pallas kernels for 7%

profile of v3, /device:TPU:0, one launch (start us, length us, event | category | flops | bytes accessed | tf_op | source)
XLA Modules:
  0.0 754.8 jit_solution(2511534548089853863)
XLA Ops:
  23.6 3.9 collective-permute-done.4
  28.3 4.5 collective-permute-done.1
  36.0 3.3 collective-permute-done.7
  44.2 3.3 copy.74
  50.3 4.5 collective-permute-done.9
  57.0 4.4 collective-permute-done.8
  89.7 3.7 collective-permute-start.19
  105.0 5.4 collective-permute-start.22
  111.7 5.4 collective-permute-start.24
  117.1 5.6 collective-permute-start.26
  122.7 3.3 copy.77
  126.0 4.4 reshape.660
  132.9 7.2 collective-permute-done.26.refs_6_
  140.2 4.1 collective-permute-done.22.refs_2_
  150.8 17.6 %sample.1 = bf16[4,176,4608]{2,1,0:T(8,128)(2,1)} custom-call(f32[4,2,1664]{2,1,0:T(2,128)} %get-tuple-element.113.pos_ref, f32[24,1]{1,0:T(8,128)} %constant.444.row_ref, bf16[4,176,512]{2,1,0:T(8,128)(2,1)} %multiply_convert_fusion.10.refs_0_, bf16[4,176,512]{2,1,0:T(8,128)(2,1)} %collective-permute-done.21.refs_1_, ...), custom_call_target="tpu_custom_call" | custom-call | flops 1 | bytes 1 | tf_op jit(solution)/shard_map/sample/pallas_call | solution.py:330
  173.7 4.6 fusion.119
  183.9 6.6 collective-permute-start.30
  190.4 8.9 %collective-permute-start.31 = (f32[4,512]{1,0:T(4,128)S(1)}, f32[4,512]{1,0:T(4,128)S(1)}, u32[]{:S(2)}, u32[]{:S(2)}) collective-permute-start(f32[4,512]{1,0:T(4,128)S(1)} %add_add_fusion.21), channel_id=1, source_target_pairs={{0,8},{1,9},{2,10},{3,11},{4,12},{5,13},{6,14},{7,15},{8,0},{9,1},... | collective-permute-start | bytes 24584 | tf_op jit(solution)/shard_map/ppermute | solution.py:50
  209.8 5.4 fusion.112
  231.4 5.3 collective-permute-done.40
  237.3 5.1 multiply_convert_fusion.3
  242.5 4.4 all-gather.7.cloned.1.call-done
  264.8 3.4 collective-permute-done.47
  281.4 4.1 conv.1
  306.4 5.0 fusion.111
  327.9 8.7 %fusion.110 = (f32[2,2048]{1,0:T(2,128)S(1)}, f32[2,2048]{1,0:T(2,128)S(1)}, f32[2,352,2048]{2,1,0:T(8,128)S(1)}, bf16[2,352,2048]{2,1,0:T(8,128)(2,1)}) fusion(f32[2,2048]{1,0:T(2,128)S(1)} %get-tuple-element.349, f32[2,352,2048]{2,1,0:T(8,128)} %get-tuple-element.384, f32[2,2048]{1,0:T(2,128)S(1)} %get-tuple-element.350, ...), kind=kLoop, calls=%fused_computation.409 | loop fusion | flops 30269440 | bytes 20269824 | tf_op jit(solution)/shard_map/reduce_sum | solution.py:730
  349.9 3.9 collective-permute-done.70
  355.7 3.3 fusion.116
  366.9 4.2 bitcast_convert_fusion.2
  372.2 3.5 collective-permute-done.77
  376.8 7.4 convolution_convert_fusion.2
  388.7 6.4 collective-permute-done.78
  395.1 5.8 fusion
  404.5 3.1 collective-permute-done.79.above
  407.7 4.6 collective-permute-done.80.below
  414.6 4.0 conv_back.1
  437.8 8.4 %fusion.109 = (f32[2,2048]{1,0:T(2,128)S(1)}, f32[2,2048]{1,0:T(2,128)S(1)}, f32[2,352,2048]{2,1,0:T(8,128)}) fusion(f32[2,2048]{1,0:T(2,128)S(1)} %get-tuple-element.346, f32[2,352,2048]{2,1,0:T(8,128)S(1)} %bitcast.417, f32[2,2048]{1,0:T(2,128)S(1)} %get-tuple-element.347, bf16[2,352,2048]{2,1,0:T(8,128)(2,1)S(1)} %bitcast.394, ...), kind=kOutput, calls=%fused_computation.408 | convolution fusion | flops 1502339072 | bytes 23085056 | tf_op jit(solution)/shard_map/dot_general | solution.py:38
  459.6 4.0 bitcast_convert_fusion
  467.6 3.5 fusion.114
  488.4 4.2 convolution_convert_fusion.1
  497.4 9.1 %convolution_convert_fusion = bf16[704,4608]{1,0:T(8,128)(2,1)} fusion(bf16[704,512]{1,0:T(8,128)(2,1)} %bitcast.459, bf16[4608,512]{1,0:T(8,128)(2,1)} %bitcast.440), kind=kOutput, calls=%fused_computation | convolution fusion | flops 3325132800 | bytes 11927552 | tf_op jit(solution)/shard_map/dot_general | solution.py:38
  509.5 4.0 fusion.3
  519.1 4.5 reshape.673
  523.6 5.8 copy.89
  532.3 15.2 %sample_back.2 = (f32[2,176,512]{2,1,0:T(8,128)S(1)}, bf16[2,176,512]{2,1,0:T(8,128)(2,1)S(1)}, bf16[2,176,512]{2,1,0:T(8,128)(2,1)S(1)}, bf16[2,176,512]{2,1,0:...) custom-call(f32[4,2,1664]{2,1,0:T(2,128)S(1)} %copy-done.17, ...), custom_call_target="tpu_custom_call" | custom-call | flops 1 | bytes 1 | tf_op jit(solution)/shard_map/sample_back/pallas_call | solution.py:352
  547.6 3.3 collective-permute-start.104
  552.2 4.4 collective-permute-start.106
  556.6 4.4 collective-permute-start.108
  565.5 3.8 collective-permute-done.108
  573.3 3.8 collective-permute-start.125
  577.7 3.6 collective-permute-done.107
  587.9 16.2 %sample_back.3 = (f32[2,176,512]{2,1,0:T(8,128)S(1)}, bf16[2,176,512]{2,1,0:T(8,128)(2,1)}, bf16[2,176,512]{2,1,0:T(8,128)(2,1)}, bf16[2,176,512]{2,1,0:T(8,128)...) custom-call(f32[4,2,1664]{2,1,0:T(2,128)S(1)} %copy-done.17, ...), custom_call_target="tpu_custom_call" | custom-call | flops 1 | bytes 1 | tf_op jit(solution)/shard_map/sample_back/pallas_call | solution.py:352
  605.0 8.4 %collective-permute-start.112 = (bf16[2,176,512]{2,1,0:T(8,128)(2,1)}, bf16[2,176,512]{2,1,0:T(8,128)(2,1)S(1)}, u32[]{:S(2)}, u32[]{:S(2)}) collective-permute-start(bf16[2,176,512]{2,1,0:T(8,128)(2,1)} %get-tuple-element.145), channel_id=1, source_target_pairs={{0,4},{4,8},{8,12},{12,16},{16,20},{20,24},{24,28},{1,5},{5,9},{9,... | collective-permute-start | bytes 1081352 | tf_op jit(solution)/shard_map/ppermute | solution.py:160
  614.6 6.3 collective-permute-start.114
  622.3 6.0 collective-permute-start.116
  635.0 8.9 %collective-permute-done.117 = bf16[2,88,512]{2,1,0:T(8,128)(2,1)} collective-permute-done((bf16[2,88,512]{2,1,0:T(8,128)(2,1)S(1)}, bf16[2,88,512]{2,1,0:T(8,128)(2,1)}, u32[]{:S(2)}, u32[]{:S(2)}) %collective-permute-start.117) | collective-permute-done | bytes 180256 | tf_op jit(solution)/shard_map/ppermute | solution.py:160
  657.9 4.8 collective-permute-start.122
  681.4 3.4 collective-permute-done.146
  685.6 3.9 collective-permute-done.144
  691.9 5.4 collective-permute-done.147
  702.2 4.3 collective-permute-done.141
  711.5 4.4 fusion.2
  720.4 5.9 reshape.686
  726.3 9.0 %copy.90 = f32[4,4,44,2048]{3,1,2,0:T(4,128)} copy(f32[4,4,44,2048]{3,2,1,0:T(8,128)} %reshape.686) | data formatting | bytes 11534336
  (805 shorter events, 380.6 us)
Async XLA Ops:
  7.2 161.2 %all-gather.5.cloned.1.call-start = ((), (), s32[]{:S(2)}) async-start(), calls=%async_computation.2 | async-start | bytes 7028736 | tf_op jit(solution)/shard_map/all_gather | solution.py:775
  11.8 235.1 %all-gather.7.cloned.1.call-start = ((), (), s32[]{:S(2)}) async-start(), calls=%async_computation.3 | async-start | bytes 9191424 | tf_op jit(solution)/shard_map/all_gather | solution.py:775
  13.5 8.9 %collective-permute-start.5 = (bf16[48,512]{1,0:T(8,128)(2,1)S(1)}, bf16[48,512]{1,0:T(8,128)(2,1)S(1)}, u32[]{:S(2)}, u32[]{:S(2)}) collective-permute-start(bf16[48,512]{1,0:T(8,128)(2,1)S(1)} %pad_maximum_fusion.17), channel_id=1, source_target_pairs={{0,8},{1,9},{2,10},{3,11},{4,12},{5,13},{6,14},{7,15},{8,0},{9,1},... | collective-permute-start | bytes 147464 | tf_op jit(solution)/shard_map/ppermute | solution.py:50
  16.5 7.0 collective-permute-start.3
  19.0 8.4 %collective-permute-start.4 = (bf16[48,512]{1,0:T(8,128)(2,1)S(1)}, bf16[48,512]{1,0:T(8,128)(2,1)S(1)}, u32[]{:S(2)}, u32[]{:S(2)}) collective-permute-start(bf16[48,512]{1,0:T(8,128)(2,1)S(1)} %pad_maximum_fusion.17), channel_id=1, source_target_pairs={{0,16},{1,17},{2,18},{3,19},{4,20},{5,21},{6,22},{7,23},{8,24},{9,... | collective-permute-start | bytes 147464 | tf_op jit(solution)/shard_map/ppermute | solution.py:50
  19.1 9.1 %collective-permute-start = (bf16[64,512]{1,0:T(8,128)(2,1)}, bf16[64,512]{1,0:T(8,128)(2,1)S(1)}, u32[]{:S(2)}, u32[]{:S(2)}) collective-permute-start(bf16[64,512]{1,0:T(8,128)(2,1)} %param.30), channel_id=1, source_target_pairs={{0,24},{1,25},{2,26},{3,27},{4,28},{5,29},{6,30},{7,31},{8,16},{9,... | collective-permute-start | bytes 196616 | tf_op jit(solution)/shard_map/ppermute | solution.py:50
  22.1 10.7 %collective-permute-start.1 = (bf16[64,512]{1,0:T(8,128)(2,1)}, bf16[64,512]{1,0:T(8,128)(2,1)S(1)}, u32[]{:S(2)}, u32[]{:S(2)}) collective-permute-start(bf16[64,512]{1,0:T(8,128)(2,1)} %param.30), channel_id=1, source_target_pairs={{0,16},{1,17},{2,18},{3,19},{4,20},{5,21},{6,22},{7,23},{8,24},{9,... | collective-permute-start | bytes 196616 | tf_op jit(solution)/shard_map/ppermute | solution.py:50
  34.5 7.5 collective-permute-start.6
  42.0 12.8 %collective-permute-start.9 = (bf16[2,2,2,48,512]{4,3,1,0,2:T(8,128)(2,1)}, bf16[2,2,2,48,512]{4,3,1,0,2:T(8,128)(2,1)}, u32[]{:S(2)}, u32[]{:S(2)}) collective-permute-start(bf16[2,2,2,48,512]{4,3,1,0,2:T(8,128)(2,1)} %pad_maximum_fusion.6), channel_id=1, source_target_pairs={{0,4},{1,5},{2,6},{3,7},{4,0},{5,1},{6,2},{7,3},{8,12},{9,13},{10,... | collective-permute-start | bytes 1179656 | tf_op jit(solution)/shard_map/ppermute | solution.py:50
  43.6 17.8 %collective-permute-start.8 = (bf16[2,2,2,64,512]{4,3,2,1,0:T(8,128)(2,1)S(1)}, bf16[2,2,2,64,512]{4,3,2,1,0:T(8,128)(2,1)}, u32[]{:S(2)}, u32[]{:S(2)}) collective-permute-start(bf16[2,2,2,64,512]{4,3,2,1,0:T(8,128)(2,1)S(1)} %pad_maximum_fusion.5), channel_id=1, source_target_pairs={{0,2},{1,3},{2,0},{3,1},{4,6},{5,7},{6,4},{7,5},{8,10},{9,11},{10,... | collective-permute-start | bytes 1572872 | tf_op jit(solution)/shard_map/ppermute | solution.py:50
  81.7 13.1 %collective-permute-start.18 = (f32[4,512]{1,0:T(4,128)S(1)}, f32[4,512]{1,0:T(4,128)S(1)}, u32[]{:S(2)}, u32[]{:S(2)}) collective-permute-start(f32[4,512]{1,0:T(4,128)S(1)} %add_add_fusion.22), channel_id=1, source_target_pairs={{0,16},{1,17},{2,18},{3,19},{4,20},{5,21},{6,22},{7,23},{8,24},{9,... | collective-permute-start | bytes 24584 | tf_op jit(solution)/shard_map/ppermute | solution.py:50
  89.7 9.2 %collective-permute-start.19 = (f32[96,352]{1,0:T(8,128)S(1)}, f32[96,352]{1,0:T(8,128)S(1)}, u32[]{:S(2)}, u32[]{:S(2)}) collective-permute-start(f32[96,352]{1,0:T(8,128)S(1)} %get-tuple-element.107), channel_id=1, source_target_pairs={{0,4},{4,8},{8,12},{12,16},{16,20},{20,24},{24,28},{1,5},{5,9},{9,... | collective-permute-start | bytes 405512 | tf_op jit(solution)/shard_map/ppermute | solution.py:160
  93.4 7.0 collective-permute-start.20
  102.4 14.7 %collective-permute-start.25 = (bf16[4,88,512]{2,1,0:T(8,128)(2,1)S(1)}, bf16[4,88,512]{2,1,0:T(8,128)(2,1)S(1)}, u32[]{:S(2)}, u32[]{:S(2)}) collective-permute-start(bf16[4,88,512]{2,1,0:T(8,128)(2,1)S(1)} %get-tuple-element.316), channel_id=1, source_target_pairs={{12,0},{16,4},{20,8},{24,12},{28,16},{13,1},{17,5},{21,9},{25,13},... | collective-permute-start | bytes 1081352 | tf_op jit(solution)/shard_map/ppermute | solution.py:160
  103.7 36.5 %collective-permute-start.21 = (bf16[4,176,512]{2,1,0:T(8,128)(2,1)}, bf16[4,176,512]{2,1,0:T(8,128)(2,1)}, u32[]{:S(2)}, u32[]{:S(2)}) collective-permute-start(bf16[4,176,512]{2,1,0:T(8,128)(2,1)} %multiply_convert_fusion.10.refs_0_), channel_id=1, source_target_pairs={{4,0},{8,4},{12,8},{16,12},{20,16},{24,20},{28,24},{5,1},{9,5},{13... | collective-permute-start | bytes 2162696 | tf_op jit(solution)/shard_map/ppermute | solution.py:160
  105.0 39.3 %collective-permute-start.22 = (bf16[4,176,512]{2,1,0:T(8,128)(2,1)}, bf16[4,176,512]{2,1,0:T(8,128)(2,1)}, u32[]{:S(2)}, u32[]{:S(2)}) collective-permute-start(bf16[4,176,512]{2,1,0:T(8,128)(2,1)} %multiply_convert_fusion.10.refs_0_), channel_id=1, source_target_pairs={{0,4},{4,8},{8,12},{12,16},{16,20},{20,24},{24,28},{1,5},{5,9},{9,... | collective-permute-start | bytes 2162696 | tf_op jit(solution)/shard_map/ppermute | solution.py:160
  110.4 34.9 %collective-permute-start.23 = (bf16[4,176,512]{2,1,0:T(8,128)(2,1)}, bf16[4,176,512]{2,1,0:T(8,128)(2,1)}, u32[]{:S(2)}, u32[]{:S(2)}) collective-permute-start(bf16[4,176,512]{2,1,0:T(8,128)(2,1)} %multiply_convert_fusion.10.refs_0_), channel_id=1, source_target_pairs={{8,0},{12,4},{16,8},{20,12},{24,16},{28,20},{9,1},{13,5},{17,9},{2... | collective-permute-start | bytes 2162696 | tf_op jit(solution)/shard_map/ppermute | solution.py:160
  111.7 33.6 %collective-permute-start.24 = (bf16[4,176,512]{2,1,0:T(8,128)(2,1)}, bf16[4,176,512]{2,1,0:T(8,128)(2,1)}, u32[]{:S(2)}, u32[]{:S(2)}) collective-permute-start(bf16[4,176,512]{2,1,0:T(8,128)(2,1)} %multiply_convert_fusion.10.refs_0_), channel_id=1, source_target_pairs={{0,8},{4,12},{8,16},{12,20},{16,24},{20,28},{1,9},{5,13},{9,17},{1... | collective-permute-start | bytes 2162696 | tf_op jit(solution)/shard_map/ppermute | solution.py:160
  117.1 23.0 %collective-permute-start.26 = (bf16[4,88,512]{2,1,0:T(8,128)(2,1)}, bf16[4,88,512]{2,1,0:T(8,128)(2,1)}, u32[]{:S(2)}, u32[]{:S(2)}) collective-permute-start(bf16[4,88,512]{2,1,0:T(8,128)(2,1)} %get-tuple-element.315), channel_id=1, source_target_pairs={{0,12},{4,16},{8,20},{12,24},{16,28},{1,13},{5,17},{9,21},{13,25},... | collective-permute-start | bytes 1081352 | tf_op jit(solution)/shard_map/ppermute | solution.py:160
  150.7 432.6 %reduce-scatter.2.cloned.1.call-start = ((), (), s32[]{:S(2)}) async-start(), calls=%async_computation.1 | async-start | bytes 3620864 | tf_op jit(solution)/shard_map/reduce_scatter | solution.py:108
  183.9 17.1 %collective-permute-start.30 = (f32[4,512]{1,0:T(4,128)S(1)}, f32[4,512]{1,0:T(4,128)S(1)}, u32[]{:S(2)}, u32[]{:S(2)}) collective-permute-start(f32[4,512]{1,0:T(4,128)S(1)} %add_add_fusion.21), channel_id=1, source_target_pairs={{0,4},{1,5},{2,6},{3,7},{4,0},{5,1},{6,2},{7,3},{8,12},{9,13},{10,... | collective-permute-start | bytes 24584 | tf_op jit(solution)/shard_map/ppermute | solution.py:50
  190.4 10.6 %collective-permute-start.31 = (f32[4,512]{1,0:T(4,128)S(1)}, f32[4,512]{1,0:T(4,128)S(1)}, u32[]{:S(2)}, u32[]{:S(2)}) collective-permute-start(f32[4,512]{1,0:T(4,128)S(1)} %add_add_fusion.21), channel_id=1, source_target_pairs={{0,8},{1,9},{2,10},{3,11},{4,12},{5,13},{6,14},{7,15},{8,0},{9,1},... | collective-permute-start | bytes 24584 | tf_op jit(solution)/shard_map/ppermute | solution.py:50
  223.2 7.8 %collective-permute-start.39 = (f32[4,2048]{1,0:T(4,128)S(1)}, f32[4,2048]{1,0:T(4,128)S(1)}, u32[]{:S(2)}, u32[]{:S(2)}) collective-permute-start(f32[4,2048]{1,0:T(4,128)S(1)} %add_add_fusion.7), channel_id=1, source_target_pairs={{0,12},{1,13},{2,14},{3,15},{4,8},{5,9},{6,10},{7,11},{8,4},{9,5},... | collective-permute-start | bytes 98312 | tf_op jit(solution)/shard_map/ppermute | solution.py:50
  270.7 8.3 %collective-permute-start.48 = (bf16[4,44,512]{2,1,0:T(8,128)(2,1)S(1)}, bf16[4,44,512]{2,1,0:T(8,128)(2,1)S(1)}, u32[]{:S(2)}, u32[]{:S(2)}) collective-permute-start(bf16[4,44,512]{2,1,0:T(8,128)(2,1)S(1)} %get-tuple-element.314), channel_id=1, source_target_pairs={{0,4},{4,8},{8,12},{12,16},{16,20},{20,24},{24,28},{1,5},{5,9},{9,... | collective-permute-start | bytes 540680 | tf_op jit(solution)/shard_map/ppermute | solution.py:160
  273.8 7.6 %collective-permute-start.49 = (bf16[4,44,512]{2,1,0:T(8,128)(2,1)S(1)}, bf16[4,44,512]{2,1,0:T(8,128)(2,1)S(1)}, u32[]{:S(2)}, u32[]{:S(2)}) collective-permute-start(bf16[4,44,512]{2,1,0:T(8,128)(2,1)S(1)} %get-tuple-element.313), channel_id=1, source_target_pairs={{4,0},{8,4},{12,8},{16,12},{20,16},{24,20},{28,24},{5,1},{9,5},{13... | collective-permute-start | bytes 540680 | tf_op jit(solution)/shard_map/ppermute | solution.py:160
  363.3 7.7 %collective-permute-start.74 = (f32[4,512]{1,0:T(4,128)S(1)}, f32[4,512]{1,0:T(4,128)S(1)}, u32[]{:S(2)}, u32[]{:S(2)}) collective-permute-start(f32[4,512]{1,0:T(4,128)S(1)} %add_add_fusion.15), channel_id=1, source_target_pairs={{0,4},{1,5},{2,6},{3,7},{4,0},{5,1},{6,2},{7,3},{8,12},{9,13},{10,... | collective-permute-start | bytes 24584 | tf_op jit(solution)/shard_map/ppermute | solution.py:50
  363.8 7.3 collective-permute-start.75
  400.9 6.7 collective-permute-start.79
  403.2 9.0 %collective-permute-start.80 = (bf16[4,44,512]{2,1,0:T(8,128)(2,1)S(1)}, bf16[4,44,512]{2,1,0:T(8,128)(2,1)S(1)}, u32[]{:S(2)}, u32[]{:S(2)}) collective-permute-start(bf16[4,44,512]{2,1,0:T(8,128)(2,1)S(1)} %get-tuple-element.311), channel_id=1, source_target_pairs={{4,0},{8,4},{12,8},{16,12},{20,16},{24,20},{28,24},{5,1},{9,5},{13... | collective-permute-start | bytes 540680 | tf_op jit(solution)/shard_map/ppermute | solution.py:160
  494.7 11.8 %collective-permute-start.103 = (bf16[2,2,2,2,128,512]{5,4,3,2,1,0:T(8,128)(2,1)}, bf16[2,2,2,2,128,512]{5,4,3,2,1,0:T(8,128)(2,1)}, u32[]{:S(2)}, u32[]{:S(2)}) collective-permute-start(bf16[2,2,2,2,128,512]{5,4,3,2,1,0:T(8,128)(2,1)} %dynamic-slice_bitcast_fusion.2), channel_id=1, source_target_pairs={{0,1},{1,0},{2,3},{3,2},{4,5},{5,4},{6,7},{7,6},{8,9},{9,8},{10,11... | collective-permute-start | bytes 6291464 | tf_op jit(solution)/shard_map/ppermute | solution.py:50
  497.4 11.5 %collective-permute-start.102 = (bf16[2,2,2,2,144,512]{5,4,3,2,1,0:T(8,128)(2,1)}, bf16[2,2,2,2,144,512]{5,4,3,2,1,0:T(8,128)(2,1)}, u32[]{:S(2)}, u32[]{:S(2)}) collective-permute-start(bf16[2,2,2,2,144,512]{5,4,3,2,1,0:T(8,128)(2,1)} %dynamic-slice_bitcast_fusion.1), channel_id=1, source_target_pairs={{0,1},{1,0},{2,3},{3,2},{4,5},{5,4},{6,7},{7,6},{8,9},{9,8},{10,11... | collective-permute-start | bytes 7077896 | tf_op jit(solution)/shard_map/ppermute | solution.py:50
  514.6 42.0 %collective-permute-start.111 = (bf16[2,2,2,128,512]{4,3,2,1,0:T(8,128)(2,1)}, bf16[2,2,2,128,512]{4,3,2,1,0:T(8,128)(2,1)}, u32[]{:S(2)}, u32[]{:S(2)}) collective-permute-start(bf16[2,2,2,128,512]{4,3,2,1,0:T(8,128)(2,1)} %dynamic-slice_bitcast_fusion.4), channel_id=1, source_target_pairs={{0,4},{1,5},{2,6},{3,7},{4,0},{5,1},{6,2},{7,3},{8,12},{9,13},{10,... | collective-permute-start | bytes 3145736 | tf_op jit(solution)/shard_map/ppermute | solution.py:50
  518.0 44.6 %collective-permute-start.110 = (bf16[2,2,2,144,512]{4,3,2,1,0:T(8,128)(2,1)}, bf16[2,2,2,144,512]{4,3,2,1,0:T(8,128)(2,1)}, u32[]{:S(2)}, u32[]{:S(2)}) collective-permute-start(bf16[2,2,2,144,512]{4,3,2,1,0:T(8,128)(2,1)} %dynamic-slice_bitcast_fusion.3), channel_id=1, source_target_pairs={{0,2},{1,3},{2,0},{3,1},{4,6},{5,7},{6,4},{7,5},{8,10},{9,11},{10,... | collective-permute-start | bytes 3538952 | tf_op jit(solution)/shard_map/ppermute | solution.py:50
  547.6 25.8 %collective-permute-start.104 = (bf16[2,176,512]{2,1,0:T(8,128)(2,1)S(1)}, bf16[2,176,512]{2,1,0:T(8,128)(2,1)S(1)}, u32[]{:S(2)}, u32[]{:S(2)}) collective-permute-start(bf16[2,176,512]{2,1,0:T(8,128)(2,1)S(1)} %get-tuple-element.133), channel_id=1, source_target_pairs={{0,4},{4,8},{8,12},{12,16},{16,20},{20,24},{24,28},{1,5},{5,9},{9,... | collective-permute-start | bytes 1081352 | tf_op jit(solution)/shard_map/ppermute | solution.py:160
  550.9 26.8 %collective-permute-start.105 = (bf16[2,176,512]{2,1,0:T(8,128)(2,1)S(1)}, bf16[2,176,512]{2,1,0:T(8,128)(2,1)S(1)}, u32[]{:S(2)}, u32[]{:S(2)}) collective-permute-start(bf16[2,176,512]{2,1,0:T(8,128)(2,1)S(1)} %get-tuple-element.134), channel_id=1, source_target_pairs={{4,0},{8,4},{12,8},{16,12},{20,16},{24,20},{28,24},{5,1},{9,5},{13... | collective-permute-start | bytes 1081352 | tf_op jit(solution)/shard_map/ppermute | solution.py:160
  552.2 25.5 %collective-permute-start.106 = (bf16[2,176,512]{2,1,0:T(8,128)(2,1)S(1)}, bf16[2,176,512]{2,1,0:T(8,128)(2,1)S(1)}, u32[]{:S(2)}, u32[]{:S(2)}) collective-permute-start(bf16[2,176,512]{2,1,0:T(8,128)(2,1)S(1)} %get-tuple-element.135), channel_id=1, source_target_pairs={{0,8},{4,12},{8,16},{12,20},{16,24},{20,28},{1,9},{5,13},{9,17},{1... | collective-permute-start | bytes 1081352 | tf_op jit(solution)/shard_map/ppermute | solution.py:160
  556.6 12.7 %collective-permute-start.108 = (bf16[2,88,512]{2,1,0:T(8,128)(2,1)S(1)}, bf16[2,88,512]{2,1,0:T(8,128)(2,1)S(1)}, u32[]{:S(2)}, u32[]{:S(2)}) collective-permute-start(bf16[2,88,512]{2,1,0:T(8,128)(2,1)S(1)} %get-tuple-element.137), channel_id=1, source_target_pairs={{0,12},{4,16},{8,20},{12,24},{16,28},{1,13},{5,17},{9,21},{13,25},... | collective-permute-start | bytes 540680 | tf_op jit(solution)/shard_map/ppermute | solution.py:160
  562.6 8.3 %collective-permute-start.109 = (bf16[2,88,512]{2,1,0:T(8,128)(2,1)S(1)}, bf16[2,88,512]{2,1,0:T(8,128)(2,1)S(1)}, u32[]{:S(2)}, u32[]{:S(2)}) collective-permute-start(bf16[2,88,512]{2,1,0:T(8,128)(2,1)S(1)} %get-tuple-element.138), channel_id=1, source_target_pairs={{12,0},{16,4},{20,8},{24,12},{28,16},{13,1},{17,5},{21,9},{25,13},... | collective-permute-start | bytes 540680 | tf_op jit(solution)/shard_map/ppermute | solution.py:160
  569.3 11.9 %collective-permute-start.107 = (bf16[2,176,512]{2,1,0:T(8,128)(2,1)S(1)}, bf16[2,176,512]{2,1,0:T(8,128)(2,1)S(1)}, u32[]{:S(2)}, u32[]{:S(2)}) collective-permute-start(bf16[2,176,512]{2,1,0:T(8,128)(2,1)S(1)} %get-tuple-element.136), channel_id=1, source_target_pairs={{8,0},{12,4},{16,8},{20,12},{24,16},{28,20},{9,1},{13,5},{17,9},{2... | collective-permute-start | bytes 1081352 | tf_op jit(solution)/shard_map/ppermute | solution.py:160
  570.9 11.6 %collective-permute-start.126 = (bf16[2,2,128,512]{3,2,1,0:T(8,128)(2,1)S(1)}, bf16[2,2,128,512]{3,2,1,0:T(8,128)(2,1)S(1)}, u32[]{:S(2)}, u32[]{:S(2)}) collective-permute-start(bf16[2,2,128,512]{3,2,1,0:T(8,128)(2,1)S(1)} %dynamic-slice_bitcast_fusion.7), channel_id=1, source_target_pairs={{0,2},{1,3},{2,0},{3,1},{4,6},{5,7},{6,4},{7,5},{8,10},{9,11},{10,... | collective-permute-start | bytes 1572872 | tf_op jit(solution)/shard_map/ppermute | solution.py:50
  573.3 48.9 %collective-permute-start.125 = (bf16[2,2,144,512]{3,2,1,0:T(8,128)(2,1)}, bf16[2,2,144,512]{3,2,1,0:T(8,128)(2,1)}, u32[]{:S(2)}, u32[]{:S(2)}) collective-permute-start(bf16[2,2,144,512]{3,2,1,0:T(8,128)(2,1)} %dynamic-slice_bitcast_fusion.5), channel_id=1, source_target_pairs={{0,4},{1,5},{2,6},{3,7},{4,0},{5,1},{6,2},{7,3},{8,12},{9,13},{10,... | collective-permute-start | bytes 1769480 | tf_op jit(solution)/shard_map/ppermute | solution.py:50
  605.0 40.4 %collective-permute-start.112 = (bf16[2,176,512]{2,1,0:T(8,128)(2,1)}, bf16[2,176,512]{2,1,0:T(8,128)(2,1)S(1)}, u32[]{:S(2)}, u32[]{:S(2)}) collective-permute-start(bf16[2,176,512]{2,1,0:T(8,128)(2,1)} %get-tuple-element.145), channel_id=1, source_target_pairs={{0,4},{4,8},{8,12},{12,16},{16,20},{20,24},{24,28},{1,5},{5,9},{9,... | collective-permute-start | bytes 1081352 | tf_op jit(solution)/shard_map/ppermute | solution.py:160
  613.3 33.6 %collective-permute-start.113 = (bf16[2,176,512]{2,1,0:T(8,128)(2,1)}, bf16[2,176,512]{2,1,0:T(8,128)(2,1)}, u32[]{:S(2)}, u32[]{:S(2)}) collective-permute-start(bf16[2,176,512]{2,1,0:T(8,128)(2,1)} %get-tuple-element.146), channel_id=1, source_target_pairs={{4,0},{8,4},{12,8},{16,12},{20,16},{24,20},{28,24},{5,1},{9,5},{13... | collective-permute-start | bytes 1081352 | tf_op jit(solution)/shard_map/ppermute | solution.py:160
  614.6 32.3 %collective-permute-start.114 = (bf16[2,176,512]{2,1,0:T(8,128)(2,1)}, bf16[2,176,512]{2,1,0:T(8,128)(2,1)}, u32[]{:S(2)}, u32[]{:S(2)}) collective-permute-start(bf16[2,176,512]{2,1,0:T(8,128)(2,1)} %get-tuple-element.147), channel_id=1, source_target_pairs={{0,8},{4,12},{8,16},{12,20},{16,24},{20,28},{1,9},{5,13},{9,17},{1... | collective-permute-start | bytes 1081352 | tf_op jit(solution)/shard_map/ppermute | solution.py:160
  621.0 26.0 %collective-permute-start.115 = (bf16[2,176,512]{2,1,0:T(8,128)(2,1)}, bf16[2,176,512]{2,1,0:T(8,128)(2,1)}, u32[]{:S(2)}, u32[]{:S(2)}) collective-permute-start(bf16[2,176,512]{2,1,0:T(8,128)(2,1)} %get-tuple-element.148), channel_id=1, source_target_pairs={{8,0},{12,4},{16,8},{20,12},{24,16},{28,20},{9,1},{13,5},{17,9},{2... | collective-permute-start | bytes 1081352 | tf_op jit(solution)/shard_map/ppermute | solution.py:160
  622.3 9.0 %collective-permute-start.116 = (bf16[2,88,512]{2,1,0:T(8,128)(2,1)S(1)}, bf16[2,88,512]{2,1,0:T(8,128)(2,1)S(1)}, u32[]{:S(2)}, u32[]{:S(2)}) collective-permute-start(bf16[2,88,512]{2,1,0:T(8,128)(2,1)S(1)} %get-tuple-element.149), channel_id=1, source_target_pairs={{0,12},{4,16},{8,20},{12,24},{16,28},{1,13},{5,17},{9,21},{13,25},... | collective-permute-start | bytes 540680 | tf_op jit(solution)/shard_map/ppermute | solution.py:160
  631.3 12.6 %collective-permute-start.117 = (bf16[2,88,512]{2,1,0:T(8,128)(2,1)S(1)}, bf16[2,88,512]{2,1,0:T(8,128)(2,1)}, u32[]{:S(2)}, u32[]{:S(2)}) collective-permute-start(bf16[2,88,512]{2,1,0:T(8,128)(2,1)S(1)} %get-tuple-element.150), channel_id=1, source_target_pairs={{12,0},{16,4},{20,8},{24,12},{28,16},{13,1},{17,5},{21,9},{25,13},... | collective-permute-start | bytes 540680 | tf_op jit(solution)/shard_map/ppermute | solution.py:160
  643.9 9.9 %collective-permute-start.127 = (bf16[32,352]{1,0:T(8,128)(2,1)}, bf16[32,352]{1,0:T(8,128)(2,1)S(1)}, u32[]{:S(2)}, u32[]{:S(2)}) collective-permute-start(bf16[32,352]{1,0:T(8,128)(2,1)} %get-tuple-element.157), channel_id=1, source_target_pairs={{0,4},{4,8},{8,12},{12,16},{16,20},{20,24},{24,28},{1,5},{5,9},{9,... | collective-permute-start | bytes 67592 | tf_op jit(solution)/shard_map/ppermute | solution.py:160
  645.4 8.4 %collective-permute-start.128 = (bf16[32,352]{1,0:T(8,128)(2,1)}, bf16[32,352]{1,0:T(8,128)(2,1)S(1)}, u32[]{:S(2)}, u32[]{:S(2)}) collective-permute-start(bf16[32,352]{1,0:T(8,128)(2,1)} %get-tuple-element.158), channel_id=1, source_target_pairs={{4,0},{8,4},{12,8},{16,12},{20,16},{24,20},{28,24},{5,1},{9,5},{13... | collective-permute-start | bytes 67592 | tf_op jit(solution)/shard_map/ppermute | solution.py:160
  655.2 9.6 %collective-permute-start.121 = (f32[4,512]{1,0:T(4,128)S(1)}, f32[4,512]{1,0:T(4,128)S(1)}, u32[]{:S(2)}, u32[]{:S(2)}) collective-permute-start(f32[4,512]{1,0:T(4,128)S(1)} %add_add_fusion.9), channel_id=1, source_target_pairs={{0,4},{1,5},{2,6},{3,7},{4,0},{5,1},{6,2},{7,3},{8,12},{9,13},{10,... | collective-permute-start | bytes 24584 | tf_op jit(solution)/shard_map/ppermute | solution.py:50
  657.9 6.9 collective-permute-start.122
  664.8 9.6 %collective-permute-start.129 = (bf16[2,2,2,2,48,512]{5,4,3,2,1,0:T(8,128)(2,1)}, bf16[2,2,2,2,48,512]{5,4,3,2,1,0:T(8,128)(2,1)}, u32[]{:S(2)}, u32[]{:S(2)}) collective-permute-start(bf16[2,2,2,2,48,512]{5,4,3,2,1,0:T(8,128)(2,1)} %bitcast.389), channel_id=1, source_target_pairs={{0,1},{1,0},{2,3},{3,2},{4,5},{5,4},{6,7},{7,6},{8,9},{9,8},{10,11... | collective-permute-start | bytes 2359304 | tf_op jit(solution)/shard_map/ppermute | solution.py:50
  676.1 8.7 %collective-permute-start.146 = (bf16[2,128,512]{2,1,0:T(8,128)(2,1)S(1)}, bf16[2,128,512]{2,1,0:T(8,128)(2,1)S(1)}, u32[]{:S(2)}, u32[]{:S(2)}) collective-permute-start(bf16[2,128,512]{2,1,0:T(8,128)(2,1)S(1)} %dynamic-slice_bitcast_fusion.10), channel_id=1, source_target_pairs={{0,8},{1,9},{2,10},{3,11},{4,12},{5,13},{6,14},{7,15},{8,0},{9,1},... | collective-permute-start | bytes 786440 | tf_op jit(solution)/shard_map/ppermute | solution.py:50
  676.2 13.2 %collective-permute-start.144 = (bf16[2,144,512]{2,1,0:T(8,128)(2,1)S(1)}, bf16[2,144,512]{2,1,0:T(8,128)(2,1)S(1)}, u32[]{:S(2)}, u32[]{:S(2)}) collective-permute-start(bf16[2,144,512]{2,1,0:T(8,128)(2,1)S(1)} %dynamic-slice_bitcast_fusion.9), channel_id=1, source_target_pairs={{0,8},{1,9},{2,10},{3,11},{4,12},{5,13},{6,14},{7,15},{8,0},{9,1},... | collective-permute-start | bytes 884744 | tf_op jit(solution)/shard_map/ppermute | solution.py:50
  678.3 19.1 %collective-permute-start.140 = (bf16[2,2,2,48,512]{4,3,2,1,0:T(8,128)(2,1)S(1)}, bf16[2,2,2,48,512]{4,3,2,1,0:T(8,128)(2,1)S(1)}, u32[]{:S(2)}, u32[]{:S(2)}) collective-permute-start(bf16[2,2,2,48,512]{4,3,2,1,0:T(8,128)(2,1)S(1)} %dynamic-slice_bitcast_fusion.8), channel_id=1, source_target_pairs={{0,4},{1,5},{2,6},{3,7},{4,0},{5,1},{6,2},{7,3},{8,12},{9,13},{10,... | collective-permute-start | bytes 1179656 | tf_op jit(solution)/shard_map/ppermute | solution.py:50
  680.8 20.1 %collective-permute-start.131 = (bf16[2,2,2,2,32,512]{5,4,3,2,1,0:T(8,128)(2,1)S(1)}, bf16[2,2,2,2,32,512]{5,4,3,2,1,0:T(8,128)(2,1)S(1)}, u32[]{:S(2)}, u32[]{:S(2)}) collective-permute-start(bf16[2,2,2,2,32,512]{5,4,3,2,1,0:T(8,128)(2,1)S(1)} %bitcast.460), channel_id=1, source_target_pairs={{0,1},{1,0},{2,3},{3,2},{4,5},{5,4},{6,7},{7,6},{8,9},{9,8},{10,11... | collective-permute-start | bytes 1572872 | tf_op jit(solution)/shard_map/ppermute | solution.py:50
  680.9 19.8 %collective-permute-start.130 = (bf16[2,2,2,2,32,512]{5,4,0,1,2,3:T(8,128)(2,1)S(1)}, bf16[2,2,2,2,32,512]{5,4,0,1,2,3:T(8,128)(2,1)S(1)}, u32[]{:S(2)}, u32[]{:S(2)}) collective-permute-start(bf16[2,2,2,2,32,512]{5,4,0,1,2,3:T(8,128)(2,1)S(1)} %dynamic-slice_bitcast_fusion.6), channel_id=1, source_target_pairs={{0,1},{1,0},{2,3},{3,2},{4,5},{5,4},{6,7},{7,6},{8,9},{9,8},{10,11... | collective-permute-start | bytes 1572872 | tf_op jit(solution)/shard_map/ppermute | solution.py:50
  685.0 12.4 %collective-permute-start.147 = (bf16[128,512]{1,0:T(8,128)(2,1)S(1)}, bf16[128,512]{1,0:T(8,128)(2,1)S(1)}, u32[]{:S(2)}, u32[]{:S(2)}) collective-permute-start(bf16[128,512]{1,0:T(8,128)(2,1)S(1)} %dynamic-slice_bitcast_fusion.15), channel_id=1, source_target_pairs={{0,16},{1,17},{2,18},{3,19},{4,20},{5,21},{6,22},{7,23},{8,24},{9,... | collective-permute-start | bytes 393224 | tf_op jit(solution)/shard_map/ppermute | solution.py:50
  689.6 10.4 %collective-permute-start.145 = (bf16[144,512]{1,0:T(8,128)(2,1)S(1)}, bf16[144,512]{1,0:T(8,128)(2,1)S(1)}, u32[]{:S(2)}, u32[]{:S(2)}) collective-permute-start(bf16[144,512]{1,0:T(8,128)(2,1)S(1)} %dynamic-slice_bitcast_fusion.14), channel_id=1, source_target_pairs={{0,16},{1,17},{2,18},{3,19},{4,20},{5,21},{6,22},{7,23},{8,24},{9,... | collective-permute-start | bytes 442376 | tf_op jit(solution)/shard_map/ppermute | solution.py:50
  698.9 7.6 %collective-permute-start.141 = (bf16[2,2,48,512]{3,2,1,0:T(8,128)(2,1)S(1)}, bf16[2,2,48,512]{3,2,1,0:T(8,128)(2,1)S(1)}, u32[]{:S(2)}, u32[]{:S(2)}) collective-permute-start(bf16[2,2,48,512]{3,2,1,0:T(8,128)(2,1)S(1)} %dynamic-slice_bitcast_fusion.13), channel_id=1, source_target_pairs={{0,2},{1,3},{2,0},{3,1},{4,6},{5,7},{6,4},{7,5},{8,10},{9,11},{10,... | collective-permute-start | bytes 589832 | tf_op jit(solution)/shard_map/ppermute | solution.py:50
  701.1 15.4 %collective-permute-start.133 = (bf16[2,2,2,32,512]{4,3,2,1,0:T(8,128)(2,1)S(1)}, bf16[2,2,2,32,512]{4,3,2,1,0:T(8,128)(2,1)S(1)}, u32[]{:S(2)}, u32[]{:S(2)}) collective-permute-start(bf16[2,2,2,32,512]{4,3,2,1,0:T(8,128)(2,1)S(1)} %dynamic-slice_bitcast_fusion.11), channel_id=1, source_target_pairs={{0,4},{1,5},{2,6},{3,7},{4,0},{5,1},{6,2},{7,3},{8,12},{9,13},{10,... | collective-permute-start | bytes 786440 | tf_op jit(solution)/shard_map/ppermute | solution.py:50
  701.2 15.4 %collective-permute-start.132 = (bf16[2,2,2,32,512]{4,3,0,1,2:T(8,128)(2,1)S(1)}, bf16[2,2,2,32,512]{4,3,0,1,2:T(8,128)(2,1)S(1)}, u32[]{:S(2)}, u32[]{:S(2)}) collective-permute-start(bf16[2,2,2,32,512]{4,3,0,1,2:T(8,128)(2,1)S(1)} %dynamic-slice_bitcast_fusion.12), channel_id=1, source_target_pairs={{0,2},{1,3},{2,0},{3,1},{4,6},{5,7},{6,4},{7,5},{8,10},{9,11},{10,... | collective-permute-start | bytes 786440 | tf_op jit(solution)/shard_map/ppermute | solution.py:50
  716.8 18.6 %collective-permute-start.134 = (bf16[2,2,32,512]{3,2,0,1:T(8,128)(2,1)S(1)}, bf16[2,2,32,512]{3,2,0,1:T(8,128)(2,1)S(1)}, u32[]{:S(2)}, u32[]{:S(2)}) collective-permute-start(bf16[2,2,32,512]{3,2,0,1:T(8,128)(2,1)S(1)} %dynamic-slice_bitcast_fusion.17), channel_id=1, source_target_pairs={{0,4},{1,5},{2,6},{3,7},{4,0},{5,1},{6,2},{7,3},{8,12},{9,13},{10,... | collective-permute-start | bytes 393224 | tf_op jit(solution)/shard_map/ppermute | solution.py:50
  719.4 18.1 %collective-permute-start.137 = (bf16[2,2,32,512]{3,2,1,0:T(8,128)(2,1)S(1)}, bf16[2,2,32,512]{3,2,1,0:T(8,128)(2,1)S(1)}, u32[]{:S(2)}, u32[]{:S(2)}) collective-permute-start(bf16[2,2,32,512]{3,2,1,0:T(8,128)(2,1)S(1)} %dynamic-slice_bitcast_fusion.16), channel_id=1, source_target_pairs={{0,2},{1,3},{2,0},{3,1},{4,6},{5,7},{6,4},{7,5},{8,10},{9,11},{10,... | collective-permute-start | bytes 393224 | tf_op jit(solution)/shard_map/ppermute | solution.py:50
  (228 other events, 1603.9 us)
Sparse Core Ops, SparseCore 0:
  11.9 81.1 all-gather.4
  150.8 95.9 all-gather.6
  454.6 92.7 reduce-scatter.1

commit v4 on v3

--- a/solution.py
+++ b/solution.py
@@ -308,17 +308,17 @@
     lax.fori_loop(0, LANES // 128, body, 0)
 
 
-def piece_specs(width, first=0):
-    full = pl.BlockSpec((1, STRIP, width), lambda i: (i + first, 0, 0))
-    half = pl.BlockSpec((1, STRIP // 2, width), lambda i: (i + first, 0, 0))
+def piece_specs(width):
+    full = pl.BlockSpec((1, STRIP, width), lambda i: (i, 0, 0))
+    half = pl.BlockSpec((1, STRIP // 2, width), lambda i: (i, 0, 0))
     return [full] * 5 + [half] * 2
 
 
-def sampler_specs(width, first=0):
+def sampler_specs(width):
     return [
-        pl.BlockSpec((1, 2, LANES), lambda i: (i + first, 0, 0)),
+        pl.BlockSpec((1, 2, LANES), lambda i: (i, 0, 0)),
         pl.BlockSpec((len(ROW_ORDER), 1), lambda i: (0, 0)),
-    ] + piece_specs(width, first)
+    ] + piece_specs(width)
 
 
 def row_ids():
@@ -345,15 +345,15 @@
     )(positions, row_ids(), *pieces)
 
 
-def sample_back(positions, pieces, upstream, first, images):
-    width = pieces[0].shape[2]
+def sample_back(positions, pieces, upstream):
+    images, _, width = pieces[0].shape
     full = (images, STRIP, width)
     half = (images, STRIP // 2, width)
     return pl.pallas_call(
         sample_back_kernel,
         grid=(images,),
-        in_specs=sampler_specs(width, first)
-        + [pl.BlockSpec((1, STRIP, 9 * width), lambda i: (i + first, 0, 0))],
+        in_specs=sampler_specs(width)
+        + [pl.BlockSpec((1, STRIP, 9 * width), lambda i: (i, 0, 0))],
         out_specs=piece_specs(width) + [pl.BlockSpec((1, 2, LANES), lambda i: (i, 0, 0))],
         out_shape=[jax.ShapeDtypeStruct(full, f32)]
         + [jax.ShapeDtypeStruct(full, bf16)] * 4
@@ -997,27 +997,17 @@
     back_sampled = dot_nt(back_second, weight_deform_one).astype(bf16).reshape(images, STRIP, -1)
     back_sampled = beside_steps(back_sampled, one_left, one_right)
 
-    def returned(upstream, first):
-        own, *others, position_grad = sample_back(
-            positions, pieces, upstream, first, images // MB
-        )
-        half_sum = jnp.concatenate([from_behind(others[4], 3), from_behind(others[5], -3)], axis=1)
-        own = (
-            own
-            + from_behind(others[0], 1).astype(f32)
-            + from_behind(others[1], -1).astype(f32)
-            + from_behind(others[2], 2).astype(f32)
-            + from_behind(others[3], -2).astype(f32)
-            + half_sum.astype(f32)
-        )
-        return own, position_grad
-
-    backs = [returned(back_sampled, 0)]
-    back_sampled = beside_steps(back_sampled, one_left, one_right)
-    back_sampled, two_shard = meet(back_sampled, two_shard)
-    backs.append(returned(back_sampled, images // MB))
-    own = jnp.concatenate([pair[0] for pair in backs], axis=0)
-    position_grad = jnp.concatenate([pair[1] for pair in backs], axis=0)
+    own, *others, position_grad = sample_back(positions, pieces, back_sampled)
+    half_sum = jnp.concatenate([from_behind(others[4], 3), from_behind(others[5], -3)], axis=1)
+    own = (
+        own
+        + from_behind(others[0], 1).astype(f32)
+        + from_behind(others[1], -1).astype(f32)
+        + from_behind(others[2], 2).astype(f32)
+        + from_behind(others[3], -2).astype(f32)
+        + half_sum.astype(f32)
+    )
+    own, two_shard = meet(own, two_shard)
     back_offsets, last_rim, first_rim = offset_slope(position_grad, squashed)
     stacked, offset_chunks = offset_back(
         back_offsets,

time: 765 us -> 758 us (level)
    ppermute x26 -> x20, starting transfers between devices: 77.2 us -> 61.4 us  [from_behind(): lax.ppermute(value, 'rows', [(source, source + steps) for source in range...]
    ppermute x122, starting transfers between devices: 140 us -> 153 us  [exchange(): lax.ppermute(value, BOTH, [(i, i ^ mask) for i in range(device_count())])]
    unnamed x305 -> x303, local copies, waits for them, and re-layouts: 55.2 us -> 51.1 us
    ppermute x26 -> x20, waiting for transfers between devices: 42.3 us -> 40.4 us  [from_behind(): lax.ppermute(value, 'rows', [(source, source + steps) for source in range...]
    pallas_call x2 -> x1, Pallas kernels: 31.4 us -> 30.1 us  [sample_back(): pl.pallas_call(sample_back_kernel, grid=(images,), in_specs=sampler_specs...]
  transfers between devices with their start and end apart: 151 -> 145, of which waited for: 92 -> 88; matrix products, arithmetic and copies ran while one was open for 23% -> 23% of each run, Pallas kernels for 7% -> 7%
where the time goes in v4:
time: 758 us; the launch traced here: 748 us
  starting transfers between devices  214 us (28%)
  waiting for transfers between devices  197 us (26%)
  local copies, waits for them, and re-layouts  102 us (13%)
  other arithmetic  81.3 us (11%)
  matrix products  73.9 us (10%)
  Pallas kernels  63.1 us (8%)
  between operations  17 us (2%)
    ppermute x122, waiting for transfers between devices, exchange(): lax.ppermute(value, BOTH, [(i, i ^ mask) for i in range(device_count())])  153 us
    ppermute x122, starting transfers between devices, exchange(): lax.ppermute(value, BOTH, [(i, i ^ mask) for i in range(device_count())])  153 us
    ppermute x20, starting transfers between devices, from_behind(): lax.ppermute(value, 'rows', [(source, source + steps) for source in range...  61.4 us
    unnamed x303, local copies, waits for them, and re-layouts  51.1 us
    ppermute x20, waiting for transfers between devices, from_behind(): lax.ppermute(value, 'rows', [(source, source + steps) for source in range...  40.4 us
    pallas_call x1, Pallas kernels, sample_back(): pl.pallas_call(sample_back_kernel, grid=(images,), in_specs=sampler_specs...  30.1 us
    dot_general x7, matrix products, dot_tn(): lax.dot_general(left, right, (((0,), (0,)), ((), ())), preferred_element_...  29.7 us
    dot_general x5, matrix products, dot_nt(): lax.dot_general(left, right, (((1,), (1,)), ((), ())), preferred_element_...  24.7 us
  transfers between devices with their start and end apart: 145, of which 88 were waited for; matrix products, arithmetic and copies ran while one was open for 23% of the time, Pallas kernels for 7%

profile of v4, /device:TPU:0, one launch (start us, length us, event | category | flops | bytes accessed | tf_op | source)
XLA Modules:
  0.0 748.2 jit_solution(113068407616251030)
XLA Ops:
  13.5 3.1 collective-permute-start.5
  23.6 3.9 collective-permute-done.4
  28.3 4.5 collective-permute-done.1
  36.0 3.3 collective-permute-done.7
  44.2 3.3 copy.73
  50.3 4.5 collective-permute-done.9
  57.0 4.4 collective-permute-done.8
  89.6 3.7 collective-permute-start.19
  105.0 5.4 collective-permute-start.22
  111.6 5.4 collective-permute-start.24
  117.1 5.6 collective-permute-start.26
  122.7 3.3 copy.76
  126.0 4.4 reshape.660
  132.9 7.2 collective-permute-done.26.refs_6_
  140.1 4.0 collective-permute-done.22.refs_2_
  150.7 17.6 %sample.1 = bf16[4,176,4608]{2,1,0:T(8,128)(2,1)} custom-call(f32[4,2,1664]{2,1,0:T(2,128)} %get-tuple-element.102.pos_ref, f32[24,1]{1,0:T(8,128)} %constant.444.row_ref, bf16[4,176,512]{2,1,0:T(8,128)(2,1)} %multiply_convert_fusion.10.refs_0_, bf16[4,176,512]{2,1,0:T(8,128)(2,1)} %collective-permute-done.21.refs_1_, ...), custom_call_target="tpu_custom_call" | custom-call | flops 1 | bytes 1 | tf_op jit(solution)/shard_map/sample/pallas_call | solution.py:330
  173.6 4.6 fusion.119
  183.8 6.6 collective-permute-start.30
  190.4 8.9 %collective-permute-start.31 = (f32[4,512]{1,0:T(4,128)S(1)}, f32[4,512]{1,0:T(4,128)S(1)}, u32[]{:S(2)}, u32[]{:S(2)}) collective-permute-start(f32[4,512]{1,0:T(4,128)S(1)} %add_add_fusion.21), channel_id=1, source_target_pairs={{0,8},{1,9},{2,10},{3,11},{4,12},{5,13},{6,14},{7,15},{8,0},{9,1},... | collective-permute-start | bytes 24584 | tf_op jit(solution)/shard_map/ppermute | solution.py:50
  209.8 5.4 fusion.112
  217.2 3.1 collective-permute-done.35
  231.3 5.4 collective-permute-done.40
  238.2 5.1 multiply_convert_fusion.3
  243.3 3.6 all-gather.7.cloned.1.call-done
  264.8 3.5 collective-permute-done.47
  271.5 3.1 collective-permute-start.48
  282.1 4.1 conv.1
  307.8 4.8 fusion.111
  329.6 8.8 %fusion.110 = (f32[2,2048]{1,0:T(2,128)S(1)}, f32[2,2048]{1,0:T(2,128)S(1)}, f32[2,352,2048]{2,1,0:T(8,128)S(1)}, bf16[2,352,2048]{2,1,0:T(8,128)(2,1)}) fusion(f32[2,2048]{1,0:T(2,128)S(1)} %get-tuple-element.325, f32[2,352,2048]{2,1,0:T(8,128)} %get-tuple-element.360, f32[2,2048]{1,0:T(2,128)S(1)} %get-tuple-element.326, ...), kind=kLoop, calls=%fused_computation.406 | loop fusion | flops 30269440 | bytes 20269824 | tf_op jit(solution)/shard_map/reduce_sum | solution.py:730
  351.3 3.8 collective-permute-done.70
  357.0 4.7 fusion.116
  369.6 4.1 bitcast_convert_fusion.2
  375.0 3.4 collective-permute-done.77
  379.4 7.4 convolution_convert_fusion.2
  391.3 6.4 collective-permute-done.78
  397.7 5.9 fusion
  407.6 3.1 collective-permute-done.79.above
  410.7 4.2 collective-permute-done.80.below
  417.3 4.0 conv_back.1
  440.5 8.4 %fusion.109 = (f32[2,2048]{1,0:T(2,128)S(1)}, f32[2,2048]{1,0:T(2,128)S(1)}, f32[2,352,2048]{2,1,0:T(8,128)}) fusion(f32[2,2048]{1,0:T(2,128)S(1)} %get-tuple-element.322, f32[2,352,2048]{2,1,0:T(8,128)S(1)} %bitcast.412, f32[2,2048]{1,0:T(2,128)S(1)} %get-tuple-element.323, bf16[2,352,2048]{2,1,0:T(8,128)(2,1)S(1)} %bitcast.394, ...), kind=kOutput, calls=%fused_computation.405 | convolution fusion | flops 1502339072 | bytes 23085056 | tf_op jit(solution)/shard_map/dot_general | solution.py:38
  463.3 4.0 bitcast_convert_fusion
  469.1 3.5 bitcast_convert_fusion.1
  472.7 3.5 fusion.114
  489.1 3.2 collective-permute-done.101
  492.8 4.2 convolution_convert_fusion.1
  500.8 6.4 convolution_convert_fusion
  507.3 3.6 fusion.4
  513.1 30.1 %sample_back.1 = (f32[4,176,512]{2,1,0:T(8,128)S(1)}, bf16[4,176,512]{2,1,0:T(8,128)(2,1)}, bf16[4,176,512]{2,1,0:T(8,128)(2,1)S(1)}, bf16[4,176,512]{2,1,0:T(8,...) custom-call(f32[4,2,1664]{2,1,0:T(2,128)S(1)} %copy-done.16, ...), custom_call_target="tpu_custom_call" | custom-call | flops 1 | bytes 1 | tf_op jit(solution)/shard_map/sample_back/pallas_call | solution.py:352
  547.5 3.7 collective-permute-start.104
  551.2 3.5 collective-permute-start.108
  557.8 3.3 collective-permute-start.119
  562.5 4.3 reshape.673
  566.8 5.9 copy.88
  576.2 11.5 %collective-permute-start.106 = (bf16[4,176,512]{2,1,0:T(8,128)(2,1)S(1)}, bf16[4,176,512]{2,1,0:T(8,128)(2,1)S(1)}, u32[]{:S(2)}, u32[]{:S(2)}) collective-permute-start(bf16[4,176,512]{2,1,0:T(8,128)(2,1)S(1)} %copy-done.24), channel_id=1, source_target_pairs={{0,8},{4,12},{8,16},{12,20},{16,24},{20,28},{1,9},{5,13},{9,17},{1... | collective-permute-start | bytes 2162696 | tf_op jit(solution)/shard_map/ppermute | solution.py:160
  591.0 8.4 %collective-permute-start.118 = (bf16[2,2,2,128,512]{4,3,2,1,0:T(8,128)(2,1)S(1)}, bf16[2,2,2,128,512]{4,3,2,1,0:T(8,128)(2,1)S(1)}, u32[]{:S(2)}, u32[]{:S(2)}) collective-permute-start(bf16[2,2,2,128,512]{4,3,2,1,0:T(8,128)(2,1)S(1)} %dynamic-slice_bitcast_fusion.4), channel_id=1, source_target_pairs={{0,4},{1,5},{2,6},{3,7},{4,0},{5,1},{6,2},{7,3},{8,12},{9,13},{10,... | collective-permute-start | bytes 3145736 | tf_op jit(solution)/shard_map/ppermute | solution.py:50
  602.6 13.7 %collective-permute-done.107 = bf16[4,176,512]{2,1,0:T(8,128)(2,1)S(1)} collective-permute-done((bf16[4,176,512]{2,1,0:T(8,128)(2,1)S(1)}, bf16[4,176,512]{2,1,0:T(8,128)(2,1)S(1)}, u32[]{:S(2)}, u32[]{:S(2)}) %collective-permute-start.107) | collective-permute-done | bytes 720928 | tf_op jit(solution)/shard_map/ppermute | solution.py:160
  616.3 3.1 convert_add_fusion.7
  635.5 10.2 %collective-permute-start.114 = (f32[4,512]{1,0:T(4,128)S(1)}, f32[4,512]{1,0:T(4,128)S(1)}, u32[]{:S(2)}, u32[]{:S(2)}) collective-permute-start(f32[4,512]{1,0:T(4,128)S(1)} %add_add_fusion.9), channel_id=1, source_target_pairs={{0,8},{1,9},{2,10},{3,11},{4,12},{5,13},{6,14},{7,15},{8,0},{9,1},... | collective-permute-start | bytes 24584 | tf_op jit(solution)/shard_map/ppermute | solution.py:50
  667.1 12.4 %collective-permute-done.132 = bf16[2,2,2,48,512]{4,3,2,1,0:T(8,128)(2,1)} collective-permute-done((bf16[2,2,2,48,512]{4,3,2,1,0:T(8,128)(2,1)}, bf16[2,2,2,48,512]{4,3,2,1,0:T(8,128)(2,1)}, u32[]{:S(2)}, u32[]{:S(2)}) %collective-permute-start.132) | collective-permute-done | bytes 393248 | tf_op jit(solution)/shard_map/ppermute | solution.py:50
  690.0 4.7 fusion.2
  697.1 3.3 collective-permute-done.134
  703.4 3.2 collective-permute-done.135
  710.7 5.9 reshape.686
  716.6 9.0 %copy.89 = f32[4,4,44,2048]{3,1,2,0:T(4,128)} copy(f32[4,4,44,2048]{3,2,1,0:T(8,128)} %reshape.686) | data formatting | bytes 11534336
  (787 shorter events, 360.5 us)
Async XLA Ops:
  7.2 161.1 %all-gather.5.cloned.1.call-start = ((), (), s32[]{:S(2)}) async-start(), calls=%async_computation.2 | async-start | bytes 7028736 | tf_op jit(solution)/shard_map/all_gather | solution.py:775
  11.8 235.1 %all-gather.7.cloned.1.call-start = ((), (), s32[]{:S(2)}) async-start(), calls=%async_computation.3 | async-start | bytes 9191424 | tf_op jit(solution)/shard_map/all_gather | solution.py:775
  13.5 8.9 %collective-permute-start.5 = (bf16[48,512]{1,0:T(8,128)(2,1)S(1)}, bf16[48,512]{1,0:T(8,128)(2,1)S(1)}, u32[]{:S(2)}, u32[]{:S(2)}) collective-permute-start(bf16[48,512]{1,0:T(8,128)(2,1)S(1)} %pad_maximum_fusion.15), channel_id=1, source_target_pairs={{0,8},{1,9},{2,10},{3,11},{4,12},{5,13},{6,14},{7,15},{8,0},{9,1},... | collective-permute-start | bytes 147464 | tf_op jit(solution)/shard_map/ppermute | solution.py:50
  16.5 7.0 collective-permute-start.3
  19.0 8.4 %collective-permute-start.4 = (bf16[48,512]{1,0:T(8,128)(2,1)S(1)}, bf16[48,512]{1,0:T(8,128)(2,1)S(1)}, u32[]{:S(2)}, u32[]{:S(2)}) collective-permute-start(bf16[48,512]{1,0:T(8,128)(2,1)S(1)} %pad_maximum_fusion.15), channel_id=1, source_target_pairs={{0,16},{1,17},{2,18},{3,19},{4,20},{5,21},{6,22},{7,23},{8,24},{9,... | collective-permute-start | bytes 147464 | tf_op jit(solution)/shard_map/ppermute | solution.py:50
  19.1 9.1 %collective-permute-start = (bf16[64,512]{1,0:T(8,128)(2,1)}, bf16[64,512]{1,0:T(8,128)(2,1)S(1)}, u32[]{:S(2)}, u32[]{:S(2)}) collective-permute-start(bf16[64,512]{1,0:T(8,128)(2,1)} %param.29), channel_id=1, source_target_pairs={{0,24},{1,25},{2,26},{3,27},{4,28},{5,29},{6,30},{7,31},{8,16},{9,... | collective-permute-start | bytes 196616 | tf_op jit(solution)/shard_map/ppermute | solution.py:50
  22.1 10.7 %collective-permute-start.1 = (bf16[64,512]{1,0:T(8,128)(2,1)}, bf16[64,512]{1,0:T(8,128)(2,1)S(1)}, u32[]{:S(2)}, u32[]{:S(2)}) collective-permute-start(bf16[64,512]{1,0:T(8,128)(2,1)} %param.29), channel_id=1, source_target_pairs={{0,16},{1,17},{2,18},{3,19},{4,20},{5,21},{6,22},{7,23},{8,24},{9,... | collective-permute-start | bytes 196616 | tf_op jit(solution)/shard_map/ppermute | solution.py:50
  32.9 6.4 collective-permute-start.7
  34.5 7.5 collective-permute-start.6
  42.0 12.8 %collective-permute-start.9 = (bf16[2,2,2,48,512]{4,3,1,0,2:T(8,128)(2,1)}, bf16[2,2,2,48,512]{4,3,1,0,2:T(8,128)(2,1)}, u32[]{:S(2)}, u32[]{:S(2)}) collective-permute-start(bf16[2,2,2,48,512]{4,3,1,0,2:T(8,128)(2,1)} %pad_maximum_fusion.5), channel_id=1, source_target_pairs={{0,4},{1,5},{2,6},{3,7},{4,0},{5,1},{6,2},{7,3},{8,12},{9,13},{10,... | collective-permute-start | bytes 1179656 | tf_op jit(solution)/shard_map/ppermute | solution.py:50
  43.6 17.8 %collective-permute-start.8 = (bf16[2,2,2,64,512]{4,3,2,1,0:T(8,128)(2,1)S(1)}, bf16[2,2,2,64,512]{4,3,2,1,0:T(8,128)(2,1)}, u32[]{:S(2)}, u32[]{:S(2)}) collective-permute-start(bf16[2,2,2,64,512]{4,3,2,1,0:T(8,128)(2,1)S(1)} %pad_maximum_fusion.4), channel_id=1, source_target_pairs={{0,2},{1,3},{2,0},{3,1},{4,6},{5,7},{6,4},{7,5},{8,10},{9,11},{10,... | collective-permute-start | bytes 1572872 | tf_op jit(solution)/shard_map/ppermute | solution.py:50
  81.7 13.0 %collective-permute-start.18 = (f32[4,512]{1,0:T(4,128)S(1)}, f32[4,512]{1,0:T(4,128)S(1)}, u32[]{:S(2)}, u32[]{:S(2)}) collective-permute-start(f32[4,512]{1,0:T(4,128)S(1)} %add_add_fusion.22), channel_id=1, source_target_pairs={{0,16},{1,17},{2,18},{3,19},{4,20},{5,21},{6,22},{7,23},{8,24},{9,... | collective-permute-start | bytes 24584 | tf_op jit(solution)/shard_map/ppermute | solution.py:50
  89.6 9.2 %collective-permute-start.19 = (f32[96,352]{1,0:T(8,128)S(1)}, f32[96,352]{1,0:T(8,128)S(1)}, u32[]{:S(2)}, u32[]{:S(2)}) collective-permute-start(f32[96,352]{1,0:T(8,128)S(1)} %get-tuple-element.96), channel_id=1, source_target_pairs={{0,4},{4,8},{8,12},{12,16},{16,20},{20,24},{24,28},{1,5},{5,9},{9,... | collective-permute-start | bytes 405512 | tf_op jit(solution)/shard_map/ppermute | solution.py:160
  93.4 7.0 collective-permute-start.20
  102.4 14.7 %collective-permute-start.25 = (bf16[4,88,512]{2,1,0:T(8,128)(2,1)S(1)}, bf16[4,88,512]{2,1,0:T(8,128)(2,1)S(1)}, u32[]{:S(2)}, u32[]{:S(2)}) collective-permute-start(bf16[4,88,512]{2,1,0:T(8,128)(2,1)S(1)} %get-tuple-element.292), channel_id=1, source_target_pairs={{12,0},{16,4},{20,8},{24,12},{28,16},{13,1},{17,5},{21,9},{25,13},... | collective-permute-start | bytes 1081352 | tf_op jit(solution)/shard_map/ppermute | solution.py:160
  103.7 36.5 %collective-permute-start.21 = (bf16[4,176,512]{2,1,0:T(8,128)(2,1)}, bf16[4,176,512]{2,1,0:T(8,128)(2,1)}, u32[]{:S(2)}, u32[]{:S(2)}) collective-permute-start(bf16[4,176,512]{2,1,0:T(8,128)(2,1)} %multiply_convert_fusion.10.refs_0_), channel_id=1, source_target_pairs={{4,0},{8,4},{12,8},{16,12},{20,16},{24,20},{28,24},{5,1},{9,5},{13... | collective-permute-start | bytes 2162696 | tf_op jit(solution)/shard_map/ppermute | solution.py:160
  105.0 39.2 %collective-permute-start.22 = (bf16[4,176,512]{2,1,0:T(8,128)(2,1)}, bf16[4,176,512]{2,1,0:T(8,128)(2,1)}, u32[]{:S(2)}, u32[]{:S(2)}) collective-permute-start(bf16[4,176,512]{2,1,0:T(8,128)(2,1)} %multiply_convert_fusion.10.refs_0_), channel_id=1, source_target_pairs={{0,4},{4,8},{8,12},{12,16},{16,20},{20,24},{24,28},{1,5},{5,9},{9,... | collective-permute-start | bytes 2162696 | tf_op jit(solution)/shard_map/ppermute | solution.py:160
  110.4 34.9 %collective-permute-start.23 = (bf16[4,176,512]{2,1,0:T(8,128)(2,1)}, bf16[4,176,512]{2,1,0:T(8,128)(2,1)}, u32[]{:S(2)}, u32[]{:S(2)}) collective-permute-start(bf16[4,176,512]{2,1,0:T(8,128)(2,1)} %multiply_convert_fusion.10.refs_0_), channel_id=1, source_target_pairs={{8,0},{12,4},{16,8},{20,12},{24,16},{28,20},{9,1},{13,5},{17,9},{2... | collective-permute-start | bytes 2162696 | tf_op jit(solution)/shard_map/ppermute | solution.py:160
  111.6 33.6 %collective-permute-start.24 = (bf16[4,176,512]{2,1,0:T(8,128)(2,1)}, bf16[4,176,512]{2,1,0:T(8,128)(2,1)}, u32[]{:S(2)}, u32[]{:S(2)}) collective-permute-start(bf16[4,176,512]{2,1,0:T(8,128)(2,1)} %multiply_convert_fusion.10.refs_0_), channel_id=1, source_target_pairs={{0,8},{4,12},{8,16},{12,20},{16,24},{20,28},{1,9},{5,13},{9,17},{1... | collective-permute-start | bytes 2162696 | tf_op jit(solution)/shard_map/ppermute | solution.py:160
  117.1 23.1 %collective-permute-start.26 = (bf16[4,88,512]{2,1,0:T(8,128)(2,1)}, bf16[4,88,512]{2,1,0:T(8,128)(2,1)}, u32[]{:S(2)}, u32[]{:S(2)}) collective-permute-start(bf16[4,88,512]{2,1,0:T(8,128)(2,1)} %get-tuple-element.291), channel_id=1, source_target_pairs={{0,12},{4,16},{8,20},{12,24},{16,28},{1,13},{5,17},{9,21},{13,25},... | collective-permute-start | bytes 1081352 | tf_op jit(solution)/shard_map/ppermute | solution.py:160
  150.6 473.0 %reduce-scatter.2.cloned.1.call-start = ((), (), s32[]{:S(2)}) async-start(), calls=%async_computation.1 | async-start | bytes 3620864 | tf_op jit(solution)/shard_map/reduce_scatter | solution.py:108
  183.8 17.1 %collective-permute-start.30 = (f32[4,512]{1,0:T(4,128)S(1)}, f32[4,512]{1,0:T(4,128)S(1)}, u32[]{:S(2)}, u32[]{:S(2)}) collective-permute-start(f32[4,512]{1,0:T(4,128)S(1)} %add_add_fusion.21), channel_id=1, source_target_pairs={{0,4},{1,5},{2,6},{3,7},{4,0},{5,1},{6,2},{7,3},{8,12},{9,13},{10,... | collective-permute-start | bytes 24584 | tf_op jit(solution)/shard_map/ppermute | solution.py:50
  190.4 10.6 %collective-permute-start.31 = (f32[4,512]{1,0:T(4,128)S(1)}, f32[4,512]{1,0:T(4,128)S(1)}, u32[]{:S(2)}, u32[]{:S(2)}) collective-permute-start(f32[4,512]{1,0:T(4,128)S(1)} %add_add_fusion.21), channel_id=1, source_target_pairs={{0,8},{1,9},{2,10},{3,11},{4,12},{5,13},{6,14},{7,15},{8,0},{9,1},... | collective-permute-start | bytes 24584 | tf_op jit(solution)/shard_map/ppermute | solution.py:50
  222.5 6.1 collective-permute-start.38
  222.5 8.4 %collective-permute-start.39 = (f32[4,2048]{1,0:T(4,128)S(1)}, f32[4,2048]{1,0:T(4,128)S(1)}, u32[]{:S(2)}, u32[]{:S(2)}) collective-permute-start(f32[4,2048]{1,0:T(4,128)S(1)} %add_add_fusion.7), channel_id=1, source_target_pairs={{0,12},{1,13},{2,14},{3,15},{4,8},{5,9},{6,10},{7,11},{8,4},{9,5},... | collective-permute-start | bytes 98312 | tf_op jit(solution)/shard_map/ppermute | solution.py:50
  271.5 8.3 %collective-permute-start.48 = (bf16[4,44,512]{2,1,0:T(8,128)(2,1)S(1)}, bf16[4,44,512]{2,1,0:T(8,128)(2,1)S(1)}, u32[]{:S(2)}, u32[]{:S(2)}) collective-permute-start(bf16[4,44,512]{2,1,0:T(8,128)(2,1)S(1)} %get-tuple-element.290), channel_id=1, source_target_pairs={{0,4},{4,8},{8,12},{12,16},{16,20},{20,24},{24,28},{1,5},{5,9},{9,... | collective-permute-start | bytes 540680 | tf_op jit(solution)/shard_map/ppermute | solution.py:160
  274.6 7.6 %collective-permute-start.49 = (bf16[4,44,512]{2,1,0:T(8,128)(2,1)S(1)}, bf16[4,44,512]{2,1,0:T(8,128)(2,1)S(1)}, u32[]{:S(2)}, u32[]{:S(2)}) collective-permute-start(bf16[4,44,512]{2,1,0:T(8,128)(2,1)S(1)} %get-tuple-element.289), channel_id=1, source_target_pairs={{4,0},{8,4},{12,8},{16,12},{20,16},{24,20},{28,24},{5,1},{9,5},{13... | collective-permute-start | bytes 540680 | tf_op jit(solution)/shard_map/ppermute | solution.py:160
  294.3 6.6 collective-permute-start.53
  366.0 7.7 %collective-permute-start.74 = (f32[4,512]{1,0:T(4,128)S(1)}, f32[4,512]{1,0:T(4,128)S(1)}, u32[]{:S(2)}, u32[]{:S(2)}) collective-permute-start(f32[4,512]{1,0:T(4,128)S(1)} %add_add_fusion.15), channel_id=1, source_target_pairs={{0,4},{1,5},{2,6},{3,7},{4,0},{5,1},{6,2},{7,3},{8,12},{9,13},{10,... | collective-permute-start | bytes 24584 | tf_op jit(solution)/shard_map/ppermute | solution.py:50
  366.8 6.9 collective-permute-start.75
  367.7 6.0 collective-permute-start.76
  391.3 6.4 collective-permute-start.78
  403.6 7.1 collective-permute-start.79
  406.3 8.7 %collective-permute-start.80 = (bf16[4,44,512]{2,1,0:T(8,128)(2,1)S(1)}, bf16[4,44,512]{2,1,0:T(8,128)(2,1)S(1)}, u32[]{:S(2)}, u32[]{:S(2)}) collective-permute-start(bf16[4,44,512]{2,1,0:T(8,128)(2,1)S(1)} %get-tuple-element.287), channel_id=1, source_target_pairs={{4,0},{8,4},{12,8},{16,12},{20,16},{24,20},{28,24},{5,1},{9,5},{13... | collective-permute-start | bytes 540680 | tf_op jit(solution)/shard_map/ppermute | solution.py:160
  498.8 8.5 %collective-permute-start.103 = (bf16[2,2,2,2,128,512]{5,4,3,2,1,0:T(8,128)(2,1)}, bf16[2,2,2,2,128,512]{5,4,3,2,1,0:T(8,128)(2,1)}, u32[]{:S(2)}, u32[]{:S(2)}) collective-permute-start(bf16[2,2,2,2,128,512]{5,4,3,2,1,0:T(8,128)(2,1)} %dynamic-slice_bitcast_fusion.2), channel_id=1, source_target_pairs={{0,1},{1,0},{2,3},{3,2},{4,5},{5,4},{6,7},{7,6},{8,9},{9,8},{10,11... | collective-permute-start | bytes 6291464 | tf_op jit(solution)/shard_map/ppermute | solution.py:50
  500.3 10.6 %collective-permute-start.102 = (bf16[2,2,2,2,144,512]{5,4,3,2,1,0:T(8,128)(2,1)}, bf16[2,2,2,2,144,512]{5,4,3,2,1,0:T(8,128)(2,1)S(1)}, u32[]{:S(2)}, u32[]{:S(2)}) collective-permute-start(bf16[2,2,2,2,144,512]{5,4,3,2,1,0:T(8,128)(2,1)} %dynamic-slice_bitcast_fusion.1), channel_id=1, source_target_pairs={{0,1},{1,0},{2,3},{3,2},{4,5},{5,4},{6,7},{7,6},{8,9},{9,8},{10,11... | collective-permute-start | bytes 7077896 | tf_op jit(solution)/shard_map/ppermute | solution.py:50
  547.5 51.9 %collective-permute-start.104 = (bf16[4,176,512]{2,1,0:T(8,128)(2,1)}, bf16[4,176,512]{2,1,0:T(8,128)(2,1)}, u32[]{:S(2)}, u32[]{:S(2)}) collective-permute-start(bf16[4,176,512]{2,1,0:T(8,128)(2,1)} %get-tuple-element.122), channel_id=1, source_target_pairs={{0,4},{4,8},{8,12},{12,16},{16,20},{20,24},{24,28},{1,5},{5,9},{9,... | collective-permute-start | bytes 2162696 | tf_op jit(solution)/shard_map/ppermute | solution.py:160
  551.2 36.5 %collective-permute-start.108 = (bf16[4,88,512]{2,1,0:T(8,128)(2,1)S(1)}, bf16[4,88,512]{2,1,0:T(8,128)(2,1)}, u32[]{:S(2)}, u32[]{:S(2)}) collective-permute-start(bf16[4,88,512]{2,1,0:T(8,128)(2,1)S(1)} %get-tuple-element.126), channel_id=1, source_target_pairs={{0,12},{4,16},{8,20},{12,24},{16,28},{1,13},{5,17},{9,21},{13,25},... | collective-permute-start | bytes 1081352 | tf_op jit(solution)/shard_map/ppermute | solution.py:160
  554.8 36.2 %collective-permute-start.109 = (bf16[4,88,512]{2,1,0:T(8,128)(2,1)}, bf16[4,88,512]{2,1,0:T(8,128)(2,1)}, u32[]{:S(2)}, u32[]{:S(2)}) collective-permute-start(bf16[4,88,512]{2,1,0:T(8,128)(2,1)} %get-tuple-element.127), channel_id=1, source_target_pairs={{12,0},{16,4},{20,8},{24,12},{28,16},{13,1},{17,5},{21,9},{25,13},... | collective-permute-start | bytes 1081352 | tf_op jit(solution)/shard_map/ppermute | solution.py:160
  557.8 17.1 %collective-permute-start.119 = (bf16[32,352]{1,0:T(8,128)(2,1)}, bf16[32,352]{1,0:T(8,128)(2,1)S(1)}, u32[]{:S(2)}, u32[]{:S(2)}) collective-permute-start(bf16[32,352]{1,0:T(8,128)(2,1)} %get-tuple-element.135), channel_id=1, source_target_pairs={{0,4},{4,8},{8,12},{12,16},{16,20},{20,24},{24,28},{1,5},{5,9},{9,... | collective-permute-start | bytes 67592 | tf_op jit(solution)/shard_map/ppermute | solution.py:160
  561.1 15.1 %collective-permute-start.120 = (bf16[32,352]{1,0:T(8,128)(2,1)}, bf16[32,352]{1,0:T(8,128)(2,1)S(1)}, u32[]{:S(2)}, u32[]{:S(2)}) collective-permute-start(bf16[32,352]{1,0:T(8,128)(2,1)} %get-tuple-element.136), channel_id=1, source_target_pairs={{4,0},{8,4},{12,8},{16,12},{20,16},{24,20},{28,24},{5,1},{9,5},{13... | collective-permute-start | bytes 67592 | tf_op jit(solution)/shard_map/ppermute | solution.py:160
  574.9 26.2 %collective-permute-start.105 = (bf16[4,176,512]{2,1,0:T(8,128)(2,1)S(1)}, bf16[4,176,512]{2,1,0:T(8,128)(2,1)S(1)}, u32[]{:S(2)}, u32[]{:S(2)}) collective-permute-start(bf16[4,176,512]{2,1,0:T(8,128)(2,1)S(1)} %copy-done.26), channel_id=1, source_target_pairs={{4,0},{8,4},{12,8},{16,12},{20,16},{24,20},{28,24},{5,1},{9,5},{13... | collective-permute-start | bytes 2162696 | tf_op jit(solution)/shard_map/ppermute | solution.py:160
  576.2 26.4 %collective-permute-start.106 = (bf16[4,176,512]{2,1,0:T(8,128)(2,1)S(1)}, bf16[4,176,512]{2,1,0:T(8,128)(2,1)S(1)}, u32[]{:S(2)}, u32[]{:S(2)}) collective-permute-start(bf16[4,176,512]{2,1,0:T(8,128)(2,1)S(1)} %copy-done.24), channel_id=1, source_target_pairs={{0,8},{4,12},{8,16},{12,20},{16,24},{20,28},{1,9},{5,13},{9,17},{1... | collective-permute-start | bytes 2162696 | tf_op jit(solution)/shard_map/ppermute | solution.py:160
  587.7 28.6 %collective-permute-start.107 = (bf16[4,176,512]{2,1,0:T(8,128)(2,1)S(1)}, bf16[4,176,512]{2,1,0:T(8,128)(2,1)S(1)}, u32[]{:S(2)}, u32[]{:S(2)}) collective-permute-start(bf16[4,176,512]{2,1,0:T(8,128)(2,1)S(1)} %copy-done.22), channel_id=1, source_target_pairs={{8,0},{12,4},{16,8},{20,12},{24,16},{28,20},{9,1},{13,5},{17,9},{2... | collective-permute-start | bytes 2162696 | tf_op jit(solution)/shard_map/ppermute | solution.py:160
  591.0 31.3 %collective-permute-start.118 = (bf16[2,2,2,128,512]{4,3,2,1,0:T(8,128)(2,1)S(1)}, bf16[2,2,2,128,512]{4,3,2,1,0:T(8,128)(2,1)S(1)}, u32[]{:S(2)}, u32[]{:S(2)}) collective-permute-start(bf16[2,2,2,128,512]{4,3,2,1,0:T(8,128)(2,1)S(1)} %dynamic-slice_bitcast_fusion.4), channel_id=1, source_target_pairs={{0,4},{1,5},{2,6},{3,7},{4,0},{5,1},{6,2},{7,3},{8,12},{9,13},{10,... | collective-permute-start | bytes 3145736 | tf_op jit(solution)/shard_map/ppermute | solution.py:50
  599.4 20.0 %collective-permute-start.121 = (bf16[2,2,2,2,48,512]{5,4,3,2,1,0:T(8,128)(2,1)S(1)}, bf16[2,2,2,2,48,512]{5,4,3,2,1,0:T(8,128)(2,1)S(1)}, u32[]{:S(2)}, u32[]{:S(2)}) collective-permute-start(bf16[2,2,2,2,48,512]{5,4,3,2,1,0:T(8,128)(2,1)S(1)} %bitcast.456), channel_id=1, source_target_pairs={{0,1},{1,0},{2,3},{3,2},{4,5},{5,4},{6,7},{7,6},{8,9},{9,8},{10,11... | collective-permute-start | bytes 2359304 | tf_op jit(solution)/shard_map/ppermute | solution.py:50
  601.1 29.0 %collective-permute-start.117 = (bf16[2,2,2,144,512]{4,3,2,1,0:T(8,128)(2,1)}, bf16[2,2,2,144,512]{4,3,2,1,0:T(8,128)(2,1)}, u32[]{:S(2)}, u32[]{:S(2)}) collective-permute-start(bf16[2,2,2,144,512]{4,3,2,1,0:T(8,128)(2,1)} %dynamic-slice_bitcast_fusion.3), channel_id=1, source_target_pairs={{0,2},{1,3},{2,0},{3,1},{4,6},{5,7},{6,4},{7,5},{8,10},{9,11},{10,... | collective-permute-start | bytes 3538952 | tf_op jit(solution)/shard_map/ppermute | solution.py:50
  633.0 12.8 %collective-permute-start.113 = (f32[4,512]{1,0:T(4,128)S(1)}, f32[4,512]{1,0:T(4,128)S(1)}, u32[]{:S(2)}, u32[]{:S(2)}) collective-permute-start(f32[4,512]{1,0:T(4,128)S(1)} %add_add_fusion.9), channel_id=1, source_target_pairs={{0,4},{1,5},{2,6},{3,7},{4,0},{5,1},{6,2},{7,3},{8,12},{9,13},{10,... | collective-permute-start | bytes 24584 | tf_op jit(solution)/shard_map/ppermute | solution.py:50
  635.5 11.9 %collective-permute-start.114 = (f32[4,512]{1,0:T(4,128)S(1)}, f32[4,512]{1,0:T(4,128)S(1)}, u32[]{:S(2)}, u32[]{:S(2)}) collective-permute-start(f32[4,512]{1,0:T(4,128)S(1)} %add_add_fusion.9), channel_id=1, source_target_pairs={{0,8},{1,9},{2,10},{3,11},{4,12},{5,13},{6,14},{7,15},{8,0},{9,1},... | collective-permute-start | bytes 24584 | tf_op jit(solution)/shard_map/ppermute | solution.py:50
  656.7 25.1 %collective-permute-start.139 = (bf16[2,2,128,512]{3,2,1,0:T(8,128)(2,1)}, bf16[2,2,128,512]{3,2,1,0:T(8,128)(2,1)}, u32[]{:S(2)}, u32[]{:S(2)}) collective-permute-start(bf16[2,2,128,512]{3,2,1,0:T(8,128)(2,1)} %dynamic-slice_bitcast_fusion.6), channel_id=1, source_target_pairs={{0,2},{1,3},{2,0},{3,1},{4,6},{5,7},{6,4},{7,5},{8,10},{9,11},{10,... | collective-permute-start | bytes 1572872 | tf_op jit(solution)/shard_map/ppermute | solution.py:50
  658.2 37.6 %collective-permute-start.136 = (bf16[2,2,144,512]{3,2,1,0:T(8,128)(2,1)}, bf16[2,2,144,512]{3,2,1,0:T(8,128)(2,1)}, u32[]{:S(2)}, u32[]{:S(2)}) collective-permute-start(bf16[2,2,144,512]{3,2,1,0:T(8,128)(2,1)} %dynamic-slice_bitcast_fusion.5), channel_id=1, source_target_pairs={{0,4},{1,5},{2,6},{3,7},{4,0},{5,1},{6,2},{7,3},{8,12},{9,13},{10,... | collective-permute-start | bytes 1769480 | tf_op jit(solution)/shard_map/ppermute | solution.py:50
  659.1 20.4 %collective-permute-start.132 = (bf16[2,2,2,48,512]{4,3,2,1,0:T(8,128)(2,1)}, bf16[2,2,2,48,512]{4,3,2,1,0:T(8,128)(2,1)}, u32[]{:S(2)}, u32[]{:S(2)}) collective-permute-start(bf16[2,2,2,48,512]{4,3,2,1,0:T(8,128)(2,1)} %dynamic-slice_bitcast_fusion.8), channel_id=1, source_target_pairs={{0,4},{1,5},{2,6},{3,7},{4,0},{5,1},{6,2},{7,3},{8,12},{9,13},{10,... | collective-permute-start | bytes 1179656 | tf_op jit(solution)/shard_map/ppermute | solution.py:50
  665.0 19.7 %collective-permute-start.123 = (bf16[2,2,2,2,32,512]{5,4,3,2,1,0:T(8,128)(2,1)}, bf16[2,2,2,2,32,512]{5,4,3,2,1,0:T(8,128)(2,1)}, u32[]{:S(2)}, u32[]{:S(2)}) collective-permute-start(bf16[2,2,2,2,32,512]{5,4,3,2,1,0:T(8,128)(2,1)} %bitcast.390), channel_id=1, source_target_pairs={{0,1},{1,0},{2,3},{3,2},{4,5},{5,4},{6,7},{7,6},{8,9},{9,8},{10,11... | collective-permute-start | bytes 1572872 | tf_op jit(solution)/shard_map/ppermute | solution.py:50
  665.9 17.5 %collective-permute-start.122 = (bf16[2,2,2,2,32,512]{5,4,0,1,2,3:T(8,128)(2,1)}, bf16[2,2,2,2,32,512]{5,4,0,1,2,3:T(8,128)(2,1)}, u32[]{:S(2)}, u32[]{:S(2)}) collective-permute-start(bf16[2,2,2,2,32,512]{5,4,0,1,2,3:T(8,128)(2,1)} %dynamic-slice_bitcast_fusion.7), channel_id=1, source_target_pairs={{0,1},{1,0},{2,3},{3,2},{4,5},{5,4},{6,7},{7,6},{8,9},{9,8},{10,11... | collective-permute-start | bytes 1572872 | tf_op jit(solution)/shard_map/ppermute | solution.py:50
  680.7 14.0 %collective-permute-start.133 = (bf16[2,2,48,512]{3,2,1,0:T(8,128)(2,1)S(1)}, bf16[2,2,48,512]{3,2,1,0:T(8,128)(2,1)S(1)}, u32[]{:S(2)}, u32[]{:S(2)}) collective-permute-start(bf16[2,2,48,512]{3,2,1,0:T(8,128)(2,1)S(1)} %dynamic-slice_bitcast_fusion.13), channel_id=1, source_target_pairs={{0,2},{1,3},{2,0},{3,1},{4,6},{5,7},{6,4},{7,5},{8,10},{9,11},{10,... | collective-permute-start | bytes 589832 | tf_op jit(solution)/shard_map/ppermute | solution.py:50
  683.0 24.3 %collective-permute-start.140 = (bf16[2,128,512]{2,1,0:T(8,128)(2,1)S(1)}, bf16[2,128,512]{2,1,0:T(8,128)(2,1)S(1)}, u32[]{:S(2)}, u32[]{:S(2)}) collective-permute-start(bf16[2,128,512]{2,1,0:T(8,128)(2,1)S(1)} %dynamic-slice_bitcast_fusion.10), channel_id=1, source_target_pairs={{0,8},{1,9},{2,10},{3,11},{4,12},{5,13},{6,14},{7,15},{8,0},{9,1},... | collective-permute-start | bytes 786440 | tf_op jit(solution)/shard_map/ppermute | solution.py:50
  686.2 22.7 %collective-permute-start.125 = (bf16[2,2,2,32,512]{4,3,2,1,0:T(8,128)(2,1)S(1)}, bf16[2,2,2,32,512]{4,3,2,1,0:T(8,128)(2,1)S(1)}, u32[]{:S(2)}, u32[]{:S(2)}) collective-permute-start(bf16[2,2,2,32,512]{4,3,2,1,0:T(8,128)(2,1)S(1)} %dynamic-slice_bitcast_fusion.11), channel_id=1, source_target_pairs={{0,4},{1,5},{2,6},{3,7},{4,0},{5,1},{6,2},{7,3},{8,12},{9,13},{10,... | collective-permute-start | bytes 786440 | tf_op jit(solution)/shard_map/ppermute | solution.py:50
  687.3 21.6 %collective-permute-start.124 = (bf16[2,2,2,32,512]{4,3,0,1,2:T(8,128)(2,1)S(1)}, bf16[2,2,2,32,512]{4,3,0,1,2:T(8,128)(2,1)S(1)}, u32[]{:S(2)}, u32[]{:S(2)}) collective-permute-start(bf16[2,2,2,32,512]{4,3,0,1,2:T(8,128)(2,1)S(1)} %dynamic-slice_bitcast_fusion.12), channel_id=1, source_target_pairs={{0,2},{1,3},{2,0},{3,1},{4,6},{5,7},{6,4},{7,5},{8,10},{9,11},{10,... | collective-permute-start | bytes 786440 | tf_op jit(solution)/shard_map/ppermute | solution.py:50
  700.4 6.2 collective-permute-start.135
  702.9 22.7 %collective-permute-start.137 = (bf16[2,144,512]{2,1,0:T(8,128)(2,1)S(1)}, bf16[2,144,512]{2,1,0:T(8,128)(2,1)S(1)}, u32[]{:S(2)}, u32[]{:S(2)}) collective-permute-start(bf16[2,144,512]{2,1,0:T(8,128)(2,1)S(1)} %dynamic-slice_bitcast_fusion.9), channel_id=1, source_target_pairs={{0,8},{1,9},{2,10},{3,11},{4,12},{5,13},{6,14},{7,15},{8,0},{9,1},... | collective-permute-start | bytes 884744 | tf_op jit(solution)/shard_map/ppermute | solution.py:50
  707.4 19.7 %collective-permute-start.141 = (bf16[128,512]{1,0:T(8,128)(2,1)S(1)}, bf16[128,512]{1,0:T(8,128)(2,1)S(1)}, u32[]{:S(2)}, u32[]{:S(2)}) collective-permute-start(bf16[128,512]{1,0:T(8,128)(2,1)S(1)} %dynamic-slice_bitcast_fusion.15), channel_id=1, source_target_pairs={{0,16},{1,17},{2,18},{3,19},{4,20},{5,21},{6,22},{7,23},{8,24},{9,... | collective-permute-start | bytes 393224 | tf_op jit(solution)/shard_map/ppermute | solution.py:50
  709.0 18.8 %collective-permute-start.126 = (bf16[2,2,32,512]{3,2,0,1:T(8,128)(2,1)S(1)}, bf16[2,2,32,512]{3,2,0,1:T(8,128)(2,1)S(1)}, u32[]{:S(2)}, u32[]{:S(2)}) collective-permute-start(bf16[2,2,32,512]{3,2,0,1:T(8,128)(2,1)S(1)} %dynamic-slice_bitcast_fusion.17), channel_id=1, source_target_pairs={{0,4},{1,5},{2,6},{3,7},{4,0},{5,1},{6,2},{7,3},{8,12},{9,13},{10,... | collective-permute-start | bytes 393224 | tf_op jit(solution)/shard_map/ppermute | solution.py:50
  709.5 20.7 %collective-permute-start.129 = (bf16[2,2,32,512]{3,2,1,0:T(8,128)(2,1)S(1)}, bf16[2,2,32,512]{3,2,1,0:T(8,128)(2,1)S(1)}, u32[]{:S(2)}, u32[]{:S(2)}) collective-permute-start(bf16[2,2,32,512]{3,2,1,0:T(8,128)(2,1)S(1)} %dynamic-slice_bitcast_fusion.16), channel_id=1, source_target_pairs={{0,2},{1,3},{2,0},{3,1},{4,6},{5,7},{6,4},{7,5},{8,10},{9,11},{10,... | collective-permute-start | bytes 393224 | tf_op jit(solution)/shard_map/ppermute | solution.py:50
  725.7 14.8 %collective-permute-start.138 = (bf16[144,512]{1,0:T(8,128)(2,1)S(1)}, bf16[144,512]{1,0:T(8,128)(2,1)S(1)}, u32[]{:S(2)}, u32[]{:S(2)}) collective-permute-start(bf16[144,512]{1,0:T(8,128)(2,1)S(1)} %dynamic-slice_bitcast_fusion.14), channel_id=1, source_target_pairs={{0,16},{1,17},{2,18},{3,19},{4,20},{5,21},{6,22},{7,23},{8,24},{9,... | collective-permute-start | bytes 442376 | tf_op jit(solution)/shard_map/ppermute | solution.py:50
  (221 other events, 1592.6 us)
Sparse Core Ops, SparseCore 0:
  11.9 81.1 all-gather.4
  150.7 96.0 all-gather.6
  457.2 84.1 reduce-scatter.1

commit v5 on v4

--- a/solution.py
+++ b/solution.py
@@ -53,9 +53,11 @@
 def all_sum(value):
     count = device_count()
     bit = 1
+    if count.bit_length() % 2 == 0:
+        value = value + exchange(value, 1)
+        bit = 2
     while bit < count:
-        masks = [bit, 2 * bit, 3 * bit] if 2 * bit < count else [bit]
-        parts = [exchange(value, mask) for mask in masks]
+        parts = [exchange(value, mask) for mask in (bit, 2 * bit, 3 * bit)]
         for part in parts:
             value = value + part
         bit *= 4

time: 758 us -> 755 us (level)
  waiting for transfers between devices: 197 us -> 187 us
  starting transfers between devices: 214 us -> 222 us
    ppermute x122, waiting for transfers between devices: 153 us -> 138 us  [exchange(): lax.ppermute(value, BOTH, [(i, i ^ mask) for i in range(device_count())])]
    ppermute x122, starting transfers between devices: 153 us -> 163 us  [exchange(): lax.ppermute(value, BOTH, [(i, i ^ mask) for i in range(device_count())])]
    unnamed x303 -> x307, local copies, waits for them, and re-layouts: 51.1 us -> 51.6 us
  transfers between devices with their start and end apart: 145 -> 145, of which waited for: 88 -> 86; matrix products, arithmetic and copies ran while one was open for 23% -> 23% of each run, Pallas kernels for 7% -> 7%
where the time goes in v5:
time: 755 us; the launch traced here: 745 us
  starting transfers between devices  222 us (29%)
  waiting for transfers between devices  187 us (25%)
  local copies, waits for them, and re-layouts  102 us (14%)
  other arithmetic  80.7 us (11%)
  matrix products  73.5 us (10%)
  Pallas kernels  63.1 us (8%)
  between operations  17.1 us (2%)
    ppermute x122, starting transfers between devices, exchange(): lax.ppermute(value, BOTH, [(i, i ^ mask) for i in range(device_count())])  163 us
    ppermute x122, waiting for transfers between devices, exchange(): lax.ppermute(value, BOTH, [(i, i ^ mask) for i in range(device_count())])  138 us
    ppermute x20, starting transfers between devices, from_behind(): lax.ppermute(value, 'rows', [(source, source + steps) for source in range...  59 us
    unnamed x307, local copies, waits for them, and re-layouts  51.6 us
    ppermute x20, waiting for transfers between devices, from_behind(): lax.ppermute(value, 'rows', [(source, source + steps) for source in range...  42 us
    pallas_call x1, Pallas kernels, sample_back(): pl.pallas_call(sample_back_kernel, grid=(images,), in_specs=sampler_specs...  30.1 us
    dot_general x7, matrix products, dot_tn(): lax.dot_general(left, right, (((0,), (0,)), ((), ())), preferred_element_...  29.7 us
    dot_general x5, matrix products, dot_nt(): lax.dot_general(left, right, (((1,), (1,)), ((), ())), preferred_element_...  24.6 us
  transfers between devices with their start and end apart: 145, of which 86 were waited for; matrix products, arithmetic and copies ran while one was open for 23% of the time, Pallas kernels for 7%

profile of v5, /device:TPU:0, one launch (start us, length us, event | category | flops | bytes accessed | tf_op | source)
XLA Modules:
  0.0 745.1 jit_solution(113573619316921251)
XLA Ops:
  13.5 3.1 collective-permute-start.5
  23.6 3.9 collective-permute-done.4
  28.3 4.5 collective-permute-done.1
  36.0 3.3 collective-permute-done.7
  44.2 3.3 copy.73
  50.3 4.5 collective-permute-done.9
  57.0 4.4 collective-permute-done.8
  90.0 3.2 collective-permute-start.19
  104.8 5.4 collective-permute-start.22
  111.5 5.4 collective-permute-start.24
  116.9 5.6 collective-permute-start.26
  122.5 3.3 copy.76
  125.8 4.4 reshape.660
  132.8 6.2 collective-permute-done.26.refs_6_
  138.9 5.0 collective-permute-done.22.refs_2_
  150.4 17.6 %sample.1 = bf16[4,176,4608]{2,1,0:T(8,128)(2,1)} custom-call(f32[4,2,1664]{2,1,0:T(2,128)} %get-tuple-element.102.pos_ref, f32[24,1]{1,0:T(8,128)} %constant.444.row_ref, bf16[4,176,512]{2,1,0:T(8,128)(2,1)} %multiply_convert_fusion.10.refs_0_, bf16[4,176,512]{2,1,0:T(8,128)(2,1)} %collective-permute-done.21.refs_1_, ...), custom_call_target="tpu_custom_call" | custom-call | flops 1 | bytes 1 | tf_op jit(solution)/shard_map/sample/pallas_call | solution.py:332
  170.8 3.0 copy-done.39
  173.9 4.6 fusion.131
  181.2 5.4 collective-permute-start.29
  191.2 8.9 %collective-permute-start.31 = (f32[4,512]{1,0:T(4,128)S(1)}, f32[4,512]{1,0:T(4,128)S(1)}, u32[]{:S(2)}, u32[]{:S(2)}) collective-permute-start(f32[4,512]{1,0:T(4,128)S(1)} %add_add_fusion.21), channel_id=1, source_target_pairs={{0,8},{1,9},{2,10},{3,11},{4,12},{5,13},{6,14},{7,15},{8,0},{9,1},... | collective-permute-start | bytes 24584 | tf_op jit(solution)/shard_map/ppermute | solution.py:50
  208.2 5.1 fusion.124
  224.0 3.6 collective-permute-start.40
  227.9 3.1 collective-permute-done.39
  232.8 5.2 multiply_convert_fusion.3
  237.9 6.7 all-gather.7.cloned.1.call-done
  269.0 3.2 collective-permute-start.48
  276.6 3.2 collective-permute-done.49.below
  279.8 4.1 conv.1
  305.4 4.8 fusion.123
  327.1 8.8 %fusion.122 = (f32[2,2048]{1,0:T(2,128)S(1)}, f32[2,2048]{1,0:T(2,128)S(1)}, f32[2,352,2048]{2,1,0:T(8,128)S(1)}, bf16[2,352,2048]{2,1,0:T(8,128)(2,1)}) fusion(f32[2,2048]{1,0:T(2,128)S(1)} %get-tuple-element.325, f32[2,352,2048]{2,1,0:T(8,128)} %get-tuple-element.360, f32[2,2048]{1,0:T(2,128)S(1)} %get-tuple-element.326, ...), kind=kLoop, calls=%fused_computation.418 | loop fusion | flops 30269440 | bytes 20269824 | tf_op jit(solution)/shard_map/reduce_sum | solution.py:732
  349.3 3.7 collective-permute-done.70
  354.9 4.7 fusion.128
  364.4 4.1 bitcast_convert_fusion.2
  377.3 7.4 convolution_convert_fusion.2
  389.2 6.4 collective-permute-done.78
  395.6 5.9 fusion
  405.3 7.3 collective-permute-done.79.above
  415.0 4.0 conv_back.1
  434.1 3.5 collective-permute-done.87
  438.6 8.4 %fusion.121 = (f32[2,2048]{1,0:T(2,128)S(1)}, f32[2,2048]{1,0:T(2,128)S(1)}, f32[2,352,2048]{2,1,0:T(8,128)}) fusion(f32[2,2048]{1,0:T(2,128)S(1)} %get-tuple-element.322, f32[2,352,2048]{2,1,0:T(8,128)S(1)} %bitcast.412, f32[2,2048]{1,0:T(2,128)S(1)} %get-tuple-element.323, bf16[2,352,2048]{2,1,0:T(8,128)(2,1)S(1)} %bitcast.394, ...), kind=kOutput, calls=%fused_computation.417 | convolution fusion | flops 1502339072 | bytes 23085056 | tf_op jit(solution)/shard_map/dot_general | solution.py:38
  453.7 3.0 collective-permute-done.91
  458.4 3.7 collective-permute-start.94
  462.1 4.0 bitcast_convert_fusion
  468.0 3.5 bitcast_convert_fusion.1
  471.6 3.5 fusion.126
  483.1 4.0 collective-permute-start.101
  491.2 4.2 convolution_convert_fusion.1
  499.2 6.4 convolution_convert_fusion
  505.7 3.6 fusion.4
  511.5 30.1 %sample_back.1 = (f32[4,176,512]{2,1,0:T(8,128)S(1)}, bf16[4,176,512]{2,1,0:T(8,128)(2,1)}, bf16[4,176,512]{2,1,0:T(8,128)(2,1)S(1)}, bf16[4,176,512]{2,1,0:T(8,...) custom-call(f32[4,2,1664]{2,1,0:T(2,128)S(1)} %copy-done.16, ...), custom_call_target="tpu_custom_call" | custom-call | flops 1 | bytes 1 | tf_op jit(solution)/shard_map/sample_back/pallas_call | solution.py:354
  548.4 3.3 collective-permute-start.108
  558.8 4.3 reshape.673
  563.2 5.9 copy.88
  569.0 3.0 collective-permute-done.119.above_ref
  573.4 11.7 %collective-permute-start.106 = (bf16[4,176,512]{2,1,0:T(8,128)(2,1)S(1)}, bf16[4,176,512]{2,1,0:T(8,128)(2,1)S(1)}, u32[]{:S(2)}, u32[]{:S(2)}) collective-permute-start(bf16[4,176,512]{2,1,0:T(8,128)(2,1)S(1)} %copy-done.24), channel_id=1, source_target_pairs={{0,8},{4,12},{8,16},{12,20},{16,24},{20,28},{1,9},{5,13},{9,17},{1... | collective-permute-start | bytes 2162696 | tf_op jit(solution)/shard_map/ppermute | solution.py:162
  588.4 7.9 %collective-permute-start.118 = (bf16[2,2,2,128,512]{4,3,2,1,0:T(8,128)(2,1)S(1)}, bf16[2,2,2,128,512]{4,3,2,1,0:T(8,128)(2,1)S(1)}, u32[]{:S(2)}, u32[]{:S(2)}) collective-permute-start(bf16[2,2,2,128,512]{4,3,2,1,0:T(8,128)(2,1)S(1)} %dynamic-slice_bitcast_fusion.4), channel_id=1, source_target_pairs={{0,4},{1,5},{2,6},{3,7},{4,0},{5,1},{6,2},{7,3},{8,12},{9,13},{10,... | collective-permute-start | bytes 3145736 | tf_op jit(solution)/shard_map/ppermute | solution.py:50
  599.5 14.2 %collective-permute-done.107 = bf16[4,176,512]{2,1,0:T(8,128)(2,1)S(1)} collective-permute-done((bf16[4,176,512]{2,1,0:T(8,128)(2,1)S(1)}, bf16[4,176,512]{2,1,0:T(8,128)(2,1)S(1)}, u32[]{:S(2)}, u32[]{:S(2)}) %collective-permute-start.107) | collective-permute-done | bytes 720928 | tf_op jit(solution)/shard_map/ppermute | solution.py:162
  613.7 3.1 convert_add_fusion.7
  636.5 9.6 %collective-permute-start.114 = (f32[4,512]{1,0:T(4,128)S(1)}, f32[4,512]{1,0:T(4,128)S(1)}, u32[]{:S(2)}, u32[]{:S(2)}) collective-permute-start(f32[4,512]{1,0:T(4,128)S(1)} %add_add_fusion.9), channel_id=1, source_target_pairs={{0,8},{1,9},{2,10},{3,11},{4,12},{5,13},{6,14},{7,15},{8,0},{9,1},... | collective-permute-start | bytes 24584 | tf_op jit(solution)/shard_map/ppermute | solution.py:50
  663.8 12.2 %collective-permute-done.132 = bf16[2,2,2,48,512]{4,3,2,1,0:T(8,128)(2,1)} collective-permute-done((bf16[2,2,2,48,512]{4,3,2,1,0:T(8,128)(2,1)}, bf16[2,2,2,48,512]{4,3,2,1,0:T(8,128)(2,1)}, u32[]{:S(2)}, u32[]{:S(2)}) %collective-permute-start.132) | collective-permute-done | bytes 393248 | tf_op jit(solution)/shard_map/ppermute | solution.py:50
  686.8 4.7 fusion.2
  708.5 5.9 reshape.686
  714.4 9.0 %copy.89 = f32[4,4,44,2048]{3,1,2,0:T(4,128)} copy(f32[4,4,44,2048]{3,2,1,0:T(8,128)} %reshape.686) | data formatting | bytes 11534336
  733.7 2.9 collective-permute-done.131
  (791 shorter events, 356.3 us)
Async XLA Ops:
  7.2 160.8 %all-gather.5.cloned.1.call-start = ((), (), s32[]{:S(2)}) async-start(), calls=%async_computation.2 | async-start | bytes 7028736 | tf_op jit(solution)/shard_map/all_gather | solution.py:777
  11.8 232.9 %all-gather.7.cloned.1.call-start = ((), (), s32[]{:S(2)}) async-start(), calls=%async_computation.3 | async-start | bytes 9191424 | tf_op jit(solution)/shard_map/all_gather | solution.py:777
  13.5 8.9 %collective-permute-start.5 = (bf16[48,512]{1,0:T(8,128)(2,1)S(1)}, bf16[48,512]{1,0:T(8,128)(2,1)S(1)}, u32[]{:S(2)}, u32[]{:S(2)}) collective-permute-start(bf16[48,512]{1,0:T(8,128)(2,1)S(1)} %pad_maximum_fusion.15), channel_id=1, source_target_pairs={{0,8},{1,9},{2,10},{3,11},{4,12},{5,13},{6,14},{7,15},{8,0},{9,1},... | collective-permute-start | bytes 147464 | tf_op jit(solution)/shard_map/ppermute | solution.py:50
  16.5 7.0 collective-permute-start.3
  19.0 8.4 %collective-permute-start.4 = (bf16[48,512]{1,0:T(8,128)(2,1)S(1)}, bf16[48,512]{1,0:T(8,128)(2,1)S(1)}, u32[]{:S(2)}, u32[]{:S(2)}) collective-permute-start(bf16[48,512]{1,0:T(8,128)(2,1)S(1)} %pad_maximum_fusion.15), channel_id=1, source_target_pairs={{0,16},{1,17},{2,18},{3,19},{4,20},{5,21},{6,22},{7,23},{8,24},{9,... | collective-permute-start | bytes 147464 | tf_op jit(solution)/shard_map/ppermute | solution.py:50
  19.1 9.1 %collective-permute-start = (bf16[64,512]{1,0:T(8,128)(2,1)}, bf16[64,512]{1,0:T(8,128)(2,1)S(1)}, u32[]{:S(2)}, u32[]{:S(2)}) collective-permute-start(bf16[64,512]{1,0:T(8,128)(2,1)} %param.29), channel_id=1, source_target_pairs={{0,24},{1,25},{2,26},{3,27},{4,28},{5,29},{6,30},{7,31},{8,16},{9,... | collective-permute-start | bytes 196616 | tf_op jit(solution)/shard_map/ppermute | solution.py:50
  22.1 10.7 %collective-permute-start.1 = (bf16[64,512]{1,0:T(8,128)(2,1)}, bf16[64,512]{1,0:T(8,128)(2,1)S(1)}, u32[]{:S(2)}, u32[]{:S(2)}) collective-permute-start(bf16[64,512]{1,0:T(8,128)(2,1)} %param.29), channel_id=1, source_target_pairs={{0,16},{1,17},{2,18},{3,19},{4,20},{5,21},{6,22},{7,23},{8,24},{9,... | collective-permute-start | bytes 196616 | tf_op jit(solution)/shard_map/ppermute | solution.py:50
  34.5 7.5 %collective-permute-start.6 = (bf16[2,2,64,512]{3,2,1,0:T(8,128)(2,1)S(1)}, bf16[2,2,64,512]{3,2,1,0:T(8,128)(2,1)S(1)}, u32[]{:S(2)}, u32[]{:S(2)}) collective-permute-start(bf16[2,2,64,512]{3,2,1,0:T(8,128)(2,1)S(1)} %pad_maximum_fusion.6), channel_id=1, source_target_pairs={{0,4},{1,5},{2,6},{3,7},{4,0},{5,1},{6,2},{7,3},{8,12},{9,13},{10,... | collective-permute-start | bytes 786440 | tf_op jit(solution)/shard_map/ppermute | solution.py:50
  42.0 12.8 %collective-permute-start.9 = (bf16[2,2,2,48,512]{4,3,1,0,2:T(8,128)(2,1)}, bf16[2,2,2,48,512]{4,3,1,0,2:T(8,128)(2,1)}, u32[]{:S(2)}, u32[]{:S(2)}) collective-permute-start(bf16[2,2,2,48,512]{4,3,1,0,2:T(8,128)(2,1)} %pad_maximum_fusion.5), channel_id=1, source_target_pairs={{0,4},{1,5},{2,6},{3,7},{4,0},{5,1},{6,2},{7,3},{8,12},{9,13},{10,... | collective-permute-start | bytes 1179656 | tf_op jit(solution)/shard_map/ppermute | solution.py:50
  43.6 17.8 %collective-permute-start.8 = (bf16[2,2,2,64,512]{4,3,2,1,0:T(8,128)(2,1)S(1)}, bf16[2,2,2,64,512]{4,3,2,1,0:T(8,128)(2,1)}, u32[]{:S(2)}, u32[]{:S(2)}) collective-permute-start(bf16[2,2,2,64,512]{4,3,2,1,0:T(8,128)(2,1)S(1)} %pad_maximum_fusion.4), channel_id=1, source_target_pairs={{0,2},{1,3},{2,0},{3,1},{4,6},{5,7},{6,4},{7,5},{8,10},{9,11},{10,... | collective-permute-start | bytes 1572872 | tf_op jit(solution)/shard_map/ppermute | solution.py:50
  79.5 15.0 %collective-permute-start.16 = (f32[4,512]{1,0:T(4,128)S(1)}, f32[4,512]{1,0:T(4,128)S(1)}, u32[]{:S(2)}, u32[]{:S(2)}) collective-permute-start(f32[4,512]{1,0:T(4,128)S(1)} %add_add_fusion.23), channel_id=1, source_target_pairs={{0,8},{1,9},{2,10},{3,11},{4,12},{5,13},{6,14},{7,15},{8,0},{9,1},... | collective-permute-start | bytes 24584 | tf_op jit(solution)/shard_map/ppermute | solution.py:50
  79.5 15.0 %collective-permute-start.17 = (f32[4,512]{1,0:T(4,128)S(1)}, f32[4,512]{1,0:T(4,128)S(1)}, u32[]{:S(2)}, u32[]{:S(2)}) collective-permute-start(f32[4,512]{1,0:T(4,128)S(1)} %add_add_fusion.23), channel_id=1, source_target_pairs={{0,16},{1,17},{2,18},{3,19},{4,20},{5,21},{6,22},{7,23},{8,24},{9,... | collective-permute-start | bytes 24584 | tf_op jit(solution)/shard_map/ppermute | solution.py:50
  81.3 13.2 %collective-permute-start.18 = (f32[4,512]{1,0:T(4,128)S(1)}, f32[4,512]{1,0:T(4,128)S(1)}, u32[]{:S(2)}, u32[]{:S(2)}) collective-permute-start(f32[4,512]{1,0:T(4,128)S(1)} %add_add_fusion.23), channel_id=1, source_target_pairs={{0,24},{1,25},{2,26},{3,27},{4,28},{5,29},{6,30},{7,31},{8,16},{9,... | collective-permute-start | bytes 24584 | tf_op jit(solution)/shard_map/ppermute | solution.py:50
  90.0 8.7 %collective-permute-start.19 = (f32[96,352]{1,0:T(8,128)S(1)}, f32[96,352]{1,0:T(8,128)S(1)}, u32[]{:S(2)}, u32[]{:S(2)}) collective-permute-start(f32[96,352]{1,0:T(8,128)S(1)} %get-tuple-element.96), channel_id=1, source_target_pairs={{0,4},{4,8},{8,12},{12,16},{16,20},{20,24},{24,28},{1,5},{5,9},{9,... | collective-permute-start | bytes 405512 | tf_op jit(solution)/shard_map/ppermute | solution.py:162
  93.2 7.0 collective-permute-start.20
  102.2 14.7 %collective-permute-start.25 = (bf16[4,88,512]{2,1,0:T(8,128)(2,1)S(1)}, bf16[4,88,512]{2,1,0:T(8,128)(2,1)S(1)}, u32[]{:S(2)}, u32[]{:S(2)}) collective-permute-start(bf16[4,88,512]{2,1,0:T(8,128)(2,1)S(1)} %get-tuple-element.292), channel_id=1, source_target_pairs={{12,0},{16,4},{20,8},{24,12},{28,16},{13,1},{17,5},{21,9},{25,13},... | collective-permute-start | bytes 1081352 | tf_op jit(solution)/shard_map/ppermute | solution.py:162
  103.5 35.5 %collective-permute-start.21 = (bf16[4,176,512]{2,1,0:T(8,128)(2,1)}, bf16[4,176,512]{2,1,0:T(8,128)(2,1)}, u32[]{:S(2)}, u32[]{:S(2)}) collective-permute-start(bf16[4,176,512]{2,1,0:T(8,128)(2,1)} %multiply_convert_fusion.10.refs_0_), channel_id=1, source_target_pairs={{4,0},{8,4},{12,8},{16,12},{20,16},{24,20},{28,24},{5,1},{9,5},{13... | collective-permute-start | bytes 2162696 | tf_op jit(solution)/shard_map/ppermute | solution.py:162
  104.8 39.1 %collective-permute-start.22 = (bf16[4,176,512]{2,1,0:T(8,128)(2,1)}, bf16[4,176,512]{2,1,0:T(8,128)(2,1)}, u32[]{:S(2)}, u32[]{:S(2)}) collective-permute-start(bf16[4,176,512]{2,1,0:T(8,128)(2,1)} %multiply_convert_fusion.10.refs_0_), channel_id=1, source_target_pairs={{0,4},{4,8},{8,12},{12,16},{16,20},{20,24},{24,28},{1,5},{5,9},{9,... | collective-permute-start | bytes 2162696 | tf_op jit(solution)/shard_map/ppermute | solution.py:162
  110.2 34.8 %collective-permute-start.23 = (bf16[4,176,512]{2,1,0:T(8,128)(2,1)}, bf16[4,176,512]{2,1,0:T(8,128)(2,1)}, u32[]{:S(2)}, u32[]{:S(2)}) collective-permute-start(bf16[4,176,512]{2,1,0:T(8,128)(2,1)} %multiply_convert_fusion.10.refs_0_), channel_id=1, source_target_pairs={{8,0},{12,4},{16,8},{20,12},{24,16},{28,20},{9,1},{13,5},{17,9},{2... | collective-permute-start | bytes 2162696 | tf_op jit(solution)/shard_map/ppermute | solution.py:162
  111.5 33.5 %collective-permute-start.24 = (bf16[4,176,512]{2,1,0:T(8,128)(2,1)}, bf16[4,176,512]{2,1,0:T(8,128)(2,1)}, u32[]{:S(2)}, u32[]{:S(2)}) collective-permute-start(bf16[4,176,512]{2,1,0:T(8,128)(2,1)} %multiply_convert_fusion.10.refs_0_), channel_id=1, source_target_pairs={{0,8},{4,12},{8,16},{12,20},{16,24},{20,28},{1,9},{5,13},{9,17},{1... | collective-permute-start | bytes 2162696 | tf_op jit(solution)/shard_map/ppermute | solution.py:162
  116.9 22.0 %collective-permute-start.26 = (bf16[4,88,512]{2,1,0:T(8,128)(2,1)}, bf16[4,88,512]{2,1,0:T(8,128)(2,1)}, u32[]{:S(2)}, u32[]{:S(2)}) collective-permute-start(bf16[4,88,512]{2,1,0:T(8,128)(2,1)} %get-tuple-element.291), channel_id=1, source_target_pairs={{0,12},{4,16},{8,20},{12,24},{16,28},{1,13},{5,17},{9,21},{13,25},... | collective-permute-start | bytes 1081352 | tf_op jit(solution)/shard_map/ppermute | solution.py:162
  150.3 470.7 %reduce-scatter.2.cloned.1.call-start = ((), (), s32[]{:S(2)}) async-start(), calls=%async_computation.1 | async-start | bytes 3620864 | tf_op jit(solution)/shard_map/reduce_scatter | solution.py:110
  179.8 7.0 collective-permute-start.28
  181.2 7.0 collective-permute-start.29
  191.2 13.1 %collective-permute-start.31 = (f32[4,512]{1,0:T(4,128)S(1)}, f32[4,512]{1,0:T(4,128)S(1)}, u32[]{:S(2)}, u32[]{:S(2)}) collective-permute-start(f32[4,512]{1,0:T(4,128)S(1)} %add_add_fusion.21), channel_id=1, source_target_pairs={{0,8},{1,9},{2,10},{3,11},{4,12},{5,13},{6,14},{7,15},{8,0},{9,1},... | collective-permute-start | bytes 24584 | tf_op jit(solution)/shard_map/ppermute | solution.py:50
  223.2 7.8 %collective-permute-start.39 = (f32[4,2048]{1,0:T(4,128)S(1)}, f32[4,2048]{1,0:T(4,128)}, u32[]{:S(2)}, u32[]{:S(2)}) collective-permute-start(f32[4,2048]{1,0:T(4,128)S(1)} %add_add_fusion.7), channel_id=1, source_target_pairs={{0,16},{1,17},{2,18},{3,19},{4,20},{5,21},{6,22},{7,23},{8,24},{9,... | collective-permute-start | bytes 98312 | tf_op jit(solution)/shard_map/ppermute | solution.py:50
  224.0 7.3 collective-permute-start.40
  269.0 7.6 %collective-permute-start.48 = (bf16[4,44,512]{2,1,0:T(8,128)(2,1)S(1)}, bf16[4,44,512]{2,1,0:T(8,128)(2,1)S(1)}, u32[]{:S(2)}, u32[]{:S(2)}) collective-permute-start(bf16[4,44,512]{2,1,0:T(8,128)(2,1)S(1)} %get-tuple-element.290), channel_id=1, source_target_pairs={{0,4},{4,8},{8,12},{12,16},{16,20},{20,24},{24,28},{1,5},{5,9},{9,... | collective-permute-start | bytes 540680 | tf_op jit(solution)/shard_map/ppermute | solution.py:162
  272.2 7.6 %collective-permute-start.49 = (bf16[4,44,512]{2,1,0:T(8,128)(2,1)S(1)}, bf16[4,44,512]{2,1,0:T(8,128)(2,1)S(1)}, u32[]{:S(2)}, u32[]{:S(2)}) collective-permute-start(bf16[4,44,512]{2,1,0:T(8,128)(2,1)S(1)} %get-tuple-element.289), channel_id=1, source_target_pairs={{4,0},{8,4},{12,8},{16,12},{20,16},{24,20},{28,24},{5,1},{9,5},{13... | collective-permute-start | bytes 540680 | tf_op jit(solution)/shard_map/ppermute | solution.py:162
  360.9 7.7 %collective-permute-start.72 = (f32[4,512]{1,0:T(4,128)S(1)}, f32[4,512]{1,0:T(4,128)S(1)}, u32[]{:S(2)}, u32[]{:S(2)}) collective-permute-start(f32[4,512]{1,0:T(4,128)S(1)} %fusion.112), channel_id=1, source_target_pairs={{0,2},{1,3},{2,0},{3,1},{4,6},{5,7},{6,4},{7,5},{8,10},{9,11},{10,... | collective-permute-start | bytes 24584 | tf_op jit(solution)/shard_map/ppermute | solution.py:50
  361.6 7.0 collective-permute-start.73
  401.5 11.1 %collective-permute-start.79 = (bf16[4,44,512]{2,1,0:T(8,128)(2,1)S(1)}, bf16[4,44,512]{2,1,0:T(8,128)(2,1)S(1)}, u32[]{:S(2)}, u32[]{:S(2)}) collective-permute-start(bf16[4,44,512]{2,1,0:T(8,128)(2,1)S(1)} %get-tuple-element.288), channel_id=1, source_target_pairs={{0,4},{4,8},{8,12},{12,16},{16,20},{20,24},{24,28},{1,5},{5,9},{9,... | collective-permute-start | bytes 540680 | tf_op jit(solution)/shard_map/ppermute | solution.py:162
  404.0 8.6 %collective-permute-start.80 = (bf16[4,44,512]{2,1,0:T(8,128)(2,1)S(1)}, bf16[4,44,512]{2,1,0:T(8,128)(2,1)S(1)}, u32[]{:S(2)}, u32[]{:S(2)}) collective-permute-start(bf16[4,44,512]{2,1,0:T(8,128)(2,1)S(1)} %get-tuple-element.287), channel_id=1, source_target_pairs={{4,0},{8,4},{12,8},{16,12},{20,16},{24,20},{28,24},{5,1},{9,5},{13... | collective-permute-start | bytes 540680 | tf_op jit(solution)/shard_map/ppermute | solution.py:162
  457.7 8.4 %collective-permute-start.92 = (f32[4,2048]{1,0:T(4,128)S(1)}, f32[4,2048]{1,0:T(4,128)S(1)}, u32[]{:S(2)}, u32[]{:S(2)}) collective-permute-start(f32[4,2048]{1,0:T(4,128)S(1)} %add_add_fusion.1), channel_id=1, source_target_pairs={{0,8},{1,9},{2,10},{3,11},{4,12},{5,13},{6,14},{7,15},{8,0},{9,1},... | collective-permute-start | bytes 98312 | tf_op jit(solution)/shard_map/ppermute | solution.py:50
  457.7 8.4 %collective-permute-start.93 = (f32[4,2048]{1,0:T(4,128)S(1)}, f32[4,2048]{1,0:T(4,128)S(1)}, u32[]{:S(2)}, u32[]{:S(2)}) collective-permute-start(f32[4,2048]{1,0:T(4,128)S(1)} %add_add_fusion.1), channel_id=1, source_target_pairs={{0,16},{1,17},{2,18},{3,19},{4,20},{5,21},{6,22},{7,23},{8,24},{9,... | collective-permute-start | bytes 98312 | tf_op jit(solution)/shard_map/ppermute | solution.py:50
  458.4 7.7 %collective-permute-start.94 = (f32[4,2048]{1,0:T(4,128)S(1)}, f32[4,2048]{1,0:T(4,128)S(1)}, u32[]{:S(2)}, u32[]{:S(2)}) collective-permute-start(f32[4,2048]{1,0:T(4,128)S(1)} %add_add_fusion.1), channel_id=1, source_target_pairs={{0,24},{1,25},{2,26},{3,27},{4,28},{5,29},{6,30},{7,31},{8,16},{9,... | collective-permute-start | bytes 98312 | tf_op jit(solution)/shard_map/ppermute | solution.py:50
  497.2 8.5 %collective-permute-start.103 = (bf16[2,2,2,2,128,512]{5,4,3,2,1,0:T(8,128)(2,1)}, bf16[2,2,2,2,128,512]{5,4,3,2,1,0:T(8,128)(2,1)}, u32[]{:S(2)}, u32[]{:S(2)}) collective-permute-start(bf16[2,2,2,2,128,512]{5,4,3,2,1,0:T(8,128)(2,1)} %dynamic-slice_bitcast_fusion.2), channel_id=1, source_target_pairs={{0,1},{1,0},{2,3},{3,2},{4,5},{5,4},{6,7},{7,6},{8,9},{9,8},{10,11... | collective-permute-start | bytes 6291464 | tf_op jit(solution)/shard_map/ppermute | solution.py:50
  498.7 10.5 %collective-permute-start.102 = (bf16[2,2,2,2,144,512]{5,4,3,2,1,0:T(8,128)(2,1)}, bf16[2,2,2,2,144,512]{5,4,3,2,1,0:T(8,128)(2,1)S(1)}, u32[]{:S(2)}, u32[]{:S(2)}) collective-permute-start(bf16[2,2,2,2,144,512]{5,4,3,2,1,0:T(8,128)(2,1)} %dynamic-slice_bitcast_fusion.1), channel_id=1, source_target_pairs={{0,1},{1,0},{2,3},{3,2},{4,5},{5,4},{6,7},{7,6},{8,9},{9,8},{10,11... | collective-permute-start | bytes 7077896 | tf_op jit(solution)/shard_map/ppermute | solution.py:50
  545.9 50.3 %collective-permute-start.104 = (bf16[4,176,512]{2,1,0:T(8,128)(2,1)}, bf16[4,176,512]{2,1,0:T(8,128)(2,1)}, u32[]{:S(2)}, u32[]{:S(2)}) collective-permute-start(bf16[4,176,512]{2,1,0:T(8,128)(2,1)} %get-tuple-element.122), channel_id=1, source_target_pairs={{0,4},{4,8},{8,12},{12,16},{16,20},{20,24},{24,28},{1,5},{5,9},{9,... | collective-permute-start | bytes 2162696 | tf_op jit(solution)/shard_map/ppermute | solution.py:162
  548.4 36.8 %collective-permute-start.108 = (bf16[4,88,512]{2,1,0:T(8,128)(2,1)S(1)}, bf16[4,88,512]{2,1,0:T(8,128)(2,1)}, u32[]{:S(2)}, u32[]{:S(2)}) collective-permute-start(bf16[4,88,512]{2,1,0:T(8,128)(2,1)S(1)} %get-tuple-element.126), channel_id=1, source_target_pairs={{0,12},{4,16},{8,20},{12,24},{16,28},{1,13},{5,17},{9,21},{13,25},... | collective-permute-start | bytes 1081352 | tf_op jit(solution)/shard_map/ppermute | solution.py:162
  551.6 36.8 %collective-permute-start.109 = (bf16[4,88,512]{2,1,0:T(8,128)(2,1)}, bf16[4,88,512]{2,1,0:T(8,128)(2,1)}, u32[]{:S(2)}, u32[]{:S(2)}) collective-permute-start(bf16[4,88,512]{2,1,0:T(8,128)(2,1)} %get-tuple-element.127), channel_id=1, source_target_pairs={{12,0},{16,4},{20,8},{24,12},{28,16},{13,1},{17,5},{21,9},{25,13},... | collective-permute-start | bytes 1081352 | tf_op jit(solution)/shard_map/ppermute | solution.py:162
  554.7 17.4 %collective-permute-start.119 = (bf16[32,352]{1,0:T(8,128)(2,1)}, bf16[32,352]{1,0:T(8,128)(2,1)S(1)}, u32[]{:S(2)}, u32[]{:S(2)}) collective-permute-start(bf16[32,352]{1,0:T(8,128)(2,1)} %get-tuple-element.135), channel_id=1, source_target_pairs={{0,4},{4,8},{8,12},{12,16},{16,20},{20,24},{24,28},{1,5},{5,9},{9,... | collective-permute-start | bytes 67592 | tf_op jit(solution)/shard_map/ppermute | solution.py:162
  557.5 15.9 %collective-permute-start.120 = (bf16[32,352]{1,0:T(8,128)(2,1)}, bf16[32,352]{1,0:T(8,128)(2,1)S(1)}, u32[]{:S(2)}, u32[]{:S(2)}) collective-permute-start(bf16[32,352]{1,0:T(8,128)(2,1)} %get-tuple-element.136), channel_id=1, source_target_pairs={{4,0},{8,4},{12,8},{16,12},{20,16},{24,20},{28,24},{5,1},{9,5},{13... | collective-permute-start | bytes 67592 | tf_op jit(solution)/shard_map/ppermute | solution.py:162
  572.1 25.9 %collective-permute-start.105 = (bf16[4,176,512]{2,1,0:T(8,128)(2,1)S(1)}, bf16[4,176,512]{2,1,0:T(8,128)(2,1)S(1)}, u32[]{:S(2)}, u32[]{:S(2)}) collective-permute-start(bf16[4,176,512]{2,1,0:T(8,128)(2,1)S(1)} %copy-done.26), channel_id=1, source_target_pairs={{4,0},{8,4},{12,8},{16,12},{20,16},{24,20},{28,24},{5,1},{9,5},{13... | collective-permute-start | bytes 2162696 | tf_op jit(solution)/shard_map/ppermute | solution.py:162
  573.4 26.1 %collective-permute-start.106 = (bf16[4,176,512]{2,1,0:T(8,128)(2,1)S(1)}, bf16[4,176,512]{2,1,0:T(8,128)(2,1)S(1)}, u32[]{:S(2)}, u32[]{:S(2)}) collective-permute-start(bf16[4,176,512]{2,1,0:T(8,128)(2,1)S(1)} %copy-done.24), channel_id=1, source_target_pairs={{0,8},{4,12},{8,16},{12,20},{16,24},{20,28},{1,9},{5,13},{9,17},{1... | collective-permute-start | bytes 2162696 | tf_op jit(solution)/shard_map/ppermute | solution.py:162
  585.2 28.6 %collective-permute-start.107 = (bf16[4,176,512]{2,1,0:T(8,128)(2,1)S(1)}, bf16[4,176,512]{2,1,0:T(8,128)(2,1)S(1)}, u32[]{:S(2)}, u32[]{:S(2)}) collective-permute-start(bf16[4,176,512]{2,1,0:T(8,128)(2,1)S(1)} %copy-done.22), channel_id=1, source_target_pairs={{8,0},{12,4},{16,8},{20,12},{24,16},{28,20},{9,1},{13,5},{17,9},{2... | collective-permute-start | bytes 2162696 | tf_op jit(solution)/shard_map/ppermute | solution.py:162
  588.4 31.3 %collective-permute-start.118 = (bf16[2,2,2,128,512]{4,3,2,1,0:T(8,128)(2,1)S(1)}, bf16[2,2,2,128,512]{4,3,2,1,0:T(8,128)(2,1)S(1)}, u32[]{:S(2)}, u32[]{:S(2)}) collective-permute-start(bf16[2,2,2,128,512]{4,3,2,1,0:T(8,128)(2,1)S(1)} %dynamic-slice_bitcast_fusion.4), channel_id=1, source_target_pairs={{0,4},{1,5},{2,6},{3,7},{4,0},{5,1},{6,2},{7,3},{8,12},{9,13},{10,... | collective-permute-start | bytes 3145736 | tf_op jit(solution)/shard_map/ppermute | solution.py:50
  596.3 20.5 %collective-permute-start.121 = (bf16[2,2,2,2,48,512]{5,4,3,2,1,0:T(8,128)(2,1)S(1)}, bf16[2,2,2,2,48,512]{5,4,3,2,1,0:T(8,128)(2,1)S(1)}, u32[]{:S(2)}, u32[]{:S(2)}) collective-permute-start(bf16[2,2,2,2,48,512]{5,4,3,2,1,0:T(8,128)(2,1)S(1)} %bitcast.456), channel_id=1, source_target_pairs={{0,1},{1,0},{2,3},{3,2},{4,5},{5,4},{6,7},{7,6},{8,9},{9,8},{10,11... | collective-permute-start | bytes 2359304 | tf_op jit(solution)/shard_map/ppermute | solution.py:50
  598.0 28.7 %collective-permute-start.117 = (bf16[2,2,2,144,512]{4,3,2,1,0:T(8,128)(2,1)}, bf16[2,2,2,144,512]{4,3,2,1,0:T(8,128)(2,1)}, u32[]{:S(2)}, u32[]{:S(2)}) collective-permute-start(bf16[2,2,2,144,512]{4,3,2,1,0:T(8,128)(2,1)} %dynamic-slice_bitcast_fusion.3), channel_id=1, source_target_pairs={{0,2},{1,3},{2,0},{3,1},{4,6},{5,7},{6,4},{7,5},{8,10},{9,11},{10,... | collective-permute-start | bytes 3538952 | tf_op jit(solution)/shard_map/ppermute | solution.py:50
  636.5 13.4 %collective-permute-start.114 = (f32[4,512]{1,0:T(4,128)S(1)}, f32[4,512]{1,0:T(4,128)S(1)}, u32[]{:S(2)}, u32[]{:S(2)}) collective-permute-start(f32[4,512]{1,0:T(4,128)S(1)} %add_add_fusion.9), channel_id=1, source_target_pairs={{0,8},{1,9},{2,10},{3,11},{4,12},{5,13},{6,14},{7,15},{8,0},{9,1},... | collective-permute-start | bytes 24584 | tf_op jit(solution)/shard_map/ppermute | solution.py:50
  653.4 25.2 %collective-permute-start.139 = (bf16[2,2,128,512]{3,2,1,0:T(8,128)(2,1)}, bf16[2,2,128,512]{3,2,1,0:T(8,128)(2,1)}, u32[]{:S(2)}, u32[]{:S(2)}) collective-permute-start(bf16[2,2,128,512]{3,2,1,0:T(8,128)(2,1)} %dynamic-slice_bitcast_fusion.6), channel_id=1, source_target_pairs={{0,2},{1,3},{2,0},{3,1},{4,6},{5,7},{6,4},{7,5},{8,10},{9,11},{10,... | collective-permute-start | bytes 1572872 | tf_op jit(solution)/shard_map/ppermute | solution.py:50
  654.9 38.6 %collective-permute-start.136 = (bf16[2,2,144,512]{3,2,1,0:T(8,128)(2,1)}, bf16[2,2,144,512]{3,2,1,0:T(8,128)(2,1)}, u32[]{:S(2)}, u32[]{:S(2)}) collective-permute-start(bf16[2,2,144,512]{3,2,1,0:T(8,128)(2,1)} %dynamic-slice_bitcast_fusion.5), channel_id=1, source_target_pairs={{0,4},{1,5},{2,6},{3,7},{4,0},{5,1},{6,2},{7,3},{8,12},{9,13},{10,... | collective-permute-start | bytes 1769480 | tf_op jit(solution)/shard_map/ppermute | solution.py:50
  657.4 18.6 %collective-permute-start.132 = (bf16[2,2,2,48,512]{4,3,2,1,0:T(8,128)(2,1)}, bf16[2,2,2,48,512]{4,3,2,1,0:T(8,128)(2,1)}, u32[]{:S(2)}, u32[]{:S(2)}) collective-permute-start(bf16[2,2,2,48,512]{4,3,2,1,0:T(8,128)(2,1)} %dynamic-slice_bitcast_fusion.8), channel_id=1, source_target_pairs={{0,4},{1,5},{2,6},{3,7},{4,0},{5,1},{6,2},{7,3},{8,12},{9,13},{10,... | collective-permute-start | bytes 1179656 | tf_op jit(solution)/shard_map/ppermute | solution.py:50
  661.7 19.6 %collective-permute-start.123 = (bf16[2,2,2,2,32,512]{5,4,3,2,1,0:T(8,128)(2,1)}, bf16[2,2,2,2,32,512]{5,4,3,2,1,0:T(8,128)(2,1)}, u32[]{:S(2)}, u32[]{:S(2)}) collective-permute-start(bf16[2,2,2,2,32,512]{5,4,3,2,1,0:T(8,128)(2,1)} %bitcast.390), channel_id=1, source_target_pairs={{0,1},{1,0},{2,3},{3,2},{4,5},{5,4},{6,7},{7,6},{8,9},{9,8},{10,11... | collective-permute-start | bytes 1572872 | tf_op jit(solution)/shard_map/ppermute | solution.py:50
  662.6 17.3 %collective-permute-start.122 = (bf16[2,2,2,2,32,512]{5,4,0,1,2,3:T(8,128)(2,1)}, bf16[2,2,2,2,32,512]{5,4,0,1,2,3:T(8,128)(2,1)}, u32[]{:S(2)}, u32[]{:S(2)}) collective-permute-start(bf16[2,2,2,2,32,512]{5,4,0,1,2,3:T(8,128)(2,1)} %dynamic-slice_bitcast_fusion.7), channel_id=1, source_target_pairs={{0,1},{1,0},{2,3},{3,2},{4,5},{5,4},{6,7},{7,6},{8,9},{9,8},{10,11... | collective-permute-start | bytes 1572872 | tf_op jit(solution)/shard_map/ppermute | solution.py:50
  677.1 14.4 %collective-permute-start.133 = (bf16[2,2,48,512]{3,2,1,0:T(8,128)(2,1)S(1)}, bf16[2,2,48,512]{3,2,1,0:T(8,128)(2,1)S(1)}, u32[]{:S(2)}, u32[]{:S(2)}) collective-permute-start(bf16[2,2,48,512]{3,2,1,0:T(8,128)(2,1)S(1)} %dynamic-slice_bitcast_fusion.13), channel_id=1, source_target_pairs={{0,2},{1,3},{2,0},{3,1},{4,6},{5,7},{6,4},{7,5},{8,10},{9,11},{10,... | collective-permute-start | bytes 589832 | tf_op jit(solution)/shard_map/ppermute | solution.py:50
  679.8 23.3 %collective-permute-start.140 = (bf16[2,128,512]{2,1,0:T(8,128)(2,1)S(1)}, bf16[2,128,512]{2,1,0:T(8,128)(2,1)S(1)}, u32[]{:S(2)}, u32[]{:S(2)}) collective-permute-start(bf16[2,128,512]{2,1,0:T(8,128)(2,1)S(1)} %dynamic-slice_bitcast_fusion.10), channel_id=1, source_target_pairs={{0,8},{1,9},{2,10},{3,11},{4,12},{5,13},{6,14},{7,15},{8,0},{9,1},... | collective-permute-start | bytes 786440 | tf_op jit(solution)/shard_map/ppermute | solution.py:50
  682.7 22.5 %collective-permute-start.125 = (bf16[2,2,2,32,512]{4,3,2,1,0:T(8,128)(2,1)S(1)}, bf16[2,2,2,32,512]{4,3,2,1,0:T(8,128)(2,1)S(1)}, u32[]{:S(2)}, u32[]{:S(2)}) collective-permute-start(bf16[2,2,2,32,512]{4,3,2,1,0:T(8,128)(2,1)S(1)} %dynamic-slice_bitcast_fusion.11), channel_id=1, source_target_pairs={{0,4},{1,5},{2,6},{3,7},{4,0},{5,1},{6,2},{7,3},{8,12},{9,13},{10,... | collective-permute-start | bytes 786440 | tf_op jit(solution)/shard_map/ppermute | solution.py:50
  684.3 20.9 %collective-permute-start.124 = (bf16[2,2,2,32,512]{4,3,0,1,2:T(8,128)(2,1)S(1)}, bf16[2,2,2,32,512]{4,3,0,1,2:T(8,128)(2,1)S(1)}, u32[]{:S(2)}, u32[]{:S(2)}) collective-permute-start(bf16[2,2,2,32,512]{4,3,0,1,2:T(8,128)(2,1)S(1)} %dynamic-slice_bitcast_fusion.12), channel_id=1, source_target_pairs={{0,2},{1,3},{2,0},{3,1},{4,6},{5,7},{6,4},{7,5},{8,10},{9,11},{10,... | collective-permute-start | bytes 786440 | tf_op jit(solution)/shard_map/ppermute | solution.py:50
  699.3 24.1 %collective-permute-start.137 = (bf16[2,144,512]{2,1,0:T(8,128)(2,1)S(1)}, bf16[2,144,512]{2,1,0:T(8,128)(2,1)S(1)}, u32[]{:S(2)}, u32[]{:S(2)}) collective-permute-start(bf16[2,144,512]{2,1,0:T(8,128)(2,1)S(1)} %dynamic-slice_bitcast_fusion.9), channel_id=1, source_target_pairs={{0,8},{1,9},{2,10},{3,11},{4,12},{5,13},{6,14},{7,15},{8,0},{9,1},... | collective-permute-start | bytes 884744 | tf_op jit(solution)/shard_map/ppermute | solution.py:50
  703.2 20.4 %collective-permute-start.141 = (bf16[128,512]{1,0:T(8,128)(2,1)S(1)}, bf16[128,512]{1,0:T(8,128)(2,1)S(1)}, u32[]{:S(2)}, u32[]{:S(2)}) collective-permute-start(bf16[128,512]{1,0:T(8,128)(2,1)S(1)} %dynamic-slice_bitcast_fusion.15), channel_id=1, source_target_pairs={{0,16},{1,17},{2,18},{3,19},{4,20},{5,21},{6,22},{7,23},{8,24},{9,... | collective-permute-start | bytes 393224 | tf_op jit(solution)/shard_map/ppermute | solution.py:50
  705.4 19.0 %collective-permute-start.126 = (bf16[2,2,32,512]{3,2,0,1:T(8,128)(2,1)S(1)}, bf16[2,2,32,512]{3,2,0,1:T(8,128)(2,1)S(1)}, u32[]{:S(2)}, u32[]{:S(2)}) collective-permute-start(bf16[2,2,32,512]{3,2,0,1:T(8,128)(2,1)S(1)} %dynamic-slice_bitcast_fusion.17), channel_id=1, source_target_pairs={{0,4},{1,5},{2,6},{3,7},{4,0},{5,1},{6,2},{7,3},{8,12},{9,13},{10,... | collective-permute-start | bytes 393224 | tf_op jit(solution)/shard_map/ppermute | solution.py:50
  707.1 19.9 %collective-permute-start.129 = (bf16[2,2,32,512]{3,2,1,0:T(8,128)(2,1)S(1)}, bf16[2,2,32,512]{3,2,1,0:T(8,128)(2,1)S(1)}, u32[]{:S(2)}, u32[]{:S(2)}) collective-permute-start(bf16[2,2,32,512]{3,2,1,0:T(8,128)(2,1)S(1)} %dynamic-slice_bitcast_fusion.16), channel_id=1, source_target_pairs={{0,2},{1,3},{2,0},{3,1},{4,6},{5,7},{6,4},{7,5},{8,10},{9,11},{10,... | collective-permute-start | bytes 393224 | tf_op jit(solution)/shard_map/ppermute | solution.py:50
  723.5 13.8 %collective-permute-start.138 = (bf16[144,512]{1,0:T(8,128)(2,1)S(1)}, bf16[144,512]{1,0:T(8,128)(2,1)S(1)}, u32[]{:S(2)}, u32[]{:S(2)}) collective-permute-start(bf16[144,512]{1,0:T(8,128)(2,1)S(1)} %dynamic-slice_bitcast_fusion.14), channel_id=1, source_target_pairs={{0,16},{1,17},{2,18},{3,19},{4,20},{5,21},{6,22},{7,23},{8,24},{9,... | collective-permute-start | bytes 442376 | tf_op jit(solution)/shard_map/ppermute | solution.py:50
  (223 other events, 1648.2 us)
Sparse Core Ops, SparseCore 0:
  11.9 81.1 all-gather.4
  150.5 94.1 all-gather.6
  452.0 84.0 reduce-scatter.1
